TPU v7x, 32 devices: a whole 2x2x4 slice. The times are simulated.
32 devices in a mesh: grp: 4 (over z), exp: 4 (over y, x), rep: 2 (over core).
Axes of the slice: x: 2, y: 2, z: 4, core: 2. Of those that a mesh axis runs over, the one named last changes fastest.
Arguments:
- tokens: bfloat16 [1024, 2048], P(('grp', 'exp', 'rep')), may hold values from -6 to 6
- cotangent: bfloat16 [1024, 2048], P(('grp', 'exp', 'rep')), may hold values from -6 to 6
- expert_ids: int32 [1024, 8], P(('grp', 'exp', 'rep')), may hold values from 0 to 15, all different within a row; in each aligned block of 32 rows (0 to 31, 32 to 63, ...) at most 24 rows name the same one
- gate_probs: float32 [1024, 8], P(('grp', 'exp', 'rep')), may hold values from 0.05 to 0.6
- gate_weight: bfloat16 [16, 2048, 768], P(('grp', 'exp'), 'rep'), may hold values from -0.125 to 0.125
- up_weight: bfloat16 [16, 2048, 768], P(('grp', 'exp'), 'rep'), may hold values from -0.125 to 0.125
- down_weight: bfloat16 [16, 768, 2048], P(('grp', 'exp'), 'rep'), may hold values from -0.21875 to 0.21875
Outputs:
- layer_out: bfloat16 [1024, 2048], P(('grp', 'exp', 'rep'))
- token_grad: bfloat16 [1024, 2048], P(('grp', 'exp', 'rep'))
- gate_grad: bfloat16 [16, 2048, 768], P(('grp', 'exp'), 'rep')
- up_grad: bfloat16 [16, 2048, 768], P(('grp', 'exp'), 'rep')
- down_grad: bfloat16 [16, 768, 2048], P(('grp', 'exp'), 'rep')
Inputs may be any that keep to these rules, and one draw needn't show every extreme that they name: `expert_ids`: each token names 8 different experts. Among the 32 tokens of one device, no expert is named more than 24 times, and in some device one expert is named exactly 24 times.
All inputs are finite; a program needn't handle non-finite values.
Results may differ from a plain program's by a relative error of at most 0.0065.
Values may be sent and summed in bfloat16 or wider, within the bound.
No kernel may reach another device: no remote copies, remote signals or barrier semaphores. Data moves between devices by JAX's collectives and lax.ppermute only.
A program may use at most 128 MiB of HBM per device.

v0:
```python
import jax
import jax.numpy as jnp
from jax import lax
from jax.sharding import PartitionSpec as P

TOP = 8


def partner_2(value, axis, bit):
    mask = 2**bit
    pairs = [(source, source ^ mask) for source in range(lax.axis_size(axis))]
    return lax.ppermute(value, axis, pairs)


def contract_rows(left, right):
    return lax.dot_general(
        left, right, (((0,), (0,)), ((), ())), preferred_element_type=jnp.float32
    )


def contract_cols(left, right):
    return lax.dot_general(
        left, right, (((1,), (1,)), ((), ())), preferred_element_type=jnp.float32
    )


def rounded_sum(first, second):
    left_part = lax.optimization_barrier(first.astype(jnp.bfloat16))
    right_part = lax.optimization_barrier(second.astype(jnp.bfloat16))
    return left_part.astype(jnp.float32) + right_part.astype(jnp.float32)


def local(tokens, cotangent, expert_ids, gate_probs, gate_weight, up_weight, down_weight):
    group_count = lax.axis_size("grp")
    inner_count = lax.axis_size("exp")
    expert_count = group_count * inner_count
    token_count = tokens.shape[0]
    model_width = tokens.shape[1]
    capacity = 3 * token_count * TOP // (2 * expert_count)
    slot_count = expert_count * capacity
    row_count = token_count * TOP
    flat_ids = expert_ids.reshape(row_count)
    flat_probs = gate_probs.reshape(row_count)
    one_hot = (flat_ids[:, None] == jnp.arange(expert_count, dtype=jnp.int32)[None, :]).astype(
        jnp.float32
    )
    earlier = (jnp.arange(row_count)[:, None] > jnp.arange(row_count)[None, :]).astype(jnp.float32)
    counted = jnp.dot(earlier, one_hot, precision=lax.Precision.HIGHEST)
    slot_rank = jnp.sum(counted * one_hot, axis=1).astype(jnp.int32)
    target = flat_ids * capacity + slot_rank
    picked = jnp.arange(slot_count, dtype=jnp.int32)[:, None] == target[None, :]
    slot_probs = jnp.dot(picked.astype(jnp.float32), flat_probs, precision=lax.Precision.HIGHEST)
    pick_tokens = picked.reshape(slot_count, token_count, TOP).any(axis=2).astype(jnp.bfloat16)
    send_tokens = jnp.dot(pick_tokens, tokens, preferred_element_type=jnp.float32).astype(
        jnp.bfloat16
    )
    send_scaled = (
        jnp.dot(pick_tokens, cotangent, preferred_element_type=jnp.float32) * slot_probs[:, None]
    ).astype(jnp.bfloat16)
    whole = (
        lax.all_gather(gate_weight, "rep", axis=1, tiled=True),
        lax.all_gather(up_weight, "rep", axis=1, tiled=True),
        lax.all_gather(down_weight, "rep", axis=1, tiled=True),
    )
    gate_mat = whole[0][0]
    up_mat = whole[1][0]
    down_mat = whole[2][0]
    arrived = (
        lax.all_to_all(
            send_tokens.reshape(expert_count, capacity, model_width),
            ("grp", "exp"),
            split_axis=0,
            concat_axis=0,
            tiled=True,
        ),
        lax.all_to_all(
            send_scaled.reshape(expert_count, capacity, model_width),
            ("grp", "exp"),
            split_axis=0,
            concat_axis=0,
            tiled=True,
        ),
    )
    rows_in = arrived[0].reshape(slot_count, model_width)
    rows_scaled = arrived[1].reshape(slot_count, model_width)
    gate_pre = jnp.dot(rows_in, gate_mat, preferred_element_type=jnp.float32)
    up_pre = jnp.dot(rows_in, up_mat, preferred_element_type=jnp.float32)
    sigma = jax.nn.sigmoid(gate_pre)
    act = gate_pre * sigma
    hidden = (act * up_pre).astype(jnp.bfloat16)
    out_rows = jnp.dot(hidden, down_mat, preferred_element_type=jnp.float32).astype(jnp.bfloat16)
    dhidden = contract_cols(rows_scaled, down_mat)
    dgate = (dhidden * up_pre * sigma * (1.0 + gate_pre * (1.0 - sigma))).astype(jnp.bfloat16)
    dup = (dhidden * act).astype(jnp.bfloat16)
    grad_rows = (contract_cols(dgate, gate_mat) + contract_cols(dup, up_mat)).astype(jnp.bfloat16)
    returned = (
        lax.all_to_all(
            out_rows.reshape(expert_count, capacity, model_width),
            ("grp", "exp"),
            split_axis=0,
            concat_axis=0,
            tiled=True,
        ),
        lax.all_to_all(
            grad_rows.reshape(expert_count, capacity, model_width),
            ("grp", "exp"),
            split_axis=0,
            concat_axis=0,
            tiled=True,
        ),
    )
    replica = lax.axis_index("rep")
    other = 1 - replica
    half_width = gate_weight.shape[1]
    half_hidden = down_weight.shape[1]
    own_in = lax.dynamic_slice_in_dim(rows_in, replica * half_width, half_width, 1)
    own_hidden = lax.dynamic_slice_in_dim(hidden, replica * half_hidden, half_hidden, 1)
    send_in = lax.dynamic_slice_in_dim(rows_in, other * half_width, half_width, 1)
    send_hidden = lax.dynamic_slice_in_dim(hidden, other * half_hidden, half_hidden, 1)
    partner = partner_2((send_in, rows_scaled, send_hidden, dgate, dup), "rep", 0)
    gate_out = rounded_sum(contract_rows(own_in, dgate), contract_rows(partner[0], partner[3]))[
        None
    ]
    up_out = rounded_sum(contract_rows(own_in, dup), contract_rows(partner[0], partner[4]))[None]
    down_out = rounded_sum(
        contract_rows(own_hidden, rows_scaled), contract_rows(partner[2], partner[1])
    )[None]
    back_out = returned[0].reshape(slot_count, model_width)
    back_grad = returned[1].reshape(slot_count, model_width)
    route_out = jnp.dot(picked.T.astype(jnp.bfloat16), back_out, preferred_element_type=jnp.float32)
    layer_out = jnp.sum(
        route_out.reshape(token_count, TOP, model_width) * gate_probs[:, :, None], axis=1
    )
    token_grad = jnp.dot(pick_tokens.T, back_grad, preferred_element_type=jnp.float32)
    return (
        layer_out.astype(jnp.bfloat16),
        token_grad.astype(jnp.bfloat16),
        gate_out.astype(jnp.bfloat16),
        up_out.astype(jnp.bfloat16),
        down_out.astype(jnp.bfloat16),
    )


def solution(mesh):
    in_specs = (
        P(("grp", "exp", "rep"), None),
        P(("grp", "exp", "rep"), None),
        P(("grp", "exp", "rep"), None),
        P(("grp", "exp", "rep"), None),
        P(("grp", "exp"), "rep", None),
        P(("grp", "exp"), "rep", None),
        P(("grp", "exp"), "rep", None),
    )
    out_specs = (
        P(("grp", "exp", "rep"), None),
        P(("grp", "exp", "rep"), None),
        P(("grp", "exp"), "rep", None),
        P(("grp", "exp"), "rep", None),
        P(("grp", "exp"), "rep", None),
    )
    return jax.shard_map(local, mesh=mesh, in_specs=in_specs, out_specs=out_specs, check_vma=False)
```

profile of v0, /device:TPU:0, one launch (start us, length us, event | category | flops | bytes accessed | tf_op | source)
XLA Modules:
  0.0 197.2 jit_solution(9967073619924406575)
XLA Ops:
  9.1 1.8 multiply_convert_fusion
  10.9 8.4 %all-to-all-start.2 = ((bf16[16,24,2048]{2,1,0:T(8,128)(2,1)}), bf16[16,24,2048]{2,1,0:T(8,128)(2,1)}, u32[]{:S(2)}, u32[]{:S(2)}) async-start(bf16[16,24,2048]{2,1,0:T(8,128)(2,1)} %bitcast.9), calls=%async_computation.2 | async-start | bytes 3145728 | tf_op jit(solution)/shard_map/all_to_all | solution.py:76
  20.2 1.8 convolution_convert_fusion.2
  22.0 31.5 %all-to-all-done.2 = bf16[16,24,2048]{2,1,0:T(8,128)(2,1)} async-done(((bf16[16,24,2048]{2,1,0:T(8,128)(2,1)}), bf16[16,24,2048]{2,1,0:T(8,128)(2,1)}, u32[]{:S(2)}, u32[]{:S(2)}) %all-to-all-start.2) | async-done | bytes 1572896 | tf_op jit(solution)/shard_map/all_to_all | solution.py:76
  53.5 7.6 %all-to-all-start = ((bf16[16,24,2048]{2,1,0:T(8,128)(2,1)}), bf16[16,24,2048]{2,1,0:T(8,128)(2,1)S(1)}, u32[]{:S(2)}, u32[]{:S(2)}) async-start(bf16[16,24,2048]{2,1,0:T(8,128)(2,1)} %bitcast.1), calls=%async_computation | async-start | bytes 3145728 | tf_op jit(solution)/shard_map/all_to_all | solution.py:69
  61.9 3.8 %fusion = f32[384,768]{1,0:T(8,128)S(1)} fusion(bf16[384,2048]{1,0:T(8,128)(2,1)} %bitcast.10, bf16[1,768,2048]{2,1,0:T(8,128)(2,1)} %all-gather.8.cloned.1.call-done), kind=kOutput, calls=%fused_computation | convolution fusion | flops 1207959552 | bytes 5898240 | tf_op jit(solution)/shard_map/dot_general | solution.py:22
  65.7 28.9 %all-to-all-done = bf16[16,24,2048]{2,1,0:T(8,128)(2,1)S(1)} async-done(((bf16[16,24,2048]{2,1,0:T(8,128)(2,1)}), bf16[16,24,2048]{2,1,0:T(8,128)(2,1)S(1)}, u32[]{:S(2)}, u32[]{:S(2)}) %all-to-all-start) | async-done | bytes 1572896 | tf_op jit(solution)/shard_map/all_to_all | solution.py:69
  94.7 4.3 %fusion.6 = f32[384,768]{1,0:T(8,128)} fusion(bf16[384,2048]{1,0:T(8,128)(2,1)S(1)} %bitcast.64, bf16[1,2048,768]{2,1,0:T(8,128)(2,1)} %all-gather.6.cloned.1.call-done), kind=kOutput, calls=%fused_computation.6 | convolution fusion | flops 1207959552 | bytes 5898240 | tf_op jit(solution)/shard_map/dot_general | solution.py:87
  98.9 5.2 %multiply_convert_fusion.2 = (bf16[384,768]{1,0:T(8,128)(2,1)}, bf16[384,768]{1,0:T(8,128)(2,1)}, bf16[384,768]{1,0:T(8,128)(2,1)S(1)}) fusion(f32[384,768]{1,0:T(8,128)S(1)} %fusion, f32[384,768]{1,0:T(8,128)} %fusion.6, bf16[384,2048]{1,0:T(8,128)(2,1)S(1)} %bitcast.65, bf16[1,2048,768]{2,1,0:T(8,128)(2,1)} %all-gather.4.cloned.1.call-done), kind=kOutput, calls=%fused_computation.32 | convolution fusion | flops 1212383232 | bytes 8847360 | tf_op jit(solution)/shard_map/dot_general | solution.py:86
  104.1 2.5 %fusion.14 = bf16[384,2048]{1,0:T(8,128)(2,1)} fusion(bf16[384,768]{1,0:T(8,128)(2,1)S(1)} %get-tuple-element.7, bf16[1,768,2048]{2,1,0:T(8,128)(2,1)S(1)} %copy-done.10), kind=kOutput, calls=%fused_computation.17 | convolution fusion | flops 1208745984 | bytes 5308416 | tf_op jit(solution)/shard_map/dot_general | solution.py:91
  106.7 7.3 %all-to-all-start.1 = ((bf16[16,24,2048]{2,1,0:T(8,128)(2,1)}), bf16[16,24,2048]{2,1,0:T(8,128)(2,1)S(1)}, u32[]{:S(2)}, u32[]{:S(2)}) async-start(bf16[16,24,2048]{2,1,0:T(8,128)(2,1)} %bitcast.70), calls=%async_computation.1 | async-start | bytes 3145728 | tf_op jit(solution)/shard_map/all_to_all | solution.py:97
  116.0 3.7 %fusion.4 = f32[384,2048]{1,0:T(8,128)S(1)} fusion(bf16[384,768]{1,0:T(8,128)(2,1)} %get-tuple-element.6, bf16[1,2048,768]{2,1,0:T(8,128)(2,1)} %all-gather.6.cloned.1.call-done), kind=kOutput, calls=%fused_computation.4 | convolution fusion | flops 1207959552 | bytes 6881280 | tf_op jit(solution)/shard_map/dot_general | solution.py:22
  119.8 3.7 %add_convert_fusion.3 = bf16[384,2048]{1,0:T(8,128)(2,1)} fusion(f32[384,2048]{1,0:T(8,128)S(1)} %fusion.4, bf16[384,768]{1,0:T(8,128)(2,1)} %get-tuple-element.5, bf16[1,2048,768]{2,1,0:T(8,128)(2,1)S(1)} %copy-done.9), kind=kOutput, calls=%fused_computation.15 | convolution fusion | flops 1209532416 | bytes 8454144 | tf_op jit(solution)/shard_map/dot_general | solution.py:22
  123.5 3.2 %convolution_convert_fusion.7 = bf16[1024,768]{1,0:T(8,128)(2,1)} fusion(bf16[384,768]{1,0:T(8,128)(2,1)} %get-tuple-element.5, bf16[384,2048]{1,0:T(8,128)(2,1)S(1)} %bitcast.67, s32[]{:T(128)S(6)} %select_n.12), kind=kOutput, calls=%fused_computation.26 | convolution fusion | flops 604766208 | bytes 2949124 | tf_op jit(solution)/shard_map/dot_general | solution.py:16
  126.7 20.9 %all-to-all-done.1 = bf16[16,24,2048]{2,1,0:T(8,128)(2,1)S(1)} async-done(((bf16[16,24,2048]{2,1,0:T(8,128)(2,1)}), bf16[16,24,2048]{2,1,0:T(8,128)(2,1)S(1)}, u32[]{:S(2)}, u32[]{:S(2)}) %all-to-all-start.1) | async-done | bytes 1572896 | tf_op jit(solution)/shard_map/all_to_all | solution.py:97
  148.8 7.3 %all-to-all-start.3 = ((bf16[16,24,2048]{2,1,0:T(8,128)(2,1)}), bf16[16,24,2048]{2,1,0:T(8,128)(2,1)S(1)}, u32[]{:S(2)}, u32[]{:S(2)}) async-start(bf16[16,24,2048]{2,1,0:T(8,128)(2,1)} %bitcast.71), calls=%async_computation.3 | async-start | bytes 3145728 | tf_op jit(solution)/shard_map/all_to_all | solution.py:104
  156.1 2.1 %convolution_convert_fusion.5 = bf16[1024,768]{1,0:T(8,128)(2,1)S(1)} fusion(bf16[384,768]{1,0:T(8,128)(2,1)} %get-tuple-element.6, bf16[384,2048]{1,0:T(8,128)(2,1)S(1)} %bitcast.68, s32[]{:T(128)S(6)} %select_n.12), kind=kOutput, calls=%fused_computation.24 | convolution fusion | flops 604766208 | bytes 2949124 | tf_op jit(solution)/shard_map/dot_general | solution.py:16
  158.4 2.4 %convolution_convert_fusion.1 = bf16[384,2048]{1,0:T(8,128)(2,1)S(1)} fusion(bf16[384,2048]{1,0:T(8,128)(2,1)} %bitcast.10, bf16[384,768]{1,0:T(8,128)(2,1)S(1)} %copy-done.5, s32[]{:T(128)S(6)} %select_n.14), kind=kOutput, calls=%fused_computation.19 | convolution fusion | flops 604766208 | bytes 3440644 | tf_op jit(solution)/shard_map/dot_general | solution.py:16
  160.8 2.3 %convolution_convert_fusion.6 = bf16[1024,768]{1,0:T(8,128)(2,1)S(1)} fusion(bf16[384,1024]{1,0:T(8,128)(2,1)} %collective-permute-done, bf16[384,768]{1,0:T(8,128)(2,1)} %collective-permute-done.1), kind=kOutput, calls=%fused_computation.25 | convolution fusion | flops 604766208 | bytes 2949120 | tf_op jit(solution)/shard_map/dot_general | solution.py:16
  163.2 2.4 %convolution_convert_fusion.4 = bf16[1024,768]{1,0:T(8,128)(2,1)S(1)} fusion(bf16[384,1024]{1,0:T(8,128)(2,1)} %collective-permute-done, bf16[384,768]{1,0:T(8,128)(2,1)} %collective-permute-done.2), kind=kOutput, calls=%fused_computation.23 | convolution fusion | flops 604766208 | bytes 2949120 | tf_op jit(solution)/shard_map/dot_general | solution.py:16
  168.8 2.4 %convolution_convert_fusion = bf16[384,2048]{1,0:T(8,128)(2,1)S(1)} fusion(bf16[384,384]{1,0:T(8,128)(2,1)S(1)} %collective-permute-done.3, bf16[384,2048]{1,0:T(8,128)(2,1)} %collective-permute-done.4), kind=kOutput, calls=%fused_computation.18 | convolution fusion | flops 604766208 | bytes 3440640 | tf_op jit(solution)/shard_map/dot_general | solution.py:16
  171.3 1.8 fusion.19
  173.0 1.7 fusion.20
  174.7 15.0 %all-to-all-done.3 = bf16[16,24,2048]{2,1,0:T(8,128)(2,1)S(1)} async-done(((bf16[16,24,2048]{2,1,0:T(8,128)(2,1)}), bf16[16,24,2048]{2,1,0:T(8,128)(2,1)S(1)}, u32[]{:S(2)}, u32[]{:S(2)}) %all-to-all-start.3) | async-done | bytes 1572896 | tf_op jit(solution)/shard_map/all_to_all | solution.py:104
  (57 shorter events, 11.1 us)
Async XLA Ops:
  7.2 2.0 copy-start
  7.2 0.8 copy-start.7
  7.2 1.2 copy-start.8
  7.2 54.7 %all-gather.8.cloned.1.call-start = ((), (), s32[]{:S(2)}) async-start(), calls=%async_computation.6 | async-start | bytes 4718592 | tf_op jit(solution)/shard_map/all_gather | solution.py:63
  10.9 42.6 %all-to-all-start.2 = ((bf16[16,24,2048]{2,1,0:T(8,128)(2,1)}), bf16[16,24,2048]{2,1,0:T(8,128)(2,1)}, u32[]{:S(2)}, u32[]{:S(2)}) async-start(bf16[16,24,2048]{2,1,0:T(8,128)(2,1)} %bitcast.9), calls=%async_computation.2 | async-start | bytes 3145728 | tf_op jit(solution)/shard_map/all_to_all | solution.py:76
  19.3 0.9 copy-start.6
  19.3 75.4 %all-gather.6.cloned.1.call-start = ((), (), s32[]{:S(2)}) async-start(), calls=%async_computation.5 | async-start | bytes 4718592 | tf_op jit(solution)/shard_map/all_gather | solution.py:62
  53.5 41.1 %all-to-all-start = ((bf16[16,24,2048]{2,1,0:T(8,128)(2,1)}), bf16[16,24,2048]{2,1,0:T(8,128)(2,1)S(1)}, u32[]{:S(2)}, u32[]{:S(2)}) async-start(bf16[16,24,2048]{2,1,0:T(8,128)(2,1)} %bitcast.1), calls=%async_computation | async-start | bytes 3145728 | tf_op jit(solution)/shard_map/all_to_all | solution.py:69
  61.1 37.8 %all-gather.4.cloned.1.call-start = ((), (), s32[]{:S(2)}) async-start(), calls=%async_computation.4 | async-start | bytes 4718592 | tf_op jit(solution)/shard_map/all_gather | solution.py:61
  98.9 5.2 %copy-start.10 = (bf16[1,768,2048]{2,1,0:T(8,128)(2,1)S(1)}, bf16[1,768,2048]{2,1,0:T(8,128)(2,1)}, u32[]{:S(2)}) copy-start(bf16[1,768,2048]{2,1,0:T(8,128)(2,1)} %all-gather.8.cloned.1.call-done) | copy-start | bytes 9437188
  104.1 2.5 %copy-start.4 = (bf16[384,768]{1,0:T(8,128)(2,1)}, bf16[384,768]{1,0:T(8,128)(2,1)S(1)}, u32[]{:S(2)}) copy-start(bf16[384,768]{1,0:T(8,128)(2,1)S(1)} %get-tuple-element.7) | copy-start | bytes 1769476
  106.7 40.9 %all-to-all-start.1 = ((bf16[16,24,2048]{2,1,0:T(8,128)(2,1)}), bf16[16,24,2048]{2,1,0:T(8,128)(2,1)S(1)}, u32[]{:S(2)}, u32[]{:S(2)}) async-start(bf16[16,24,2048]{2,1,0:T(8,128)(2,1)} %bitcast.70), calls=%async_computation.1 | async-start | bytes 3145728 | tf_op jit(solution)/shard_map/all_to_all | solution.py:97
  114.0 54.8 %collective-permute-start.4 = (bf16[384,2048]{1,0:T(8,128)(2,1)}, bf16[384,2048]{1,0:T(8,128)(2,1)}, u32[]{:S(2)}, u32[]{:S(2)}) collective-permute-start(bf16[384,2048]{1,0:T(8,128)(2,1)} %bitcast.10), channel_id=1, source_target_pairs={{0,1},{1,0},{2,3},{3,2},{4,5},{5,4},{6,7},{7,6},{8,9},{9,8},{10,11... | collective-permute-start | bytes 4718600 | tf_op jit(solution)/shard_map/ppermute | solution.py:12
  115.0 45.8 %collective-permute-start = (bf16[384,1024]{1,0:T(8,128)(2,1)}, bf16[384,1024]{1,0:T(8,128)(2,1)}, u32[]{:S(2)}, u32[]{:S(2)}) collective-permute-start(bf16[384,1024]{1,0:T(8,128)(2,1)} %constant_dynamic-slice_fusion.1), channel_id=1, source_target_pairs={{0,1},{1,0},{2,3},{3,2},{4,5},{5,4},{6,7},{7,6},{8,9},{9,8},{10,11... | collective-permute-start | bytes 2359304 | tf_op jit(solution)/shard_map/ppermute | solution.py:12
  115.5 45.3 %collective-permute-start.1 = (bf16[384,768]{1,0:T(8,128)(2,1)}, bf16[384,768]{1,0:T(8,128)(2,1)}, u32[]{:S(2)}, u32[]{:S(2)}) collective-permute-start(bf16[384,768]{1,0:T(8,128)(2,1)} %get-tuple-element.5), channel_id=1, source_target_pairs={{0,1},{1,0},{2,3},{3,2},{4,5},{5,4},{6,7},{7,6},{8,9},{9,8},{10,11... | collective-permute-start | bytes 1769480 | tf_op jit(solution)/shard_map/ppermute | solution.py:12
  115.5 4.2 %copy-start.9 = (bf16[1,2048,768]{2,1,0:T(8,128)(2,1)S(1)}, bf16[1,2048,768]{2,1,0:T(8,128)(2,1)}, u32[]{:S(2)}) copy-start(bf16[1,2048,768]{2,1,0:T(8,128)(2,1)} %all-gather.4.cloned.1.call-done) | copy-start | bytes 9437188
  115.5 47.6 %collective-permute-start.2 = (bf16[384,768]{1,0:T(8,128)(2,1)}, bf16[384,768]{1,0:T(8,128)(2,1)}, u32[]{:S(2)}, u32[]{:S(2)}) collective-permute-start(bf16[384,768]{1,0:T(8,128)(2,1)} %get-tuple-element.6), channel_id=1, source_target_pairs={{0,1},{1,0},{2,3},{3,2},{4,5},{5,4},{6,7},{7,6},{8,9},{9,8},{10,11... | collective-permute-start | bytes 1769480 | tf_op jit(solution)/shard_map/ppermute | solution.py:12
  147.6 1.2 copy-start.1
  148.8 40.9 %all-to-all-start.3 = ((bf16[16,24,2048]{2,1,0:T(8,128)(2,1)}), bf16[16,24,2048]{2,1,0:T(8,128)(2,1)S(1)}, u32[]{:S(2)}, u32[]{:S(2)}) async-start(bf16[16,24,2048]{2,1,0:T(8,128)(2,1)} %bitcast.71), calls=%async_computation.3 | async-start | bytes 3145728 | tf_op jit(solution)/shard_map/all_to_all | solution.py:104
  156.1 2.2 %copy-start.5 = (bf16[384,768]{1,0:T(8,128)(2,1)S(1)}, bf16[384,768]{1,0:T(8,128)(2,1)}, u32[]{:S(2)}) copy-start(bf16[384,768]{1,0:T(8,128)(2,1)} %copy-done.4) | copy-start | bytes 1769476
  158.3 10.5 %collective-permute-start.3 = (bf16[384,384]{1,0:T(8,128)(2,1)S(1)}, bf16[384,384]{1,0:T(8,128)(2,1)S(1)}, u32[]{:S(2)}, u32[]{:S(2)}) collective-permute-start(bf16[384,384]{1,0:T(8,128)(2,1)S(1)} %constant_dynamic-slice_fusion), channel_id=1, source_target_pairs={{0,1},{1,0},{2,3},{3,2},{4,5},{5,4},{6,7},{7,6},{8,9},{9,8},{10,11... | collective-permute-start | bytes 884744 | tf_op jit(solution)/shard_map/ppermute | solution.py:12
  163.2 2.5 %copy-start.3 = (bf16[1024,768]{1,0:T(8,128)(2,1)S(1)}, bf16[1024,768]{1,0:T(8,128)(2,1)}, u32[]{:S(2)}) copy-start(bf16[1024,768]{1,0:T(8,128)(2,1)} %convolution_convert_fusion.7) | copy-start | bytes 4718596
  171.3 1.8 copy-start.2
Sparse Core Ops, SparseCore 0:
  9.6 14.8 all-gather.7
  26.0 13.2 all-gather.5
  63.5 13.4 all-gather.3
where the time goes:
time: 200 us; the launch traced here: 197 us
  waiting for transfers between devices  98.4 us (49%)
  matrix products  44.9 us (22%)
  starting transfers between devices  31.9 us (16%)
  between operations  14 us (7%)
  other arithmetic  5.17 us (3%)
  local copies, waits for them, and re-layouts  2.79 us (1%)
    all_to_all x1, waiting for transfers between devices, local(): lax.all_to_all(send_scaled.reshape(expert_count, capacity, model_width),...  31.5 us
    all_to_all x1, waiting for transfers between devices, local(): lax.all_to_all(send_tokens.reshape(expert_count, capacity, model_width),...  28.9 us
    all_to_all x1, waiting for transfers between devices, local(): lax.all_to_all(out_rows.reshape(expert_count, capacity, model_width), ('g...  20.9 us
    all_to_all x1, waiting for transfers between devices, local(): lax.all_to_all(grad_rows.reshape(expert_count, capacity, model_width), ('...  15 us
    dot_general x6, matrix products, contract_rows(): lax.dot_general(left, right, (((0,), (0,)), ((), ())), preferred_element_...  15 us
    dot_general x3, matrix products, contract_cols(): lax.dot_general(left, right, (((1,), (1,)), ((), ())), preferred_element_...  11.2 us
    all_to_all x1, starting transfers between devices, local(): lax.all_to_all(send_scaled.reshape(expert_count, capacity, model_width),...  8.36 us
    all_to_all x1, starting transfers between devices, local(): lax.all_to_all(send_tokens.reshape(expert_count, capacity, model_width),...  7.64 us
  transfers between devices with their start and end apart: 12, of which 4 were waited for; matrix products, arithmetic and copies ran while one was open for 22% of the time, Pallas kernels for 0%

commit v1 on v0

--- a/solution.py
+++ b/solution.py
@@ -30,7 +30,7 @@
     return left_part.astype(jnp.float32) + right_part.astype(jnp.float32)
 
 
-def local(tokens, cotangent, expert_ids, gate_probs, gate_weight, up_weight, down_weight):
+def routed_local(tokens, cotangent, expert_ids, gate_probs, gate_weight, up_weight, down_weight):
     group_count = lax.axis_size("grp")
     inner_count = lax.axis_size("exp")
     expert_count = group_count * inner_count
@@ -141,6 +141,113 @@
     )
 
 
+def shift_group(value, step):
+    count = lax.axis_size("grp")
+    return lax.ppermute(value, "grp", [(i, (i + step) % count) for i in range(count)])
+
+
+def swap_inner(value, masks):
+    inner, reps = lax.axis_size("exp"), lax.axis_size("rep")
+    pairs = [
+        (e * reps + r, (e ^ masks[r]) * reps + r) for e in range(inner) for r in range(reps)
+    ]
+    return lax.ppermute(value, ("exp", "rep"), pairs)
+
+
+FIRST, SECOND = (1, 2), (2, 1)
+
+
+def gather_blocks(block):
+    count = lax.axis_size("grp")
+    column = [block] + [shift_group(block, step) for step in range(1, count)]
+    first = [swap_inner(piece, FIRST) for piece in column]
+    second = [swap_inner(piece, SECOND) for piece in column]
+    both = [swap_inner(piece, SECOND) for piece in first]
+    return jnp.concatenate(column + first + second + both, axis=0)
+
+
+def add_bf16(left, right):
+    return (left.astype(jnp.float32) + right.astype(jnp.float32)).astype(jnp.bfloat16)
+
+
+def reduce_blocks(rows, cuts):
+    count = lax.axis_size("grp")
+    width = rows.shape[1]
+    blocks = rows.reshape(4, count, rows.shape[0] // (4 * count), width)
+    part = count // cuts
+    column = []
+    for cut in range(cuts):
+        here = blocks[:, cut * part : (cut + 1) * part]
+        kept = add_bf16(here[:2], swap_inner(here[2:], SECOND))
+        kept = add_bf16(kept[0], swap_inner(kept[1], FIRST))
+        column += [kept[i] for i in range(part)]
+    total = column[0].astype(jnp.float32)
+    for step in range(1, count):
+        total = total + shift_group(column[step], -step).astype(jnp.float32)
+    return total.astype(jnp.bfloat16)
+
+
+def route_weights(expert_ids, gate_probs, expert_count):
+    group_count, inner_count = lax.axis_size("grp"), lax.axis_size("exp")
+    named = expert_ids[None] == jnp.arange(expert_count, dtype=jnp.int32)[:, None, None]
+    dense = jnp.sum(jnp.where(named, gate_probs[None], 0.0), axis=2)
+    arrived = lax.all_to_all(dense, ("grp", "exp"), split_axis=0, concat_axis=0, tiled=True)
+    group, inner, replica = lax.axis_index("grp"), lax.axis_index("exp"), lax.axis_index("rep")
+    first = jnp.where(replica == 0, FIRST[0], FIRST[1])
+    second = jnp.where(replica == 0, SECOND[0], SECOND[1])
+    masks = jnp.stack([jnp.zeros_like(first), first, second, first ^ second])
+    source = (
+        jnp.mod(group - jnp.arange(group_count), group_count)[None, :] * inner_count
+        + (inner ^ masks)[:, None]
+    ).reshape(expert_count)
+    picked = source[:, None] == jnp.arange(expert_count)[None, :]
+    ordered = jnp.sum(jnp.where(picked[:, :, None], arrived[None], 0.0), axis=1)
+    return ordered.reshape(expert_count * expert_ids.shape[0], 1)
+
+
+def dense_local(tokens, cotangent, expert_ids, gate_probs, gate_weight, up_weight, down_weight):
+    expert_count = lax.axis_size("grp") * lax.axis_size("exp")
+    replica = lax.axis_index("rep")
+    gate_mat = lax.all_gather(gate_weight, "rep", axis=1, tiled=True)[0]
+    up_mat = lax.all_gather(up_weight, "rep", axis=1, tiled=True)[0]
+    down_mat = lax.all_gather(down_weight, "rep", axis=1, tiled=True)[0]
+    probs = route_weights(expert_ids, gate_probs, expert_count)
+    rows_in = gather_blocks(tokens)
+    rows_dy = gather_blocks(cotangent)
+    gate_pre = jnp.dot(rows_in, gate_mat, preferred_element_type=jnp.float32)
+    up_pre = jnp.dot(rows_in, up_mat, preferred_element_type=jnp.float32)
+    sigma = jax.nn.sigmoid(gate_pre)
+    act = gate_pre * sigma
+    hidden = (act * up_pre).astype(jnp.bfloat16)
+    out_rows = (jnp.dot(hidden, down_mat, preferred_element_type=jnp.float32) * probs).astype(
+        jnp.bfloat16
+    )
+    layer_out = reduce_blocks(out_rows, 2)
+    rows_scaled = (rows_dy.astype(jnp.float32) * probs).astype(jnp.bfloat16)
+    dhidden = contract_cols(rows_scaled, down_mat)
+    dgate = (dhidden * up_pre * sigma * (1.0 + gate_pre * (1.0 - sigma))).astype(jnp.bfloat16)
+    dup = (dhidden * act).astype(jnp.bfloat16)
+    grad_rows = (contract_cols(dgate, gate_mat) + contract_cols(dup, up_mat)).astype(jnp.bfloat16)
+    token_grad = reduce_blocks(grad_rows, 2)
+    half_width = gate_weight.shape[1]
+    half_hidden = down_weight.shape[1]
+
+    def half(value, which, size):
+        return lax.dynamic_slice_in_dim(value, which * size, size, 1)
+
+    other = 1 - replica
+    sent = (
+        contract_rows(half(rows_in, other, half_width), dgate).astype(jnp.bfloat16),
+        contract_rows(half(rows_in, other, half_width), dup).astype(jnp.bfloat16),
+        contract_rows(half(hidden, other, half_hidden), rows_scaled).astype(jnp.bfloat16),
+    )
+    partner = partner_2(sent, "rep", 0)
+    gate_out = add_bf16(contract_rows(half(rows_in, replica, half_width), dgate), partner[0])
+    up_out = add_bf16(contract_rows(half(rows_in, replica, half_width), dup), partner[1])
+    down_out = add_bf16(contract_rows(half(hidden, replica, half_hidden), rows_scaled), partner[2])
+    return layer_out, token_grad, gate_out[None], up_out[None], down_out[None]
+
+
 def solution(mesh):
     in_specs = (
         P(("grp", "exp", "rep"), None),
@@ -158,4 +265,7 @@
         P(("grp", "exp"), "rep", None),
         P(("grp", "exp"), "rep", None),
     )
+    sizes = dict(mesh.shape)
+    whole_blocks = sizes["exp"] == 4 and sizes["rep"] == 2 and sizes["grp"] * sizes["exp"] <= 2 * TOP
+    local = dense_local if whole_blocks else routed_local
     return jax.shard_map(local, mesh=mesh, in_specs=in_specs, out_specs=out_specs, check_vma=False)

time: 200 us -> 177 us (0.89); the launches traced: 197 us -> 177 us
  waiting for transfers between devices: 98.4 us -> 70.2 us
  starting transfers between devices: 31.9 us -> 46.2 us
  matrix products: 44.9 us -> 31.7 us
  local copies, waits for them, and re-layouts: 2.79 us -> 11.3 us
    all_to_all x4 -> x1, waiting for transfers between devices: 96.3 us -> 5.42 us  [route_weights(): lax.all_to_all(dense, ('grp', 'exp'), split_axis=0, concat_axis=0, tiled=...]
    ppermute x0 -> x44, waiting for transfers between devices: none -> 62.7 us  [the longest x32 47.4 us: swap_inner(): return lax.ppermute(value, ('exp', 'rep'), pairs)]
    ppermute x0 -> x44, starting transfers between devices: none -> 42 us  [the longest x32 25 us: swap_inner(): return lax.ppermute(value, ('exp', 'rep'), pairs)]
    all_to_all x4 -> x1, starting transfers between devices: 30.6 us -> 3.47 us  [route_weights(): lax.all_to_all(dense, ('grp', 'exp'), split_axis=0, concat_axis=0, tiled=...]
    unnamed x24 -> x46, local copies, waits for them, and re-layouts: 1.53 us -> 10.2 us
    dot_general x9 -> x3, matrix products: 18.7 us -> 13.2 us  [the longest x1 5.89 us: dense_local(): gate_pre = jnp.dot(rows_in, gate_mat, preferred_element_type=jnp.float32)]
    dot_general x6, matrix products: 15 us -> 10 us  [contract_rows(): lax.dot_general(left, right, (((0,), (0,)), ((), ())), preferred_element_...]
    dot_general x3, matrix products: 11.2 us -> 8.52 us  [contract_cols(): lax.dot_general(left, right, (((1,), (1,)), ((), ())), preferred_element_...]
  transfers between devices with their start and end apart: 12 -> 51, of which waited for: 4 -> 25; matrix products, arithmetic and copies ran while one was open for 22% -> 20% of each run, Pallas kernels for 0% -> 0%
where the time goes in v1:
time: 177 us
  waiting for transfers between devices  70.2 us (40%)
  starting transfers between devices  46.2 us (26%)
  matrix products  31.7 us (18%)
  between operations  14.2 us (8%)
  local copies, waits for them, and re-layouts  11.3 us (6%)
  other arithmetic  3.42 us (2%)
    ppermute x32, waiting for transfers between devices, swap_inner(): return lax.ppermute(value, ('exp', 'rep'), pairs)  47.4 us
    ppermute x32, starting transfers between devices, swap_inner(): return lax.ppermute(value, ('exp', 'rep'), pairs)  25 us
    ppermute x12, starting transfers between devices, shift_group(): lax.ppermute(value, 'grp', [(i, (i + step) % count) for i in range(count)])  17 us
    ppermute x12, waiting for transfers between devices, shift_group(): lax.ppermute(value, 'grp', [(i, (i + step) % count) for i in range(count)])  15.3 us
    unnamed x46, local copies, waits for them, and re-layouts  10.2 us
    dot_general x6, matrix products, contract_rows(): lax.dot_general(left, right, (((0,), (0,)), ((), ())), preferred_element_...  10 us
    dot_general x3, matrix products, contract_cols(): lax.dot_general(left, right, (((1,), (1,)), ((), ())), preferred_element_...  8.52 us
    dot_general x1, matrix products, dense_local(): gate_pre = jnp.dot(rows_in, gate_mat, preferred_element_type=jnp.float32)  5.89 us
  transfers between devices with their start and end apart: 51, of which 25 were waited for; matrix products, arithmetic and copies ran while one was open for 20% of the time, Pallas kernels for 0%

profile of v1, /device:TPU:0, one launch (start us, length us, event | category | flops | bytes accessed | tf_op | source)
XLA Modules:
  0.0 177.1 jit_solution(14025884112932173444)
XLA Ops:
  8.7 3.1 %collective-permute-start.22 = (bf16[32,2048]{1,0:T(8,128)(2,1)S(1)}, bf16[32,2048]{1,0:T(8,128)(2,1)S(1)}, u32[]{:S(2)}, u32[]{:S(2)}) collective-permute-start(bf16[32,2048]{1,0:T(8,128)(2,1)S(1)} %copy-done), channel_id=1, source_target_pairs={{0,8},{8,16},{16,24},{24,0},{1,9},{9,17},{17,25},{25,1},{2,10},{10... | collective-permute-start | bytes 393224 | tf_op jit(solution)/shard_map/ppermute | solution.py:146
  11.8 2.6 %collective-permute-start.23 = (bf16[32,2048]{1,0:T(8,128)(2,1)S(1)}, bf16[32,2048]{1,0:T(8,128)(2,1)S(1)}, u32[]{:S(2)}, u32[]{:S(2)}) collective-permute-start(bf16[32,2048]{1,0:T(8,128)(2,1)S(1)} %copy-done), channel_id=1, source_target_pairs={{0,16},{8,24},{16,0},{24,8},{1,17},{9,25},{17,1},{25,9},{2,18},{10... | collective-permute-start | bytes 393224 | tf_op jit(solution)/shard_map/ppermute | solution.py:146
  19.4 3.5 %all-to-all-start = ((f32[16,1,32]{2,1,0:T(1,128)}), f32[16,1,32]{2,1,0:T(1,128)S(1)}, u32[]{:S(2)}, u32[]{:S(2)}) async-start(f32[16,1,32]{2,1,0:T(1,128)} %bitcast.7), calls=%async_computation | async-start | bytes 16384 | tf_op jit(solution)/shard_map/all_to_all | solution.py:194
  24.6 5.4 %all-to-all-done = f32[16,1,32]{2,1,0:T(1,128)S(1)} async-done(((f32[16,1,32]{2,1,0:T(1,128)}), f32[16,1,32]{2,1,0:T(1,128)S(1)}, u32[]{:S(2)}, u32[]{:S(2)}) %all-to-all-start) | async-done | bytes 2080 | tf_op jit(solution)/shard_map/all_to_all | solution.py:194
  31.4 2.8 %collective-permute-start.2 = (bf16[32,2048]{1,0:T(8,128)(2,1)S(1)}, bf16[32,2048]{1,0:T(8,128)(2,1)S(1)}, u32[]{:S(2)}, u32[]{:S(2)}) collective-permute-start(bf16[32,2048]{1,0:T(8,128)(2,1)S(1)} %copy-done.1), channel_id=1, source_target_pairs={{0,24},{8,0},{16,8},{24,16},{1,25},{9,1},{17,9},{25,17},{2,26},{10... | collective-permute-start | bytes 393224 | tf_op jit(solution)/shard_map/ppermute | solution.py:146
  34.9 2.9 %collective-permute-done = bf16[32,2048]{1,0:T(8,128)(2,1)S(1)} collective-permute-done((bf16[32,2048]{1,0:T(8,128)(2,1)S(1)}, bf16[32,2048]{1,0:T(8,128)(2,1)S(1)}, u32[]{:S(2)}, u32[]{:S(2)}) %collective-permute-start) | collective-permute-done | bytes 131104 | tf_op jit(solution)/shard_map/ppermute | solution.py:146
  47.4 2.8 %collective-permute-done.27 = bf16[32,2048]{1,0:T(8,128)(2,1)S(1)} collective-permute-done((bf16[32,2048]{1,0:T(8,128)(2,1)S(1)}, bf16[32,2048]{1,0:T(8,128)(2,1)S(1)}, u32[]{:S(2)}, u32[]{:S(2)}) %collective-permute-start.27) | collective-permute-done | bytes 131104 | tf_op jit(solution)/shard_map/ppermute | solution.py:154
  50.2 2.8 %collective-permute-done.28 = bf16[32,2048]{1,0:T(8,128)(2,1)S(1)} collective-permute-done((bf16[32,2048]{1,0:T(8,128)(2,1)S(1)}, bf16[32,2048]{1,0:T(8,128)(2,1)S(1)}, u32[]{:S(2)}, u32[]{:S(2)}) %collective-permute-start.28) | collective-permute-done | bytes 131104 | tf_op jit(solution)/shard_map/ppermute | solution.py:154
  53.0 2.1 %collective-permute-start.33 = (bf16[32,2048]{1,0:T(8,128)(2,1)S(1)}, bf16[32,2048]{1,0:T(8,128)(2,1)S(1)}, u32[]{:S(2)}, u32[]{:S(2)}) collective-permute-start(bf16[32,2048]{1,0:T(8,128)(2,1)S(1)} %collective-permute-done.25), channel_id=1, source_target_pairs={{0,4},{1,3},{2,6},{3,1},{4,0},{5,7},{6,2},{7,5},{8,12},{9,11},{10,... | collective-permute-start | bytes 393224 | tf_op jit(solution)/shard_map/ppermute | solution.py:154
  65.1 2.1 %collective-permute-done.6 = bf16[32,2048]{1,0:T(8,128)(2,1)S(1)} collective-permute-done((bf16[32,2048]{1,0:T(8,128)(2,1)S(1)}, bf16[32,2048]{1,0:T(8,128)(2,1)S(1)}, u32[]{:S(2)}, u32[]{:S(2)}) %collective-permute-start.6) | collective-permute-done | bytes 131104 | tf_op jit(solution)/shard_map/ppermute | solution.py:154
  67.9 2.0 %collective-permute-start.34 = (bf16[32,2048]{1,0:T(8,128)(2,1)S(1)}, bf16[32,2048]{1,0:T(8,128)(2,1)S(1)}, u32[]{:S(2)}, u32[]{:S(2)}) collective-permute-start(bf16[32,2048]{1,0:T(8,128)(2,1)S(1)} %collective-permute-done.26), channel_id=1, source_target_pairs={{0,4},{1,3},{2,6},{3,1},{4,0},{5,7},{6,2},{7,5},{8,12},{9,11},{10,... | collective-permute-start | bytes 393224 | tf_op jit(solution)/shard_map/ppermute | solution.py:154
  82.9 5.5 %fusion.5 = f32[512,768]{1,0:T(8,128)} fusion(bf16[512,2048]{1,0:T(8,128)(2,1)} %constant_dynamic-update-slice_fusion, bf16[1,2048,768]{2,1,0:T(8,128)(2,1)} %all-gather.6.cloned.1.call-done), kind=kOutput, calls=%fused_computation.8 | convolution fusion | flops 1610612736 | bytes 6815744 | tf_op jit(solution)/shard_map/dot_general | solution.py:218
  88.4 4.9 %fusion = f32[512,768]{1,0:T(8,128)} fusion(bf16[1,768,2048]{2,1,0:T(8,128)(2,1)} %all-gather.8.cloned.1.call-done, bf16[512,2048]{1,0:T(8,128)(2,1)S(1)} %constant_dynamic-update-slice_fusion.16, f32[512]{0:T(512)S(1)} %mul.62), kind=kOutput, calls=%fused_computation.3 | convolution fusion | flops 1613758464 | bytes 6817792 | tf_op jit(solution)/shard_map/dot_general | solution.py:22
  93.2 5.9 %multiply_convert_fusion.3 = (bf16[512,768]{1,0:T(8,128)(2,1)S(1)}, bf16[512,768]{1,0:T(8,128)(2,1)S(1)}, bf16[512,768]{1,0:T(8,128)(2,1)S(1)}) fusion(f32[512,768]{1,0:T(8,128)} %fusion, f32[512,768]{1,0:T(8,128)} %fusion.5, bf16[512,2048]{1,0:T(8,128)(2,1)} %constant_dynamic-update-slice_fusion, bf16[1,2048,768]{2,1,0:T(8,128)(2,1)} %all-gather.4.cloned.1.call-done), kind=kOutput, calls=%fused_computation.22 | convolution fusion | flops 1616510976 | bytes 10747904 | tf_op jit(solution)/shard_map/dot_general | solution.py:217
  113.2 2.8 %collective-permute-done.18 = bf16[2,2,32,2048]{3,2,1,0:T(8,128)(2,1)S(1)} collective-permute-done((bf16[2,2,32,2048]{3,2,1,0:T(8,128)(2,1)S(1)}, bf16[2,2,32,2048]{3,2,1,0:T(8,128)(2,1)S(1)}, u32[]{:S(2)}, u32[]{:S(2)}) %collective-permute-start.18) | collective-permute-done | bytes 524320 | tf_op jit(solution)/shard_map/ppermute | solution.py:154
  116.5 10.3 %collective-permute-done.37 = bf16[2,2,32,2048]{3,2,1,0:T(8,128)(2,1)S(1)} collective-permute-done((bf16[2,2,32,2048]{3,2,1,0:T(8,128)(2,1)S(1)}, bf16[2,2,32,2048]{3,2,1,0:T(8,128)(2,1)S(1)}, u32[]{:S(2)}, u32[]{:S(2)}) %collective-permute-start.37) | collective-permute-done | bytes 524320 | tf_op jit(solution)/shard_map/ppermute | solution.py:154
  126.9 11.2 %collective-permute-done.40 = bf16[2,2,32,2048]{3,2,1,0:T(8,128)(2,1)S(1)} collective-permute-done((bf16[2,2,32,2048]{3,2,1,0:T(8,128)(2,1)S(1)}, bf16[2,2,32,2048]{3,2,1,0:T(8,128)(2,1)S(1)}, u32[]{:S(2)}, u32[]{:S(2)}) %collective-permute-start.40) | collective-permute-done | bytes 524320 | tf_op jit(solution)/shard_map/ppermute | solution.py:154
  138.6 2.1 %collective-permute-start.38 = (bf16[2,32,2048]{2,1,0:T(8,128)(2,1)S(1)}, bf16[2,32,2048]{2,1,0:T(8,128)(2,1)S(1)}, u32[]{:S(2)}, u32[]{:S(2)}) collective-permute-start(bf16[2,32,2048]{2,1,0:T(8,128)(2,1)S(1)} %slice_bitcast_fusion.2), channel_id=1, source_target_pairs={{0,2},{1,5},{2,0},{3,7},{4,6},{5,1},{6,4},{7,3},{8,10},{9,13},{10,... | collective-permute-start | bytes 786440 | tf_op jit(solution)/shard_map/ppermute | solution.py:154
  140.9 4.0 %collective-permute-done.41 = bf16[2,32,2048]{2,1,0:T(8,128)(2,1)S(1)} collective-permute-done((bf16[2,32,2048]{2,1,0:T(8,128)(2,1)S(1)}, bf16[2,32,2048]{2,1,0:T(8,128)(2,1)S(1)}, u32[]{:S(2)}, u32[]{:S(2)}) %collective-permute-start.41) | collective-permute-done | bytes 262176 | tf_op jit(solution)/shard_map/ppermute | solution.py:154
  154.5 2.8 %collective-permute-done.43 = bf16[32,2048]{1,0:T(8,128)(2,1)S(1)} collective-permute-done((bf16[32,2048]{1,0:T(8,128)(2,1)S(1)}, bf16[32,2048]{1,0:T(8,128)(2,1)S(1)}, u32[]{:S(2)}, u32[]{:S(2)}) %collective-permute-start.43) | collective-permute-done | bytes 131104 | tf_op jit(solution)/shard_map/ppermute | solution.py:146
  158.2 3.6 %collective-permute-done.42 = bf16[32,2048]{1,0:T(8,128)(2,1)S(1)} collective-permute-done((bf16[32,2048]{1,0:T(8,128)(2,1)S(1)}, bf16[32,2048]{1,0:T(8,128)(2,1)S(1)}, u32[]{:S(2)}, u32[]{:S(2)}) %collective-permute-start.42) | collective-permute-done | bytes 131104 | tf_op jit(solution)/shard_map/ppermute | solution.py:146
  163.9 2.2 %fusion.15 = bf16[1,1024,768]{2,1,0:T(8,128)(2,1)} fusion(bf16[1024,768]{1,0:T(8,128)(2,1)S(1)} %collective-permute-done.44, bf16[512,768]{1,0:T(8,128)(2,1)S(1)} %get-tuple-element.5, bf16[512,2048]{1,0:T(8,128)(2,1)S(1)} %copy-done.2, s32[]{:T(128)S(6)} %select_n.45), kind=kOutput, calls=%fused_computation.26 | convolution fusion | flops 807665664 | bytes 4980740 | tf_op jit(solution)/shard_map/dot_general | solution.py:16
  166.1 2.2 %fusion.16 = bf16[1,1024,768]{2,1,0:T(8,128)(2,1)} fusion(bf16[1024,768]{1,0:T(8,128)(2,1)S(1)} %collective-permute-done.45, bf16[512,768]{1,0:T(8,128)(2,1)S(1)} %get-tuple-element.6, bf16[512,2048]{1,0:T(8,128)(2,1)S(1)} %copy-done.2, s32[]{:T(128)S(6)} %select_n.45), kind=kOutput, calls=%fused_computation.27 | convolution fusion | flops 807665664 | bytes 4980740 | tf_op jit(solution)/shard_map/dot_general | solution.py:16
  168.3 2.3 %fusion.13 = bf16[1,384,2048]{2,1,0:T(8,128)(2,1)} fusion(bf16[384,2048]{1,0:T(8,128)(2,1)S(1)} %collective-permute-done.46, bf16[512,768]{1,0:T(8,128)(2,1)S(1)} %get-tuple-element.7, s32[]{:T(128)S(6)} %select_n.47, bf16[512,2048]{1,0:T(8,128)(2,1)S(1)} %constant_dynamic-update-slice_fusion.16, f32[512]{0:T(512)S(1)} %mul.62), kind=kOutput, calls=%fused_computation.18 | convolution fusion | flops 810811392 | bytes 5638148 | tf_op jit(solution)/shard_map/dot_general | solution.py:16
  (166 shorter events, 71.0 us)
Async XLA Ops:
  7.2 75.7 %all-gather.6.cloned.1.call-start = ((), (), s32[]{:S(2)}) async-start(), calls=%async_computation.2 | async-start | bytes 4718592 | tf_op jit(solution)/shard_map/all_gather | solution.py:212
  7.9 80.4 %all-gather.8.cloned.1.call-start = ((), (), s32[]{:S(2)}) async-start(), calls=%async_computation.3 | async-start | bytes 4718592 | tf_op jit(solution)/shard_map/all_gather | solution.py:213
  8.7 21.5 %collective-permute-start.22 = (bf16[32,2048]{1,0:T(8,128)(2,1)S(1)}, bf16[32,2048]{1,0:T(8,128)(2,1)S(1)}, u32[]{:S(2)}, u32[]{:S(2)}) collective-permute-start(bf16[32,2048]{1,0:T(8,128)(2,1)S(1)} %copy-done), channel_id=1, source_target_pairs={{0,8},{8,16},{16,24},{24,0},{1,9},{9,17},{17,25},{25,1},{2,10},{10... | collective-permute-start | bytes 393224 | tf_op jit(solution)/shard_map/ppermute | solution.py:146
  11.8 19.0 %collective-permute-start.23 = (bf16[32,2048]{1,0:T(8,128)(2,1)S(1)}, bf16[32,2048]{1,0:T(8,128)(2,1)S(1)}, u32[]{:S(2)}, u32[]{:S(2)}) collective-permute-start(bf16[32,2048]{1,0:T(8,128)(2,1)S(1)} %copy-done), channel_id=1, source_target_pairs={{0,16},{8,24},{16,0},{24,8},{1,17},{9,25},{17,1},{25,9},{2,18},{10... | collective-permute-start | bytes 393224 | tf_op jit(solution)/shard_map/ppermute | solution.py:146
  14.4 17.1 %collective-permute-start.24 = (bf16[32,2048]{1,0:T(8,128)(2,1)S(1)}, bf16[32,2048]{1,0:T(8,128)(2,1)S(1)}, u32[]{:S(2)}, u32[]{:S(2)}) collective-permute-start(bf16[32,2048]{1,0:T(8,128)(2,1)S(1)} %copy-done), channel_id=1, source_target_pairs={{0,24},{8,0},{16,8},{24,16},{1,25},{9,1},{17,9},{25,17},{2,26},{10... | collective-permute-start | bytes 393224 | tf_op jit(solution)/shard_map/ppermute | solution.py:146
  15.7 18.5 %collective-permute-start.25 = (bf16[32,2048]{1,0:T(8,128)(2,1)S(1)}, bf16[32,2048]{1,0:T(8,128)(2,1)S(1)}, u32[]{:S(2)}, u32[]{:S(2)}) collective-permute-start(bf16[32,2048]{1,0:T(8,128)(2,1)S(1)} %copy-done), channel_id=1, source_target_pairs={{0,2},{1,5},{2,0},{3,7},{4,6},{5,1},{6,4},{7,3},{8,10},{9,13},{10,... | collective-permute-start | bytes 393224 | tf_op jit(solution)/shard_map/ppermute | solution.py:154
  17.2 35.8 %collective-permute-start.29 = (bf16[32,2048]{1,0:T(8,128)(2,1)S(1)}, bf16[32,2048]{1,0:T(8,128)(2,1)S(1)}, u32[]{:S(2)}, u32[]{:S(2)}) collective-permute-start(bf16[32,2048]{1,0:T(8,128)(2,1)S(1)} %copy-done), channel_id=1, source_target_pairs={{0,4},{1,3},{2,6},{3,1},{4,0},{5,7},{6,2},{7,5},{8,12},{9,11},{10,... | collective-permute-start | bytes 393224 | tf_op jit(solution)/shard_map/ppermute | solution.py:154
  19.4 10.6 %all-to-all-start = ((f32[16,1,32]{2,1,0:T(1,128)}), f32[16,1,32]{2,1,0:T(1,128)S(1)}, u32[]{:S(2)}, u32[]{:S(2)}) async-start(f32[16,1,32]{2,1,0:T(1,128)} %bitcast.7), calls=%async_computation | async-start | bytes 16384 | tf_op jit(solution)/shard_map/all_to_all | solution.py:194
  22.8 70.4 %all-gather.4.cloned.1.call-start = ((), (), s32[]{:S(2)}) async-start(), calls=%async_computation.1 | async-start | bytes 4718592 | tf_op jit(solution)/shard_map/all_gather | solution.py:211
  30.8 10.2 %collective-permute-start.1 = (bf16[32,2048]{1,0:T(8,128)(2,1)S(1)}, bf16[32,2048]{1,0:T(8,128)(2,1)S(1)}, u32[]{:S(2)}, u32[]{:S(2)}) collective-permute-start(bf16[32,2048]{1,0:T(8,128)(2,1)S(1)} %copy-done.1), channel_id=1, source_target_pairs={{0,16},{8,24},{16,0},{24,8},{1,17},{9,25},{17,1},{25,9},{2,18},{10... | collective-permute-start | bytes 393224 | tf_op jit(solution)/shard_map/ppermute | solution.py:146
  31.4 10.8 %collective-permute-start.2 = (bf16[32,2048]{1,0:T(8,128)(2,1)S(1)}, bf16[32,2048]{1,0:T(8,128)(2,1)S(1)}, u32[]{:S(2)}, u32[]{:S(2)}) collective-permute-start(bf16[32,2048]{1,0:T(8,128)(2,1)S(1)} %copy-done.1), channel_id=1, source_target_pairs={{0,24},{8,0},{16,8},{24,16},{1,25},{9,1},{17,9},{25,17},{2,26},{10... | collective-permute-start | bytes 393224 | tf_op jit(solution)/shard_map/ppermute | solution.py:146
  34.2 10.1 %collective-permute-start.3 = (bf16[32,2048]{1,0:T(8,128)(2,1)S(1)}, bf16[32,2048]{1,0:T(8,128)(2,1)S(1)}, u32[]{:S(2)}, u32[]{:S(2)}) collective-permute-start(bf16[32,2048]{1,0:T(8,128)(2,1)S(1)} %copy-done.1), channel_id=1, source_target_pairs={{0,2},{1,5},{2,0},{3,7},{4,6},{5,1},{6,4},{7,3},{8,10},{9,13},{10,... | collective-permute-start | bytes 393224 | tf_op jit(solution)/shard_map/ppermute | solution.py:154
  37.8 30.1 %collective-permute-start.7 = (bf16[32,2048]{1,0:T(8,128)(2,1)S(1)}, bf16[32,2048]{1,0:T(8,128)(2,1)S(1)}, u32[]{:S(2)}, u32[]{:S(2)}) collective-permute-start(bf16[32,2048]{1,0:T(8,128)(2,1)S(1)} %copy-done.1), channel_id=1, source_target_pairs={{0,4},{1,3},{2,6},{3,1},{4,0},{5,7},{6,2},{7,5},{8,12},{9,11},{10,... | collective-permute-start | bytes 393224 | tf_op jit(solution)/shard_map/ppermute | solution.py:154
  60.0 10.6 %collective-permute-start.8 = (bf16[32,2048]{1,0:T(8,128)(2,1)S(1)}, bf16[32,2048]{1,0:T(8,128)(2,1)S(1)}, u32[]{:S(2)}, u32[]{:S(2)}) collective-permute-start(bf16[32,2048]{1,0:T(8,128)(2,1)S(1)} %collective-permute-done), channel_id=1, source_target_pairs={{0,4},{1,3},{2,6},{3,1},{4,0},{5,7},{6,2},{7,5},{8,12},{9,11},{10,... | collective-permute-start | bytes 393224 | tf_op jit(solution)/shard_map/ppermute | solution.py:154
  61.6 9.6 %collective-permute-start.9 = (bf16[32,2048]{1,0:T(8,128)(2,1)S(1)}, bf16[32,2048]{1,0:T(8,128)(2,1)S(1)}, u32[]{:S(2)}, u32[]{:S(2)}) collective-permute-start(bf16[32,2048]{1,0:T(8,128)(2,1)S(1)} %collective-permute-done.1), channel_id=1, source_target_pairs={{0,4},{1,3},{2,6},{3,1},{4,0},{5,7},{6,2},{7,5},{8,12},{9,11},{10,... | collective-permute-start | bytes 393224 | tf_op jit(solution)/shard_map/ppermute | solution.py:154
  101.1 11.5 %collective-permute-start.15 = (bf16[2,2,32,2048]{3,2,1,0:T(8,128)(2,1)S(1)}, bf16[2,2,32,2048]{3,2,1,0:T(8,128)(2,1)S(1)}, u32[]{:S(2)}, u32[]{:S(2)}) collective-permute-start(bf16[2,2,32,2048]{3,2,1,0:T(8,128)(2,1)S(1)} %get-tuple-element.14), channel_id=1, source_target_pairs={{0,4},{1,3},{2,6},{3,1},{4,0},{5,7},{6,2},{7,5},{8,12},{9,11},{10,... | collective-permute-start | bytes 1572872 | tf_op jit(solution)/shard_map/ppermute | solution.py:154
  101.9 14.1 %collective-permute-start.18 = (bf16[2,2,32,2048]{3,2,1,0:T(8,128)(2,1)S(1)}, bf16[2,2,32,2048]{3,2,1,0:T(8,128)(2,1)S(1)}, u32[]{:S(2)}, u32[]{:S(2)}) collective-permute-start(bf16[2,2,32,2048]{3,2,1,0:T(8,128)(2,1)S(1)} %get-tuple-element.15), channel_id=1, source_target_pairs={{0,4},{1,3},{2,6},{3,1},{4,0},{5,7},{6,2},{7,5},{8,12},{9,11},{10,... | collective-permute-start | bytes 1572872 | tf_op jit(solution)/shard_map/ppermute | solution.py:154
  107.0 19.8 %collective-permute-start.37 = (bf16[2,2,32,2048]{3,2,1,0:T(8,128)(2,1)S(1)}, bf16[2,2,32,2048]{3,2,1,0:T(8,128)(2,1)S(1)}, u32[]{:S(2)}, u32[]{:S(2)}) collective-permute-start(bf16[2,2,32,2048]{3,2,1,0:T(8,128)(2,1)S(1)} %get-tuple-element.10), channel_id=1, source_target_pairs={{0,4},{1,3},{2,6},{3,1},{4,0},{5,7},{6,2},{7,5},{8,12},{9,11},{10,... | collective-permute-start | bytes 1572872 | tf_op jit(solution)/shard_map/ppermute | solution.py:154
  107.8 30.2 %collective-permute-start.40 = (bf16[2,2,32,2048]{3,2,1,0:T(8,128)(2,1)S(1)}, bf16[2,2,32,2048]{3,2,1,0:T(8,128)(2,1)S(1)}, u32[]{:S(2)}, u32[]{:S(2)}) collective-permute-start(bf16[2,2,32,2048]{3,2,1,0:T(8,128)(2,1)S(1)} %get-tuple-element.11), channel_id=1, source_target_pairs={{0,4},{1,3},{2,6},{3,1},{4,0},{5,7},{6,2},{7,5},{8,12},{9,11},{10,... | collective-permute-start | bytes 1572872 | tf_op jit(solution)/shard_map/ppermute | solution.py:154
  110.4 53.5 %collective-permute-start.44 = (bf16[1024,768]{1,0:T(8,128)(2,1)S(1)}, bf16[1024,768]{1,0:T(8,128)(2,1)S(1)}, u32[]{:S(2)}, u32[]{:S(2)}) collective-permute-start(bf16[1024,768]{1,0:T(8,128)(2,1)S(1)} %convolution_convert_fusion.2), channel_id=1, source_target_pairs={{0,1},{1,0},{2,3},{3,2},{4,5},{5,4},{6,7},{7,6},{8,9},{9,8},{10,11... | collective-permute-start | bytes 4718600 | tf_op jit(solution)/shard_map/ppermute | solution.py:12
  112.6 53.5 %collective-permute-start.45 = (bf16[1024,768]{1,0:T(8,128)(2,1)S(1)}, bf16[1024,768]{1,0:T(8,128)(2,1)S(1)}, u32[]{:S(2)}, u32[]{:S(2)}) collective-permute-start(bf16[1024,768]{1,0:T(8,128)(2,1)S(1)} %convolution_convert_fusion.1), channel_id=1, source_target_pairs={{0,1},{1,0},{2,3},{3,2},{4,5},{5,4},{6,7},{7,6},{8,9},{9,8},{10,11... | collective-permute-start | bytes 4718600 | tf_op jit(solution)/shard_map/ppermute | solution.py:12
  116.4 22.2 %collective-permute-start.19 = (bf16[2,32,2048]{2,1,0:T(8,128)(2,1)S(1)}, bf16[2,32,2048]{2,1,0:T(8,128)(2,1)S(1)}, u32[]{:S(2)}, u32[]{:S(2)}) collective-permute-start(bf16[2,32,2048]{2,1,0:T(8,128)(2,1)S(1)} %slice_bitcast_fusion.4), channel_id=1, source_target_pairs={{0,2},{1,5},{2,0},{3,7},{4,6},{5,1},{6,4},{7,3},{8,10},{9,13},{10,... | collective-permute-start | bytes 786440 | tf_op jit(solution)/shard_map/ppermute | solution.py:154
  126.8 13.9 %collective-permute-start.16 = (bf16[2,32,2048]{2,1,0:T(8,128)(2,1)S(1)}, bf16[2,32,2048]{2,1,0:T(8,128)(2,1)S(1)}, u32[]{:S(2)}, u32[]{:S(2)}) collective-permute-start(bf16[2,32,2048]{2,1,0:T(8,128)(2,1)S(1)} %slice_bitcast_fusion.6), channel_id=1, source_target_pairs={{0,2},{1,5},{2,0},{3,7},{4,6},{5,1},{6,4},{7,3},{8,10},{9,13},{10,... | collective-permute-start | bytes 786440 | tf_op jit(solution)/shard_map/ppermute | solution.py:154
  150.8 17.5 %collective-permute-start.46 = (bf16[384,2048]{1,0:T(8,128)(2,1)S(1)}, bf16[384,2048]{1,0:T(8,128)(2,1)S(1)}, u32[]{:S(2)}, u32[]{:S(2)}) collective-permute-start(bf16[384,2048]{1,0:T(8,128)(2,1)S(1)} %convolution_convert_fusion), channel_id=1, source_target_pairs={{0,1},{1,0},{2,3},{3,2},{4,5},{5,4},{6,7},{7,6},{8,9},{9,8},{10,11... | collective-permute-start | bytes 4718600 | tf_op jit(solution)/shard_map/ppermute | solution.py:12
  (35 other events, 247.4 us)
Sparse Core Ops, SparseCore 0:
  9.6 14.8 all-gather.5
  26.0 13.2 all-gather.7
  40.9 13.2 all-gather.3

commit v2 on v1

--- a/solution.py
+++ b/solution.py
@@ -1,6 +1,10 @@
+import functools
+
 import jax
 import jax.numpy as jnp
 from jax import lax
+from jax.experimental import pallas as pl
+from jax.experimental.pallas import tpu as pltpu
 from jax.sharding import PartitionSpec as P
 
 TOP = 8
@@ -141,6 +145,13 @@
     )
 
 
+FIRST, SECOND = (1, 2), (2, 1)
+VMEM_LIMIT = 56 * 2**20
+ANY = pl.BlockSpec(memory_space=pl.ANY)
+VMEM = pl.BlockSpec(memory_space=pltpu.VMEM)
+SMEM = pl.BlockSpec(memory_space=pltpu.SMEM)
+
+
 def shift_group(value, step):
     count = lax.axis_size("grp")
     return lax.ppermute(value, "grp", [(i, (i + step) % count) for i in range(count)])
@@ -154,36 +165,41 @@
     return lax.ppermute(value, ("exp", "rep"), pairs)
 
 
-FIRST, SECOND = (1, 2), (2, 1)
+def steps_of(count):
+    return [(q + 1) % count for q in range(count)]
 
 
 def gather_blocks(block):
     count = lax.axis_size("grp")
-    column = [block] + [shift_group(block, step) for step in range(1, count)]
+    moved = {0: block, 1: shift_group(block, 1), count - 1: shift_group(block, -1)}
+    for step in range(2, count - 1):
+        moved[step] = shift_group(moved[step - 1], 1)
+    column = [moved[step] for step in steps_of(count)]
     first = [swap_inner(piece, FIRST) for piece in column]
     second = [swap_inner(piece, SECOND) for piece in column]
     both = [swap_inner(piece, SECOND) for piece in first]
-    return jnp.concatenate(column + first + second + both, axis=0)
+    return column + first + second + both
 
 
 def add_bf16(left, right):
     return (left.astype(jnp.float32) + right.astype(jnp.float32)).astype(jnp.bfloat16)
 
 
-def reduce_blocks(rows, cuts):
+def reduce_blocks(keep, sends, rows):
     count = lax.axis_size("grp")
-    width = rows.shape[1]
-    blocks = rows.reshape(4, count, rows.shape[0] // (4 * count), width)
-    part = count // cuts
+    width = keep.shape[1]
+    keep = keep.reshape(2, count * rows, width)
+    part = count // len(sends) * rows
     column = []
-    for cut in range(cuts):
-        here = blocks[:, cut * part : (cut + 1) * part]
-        kept = add_bf16(here[:2], swap_inner(here[2:], SECOND))
-        kept = add_bf16(kept[0], swap_inner(kept[1], FIRST))
-        column += [kept[i] for i in range(part)]
-    total = column[0].astype(jnp.float32)
-    for step in range(1, count):
-        total = total + shift_group(column[step], -step).astype(jnp.float32)
+    for cut, send in enumerate(sends):
+        here = keep[:, cut * part : (cut + 1) * part]
+        came = swap_inner(send, SECOND).reshape(2, part, width)
+        passed = swap_inner(add_bf16(here[1], came[1]), FIRST)
+        total = add_bf16(here[0].astype(jnp.float32) + came[0].astype(jnp.float32), passed)
+        column += [total[i * rows : (i + 1) * rows] for i in range(part // rows)]
+    total = column[-1].astype(jnp.float32)
+    for piece, step in zip(column[:-1], steps_of(count)):
+        total = total + shift_group(piece, -step).astype(jnp.float32)
     return total.astype(jnp.bfloat16)
 
 
@@ -196,55 +212,205 @@
     first = jnp.where(replica == 0, FIRST[0], FIRST[1])
     second = jnp.where(replica == 0, SECOND[0], SECOND[1])
     masks = jnp.stack([jnp.zeros_like(first), first, second, first ^ second])
+    steps = jnp.mod(jnp.arange(group_count) + 1, group_count)
     source = (
-        jnp.mod(group - jnp.arange(group_count), group_count)[None, :] * inner_count
-        + (inner ^ masks)[:, None]
+        jnp.mod(group - steps, group_count)[None, :] * inner_count + (inner ^ masks)[:, None]
     ).reshape(expert_count)
     picked = source[:, None] == jnp.arange(expert_count)[None, :]
     ordered = jnp.sum(jnp.where(picked[:, :, None], arrived[None], 0.0), axis=1)
     return ordered.reshape(expert_count * expert_ids.shape[0], 1)
 
 
+def start_halves(halves, whole, sems, first_sem, replica):
+    own, partner = halves
+    size = own.shape[0]
+    copies = []
+    for k, (half, which) in enumerate(((own, replica), (partner, 1 - replica))):
+        place = pl.ds(pl.multiple_of(which * size, size), size)
+        copies.append(pltpu.make_async_copy(half, whole.at[place, :], sems.at[first_sem + k]))
+        copies[-1].start()
+    return copies
+
+
+def start_rows(pieces, whole, offset, rows, sems):
+    copies = []
+    for k, piece in enumerate(pieces):
+        copies.append(
+            pltpu.make_async_copy(
+                piece.at[pl.ds(offset, rows), :], whole.at[pl.ds(k * rows, rows), :], sems.at[k]
+            )
+        )
+        copies[-1].start()
+    return copies
+
+
+def wait_all(copies):
+    for copy in copies:
+        copy.wait()
+
+
+def tile_of(size, most=256):
+    return most if size % most == 0 else size
+
+
+def forward_kernel(rows, count, replica_ref, probs_ref, *refs):
+    pieces, refs = refs[:count], refs[count:]
+    gate, up, down = refs[0:2], refs[2:4], refs[4:6]
+    keep_ref, send_ref, gate_pre_ref, up_pre_ref, hidden_ref, rows_ref = refs[6:12]
+    gate_all, up_all, down_all, row_sems, weight_sems = refs[12:]
+    replica = replica_ref[0]
+    row_copies = start_rows(pieces, rows_ref, 0, rows, row_sems)
+    gate_copies = start_halves(gate, gate_all, weight_sems, 0, replica)
+    up_copies = start_halves(up, up_all, weight_sems, 2, replica)
+    down_copies = start_halves(down, down_all, weight_sems, 4, replica)
+    wait_all(row_copies + gate_copies + up_copies)
+    tile = tile_of(gate_all.shape[1])
+
+    @pl.loop(0, gate_all.shape[1] // tile)
+    def _(i):
+        cols = pl.ds(pl.multiple_of(i * tile, tile), tile)
+        gate_pre = jnp.dot(rows_ref[...], gate_all[:, cols], preferred_element_type=jnp.float32)
+        up_pre = jnp.dot(rows_ref[...], up_all[:, cols], preferred_element_type=jnp.float32)
+        gate_pre_ref[:, cols] = gate_pre
+        up_pre_ref[:, cols] = up_pre
+        hidden_ref[:, cols] = (gate_pre * jax.nn.sigmoid(gate_pre) * up_pre).astype(jnp.bfloat16)
+
+    wait_all(down_copies)
+    half = keep_ref.shape[0]
+    tile = tile_of(down_all.shape[1])
+
+    @pl.loop(0, down_all.shape[1] // tile)
+    def _(i):
+        cols = pl.ds(pl.multiple_of(i * tile, tile), tile)
+        out = jnp.dot(hidden_ref[...], down_all[:, cols], preferred_element_type=jnp.float32)
+        out = (out * probs_ref[...]).astype(jnp.bfloat16)
+        keep_ref[:, cols] = out[:half]
+        send_ref[:, cols] = out[half:]
+
+
+def backward_kernel(rows, count, replica_ref, probs_ref, gate_pre_ref, up_pre_ref, *refs):
+    pieces, refs = refs[:count], refs[count:]
+    gate, up, down = refs[0:2], refs[2:4], refs[4:6]
+    keep_ref, near_ref, far_ref, dgate_ref, dup_ref, scaled_ref = refs[6:12]
+    gate_all, up_all, down_all, row_sems, weight_sems = refs[12:]
+    replica = replica_ref[0]
+    row_copies = start_rows(pieces, scaled_ref, rows, rows, row_sems)
+    down_copies = start_halves(down, down_all, weight_sems, 4, replica)
+    gate_copies = start_halves(gate, gate_all, weight_sems, 0, replica)
+    up_copies = start_halves(up, up_all, weight_sems, 2, replica)
+    wait_all(row_copies)
+    scaled_ref[...] = (scaled_ref[...].astype(jnp.float32) * probs_ref[...]).astype(jnp.bfloat16)
+    wait_all(down_copies)
+    tile = tile_of(down_all.shape[0])
+
+    @pl.loop(0, down_all.shape[0] // tile)
+    def _(i):
+        cols = pl.ds(pl.multiple_of(i * tile, tile), tile)
+        dhidden = contract_cols(scaled_ref[...], down_all[cols, :])
+        gate_pre, up_pre = gate_pre_ref[:, cols], up_pre_ref[:, cols]
+        sigma = jax.nn.sigmoid(gate_pre)
+        dgate_ref[:, cols] = (
+            dhidden * up_pre * sigma * (1.0 + gate_pre * (1.0 - sigma))
+        ).astype(jnp.bfloat16)
+        dup_ref[:, cols] = (dhidden * (gate_pre * sigma)).astype(jnp.bfloat16)
+
+    wait_all(gate_copies + up_copies)
+    half = keep_ref.shape[0]
+    part = half // 4
+    tile = tile_of(gate_all.shape[0])
+
+    @pl.loop(0, gate_all.shape[0] // tile)
+    def _(i):
+        cols = pl.ds(pl.multiple_of(i * tile, tile), tile)
+        grad = contract_cols(dgate_ref[...], gate_all[cols, :])
+        grad = (grad + contract_cols(dup_ref[...], up_all[cols, :])).astype(jnp.bfloat16)
+        keep_ref[:, cols] = grad[:half]
+        for g in range(2):
+            start = half + 2 * g * part
+            near_ref[g * part : (g + 1) * part, cols] = grad[start : start + part]
+            far_ref[g * part : (g + 1) * part, cols] = grad[start + part : start + 2 * part]
+
+
+def expert_call(kernel, outs, width, hidden_width, count, total, matmuls, inputs, in_specs):
+    return pl.pallas_call(
+        kernel,
+        out_shape=[jax.ShapeDtypeStruct(shape, dtype) for shape, dtype in outs],
+        in_specs=in_specs,
+        out_specs=[VMEM] * len(outs),
+        scratch_shapes=[
+            pltpu.VMEM((width, hidden_width), jnp.bfloat16),
+            pltpu.VMEM((width, hidden_width), jnp.bfloat16),
+            pltpu.VMEM((hidden_width, width), jnp.bfloat16),
+            pltpu.SemaphoreType.DMA((count,)),
+            pltpu.SemaphoreType.DMA((6,)),
+        ],
+        compiler_params=pltpu.CompilerParams(vmem_limit_bytes=VMEM_LIMIT),
+        cost_estimate=pl.CostEstimate(
+            flops=2 * matmuls * total * width * hidden_width,
+            bytes_accessed=6 * width * hidden_width + 8 * total * width,
+            transcendentals=total * hidden_width,
+        ),
+    )(*inputs)
+
+
 def dense_local(tokens, cotangent, expert_ids, gate_probs, gate_weight, up_weight, down_weight):
     expert_count = lax.axis_size("grp") * lax.axis_size("exp")
     replica = lax.axis_index("rep")
-    gate_mat = lax.all_gather(gate_weight, "rep", axis=1, tiled=True)[0]
-    up_mat = lax.all_gather(up_weight, "rep", axis=1, tiled=True)[0]
-    down_mat = lax.all_gather(down_weight, "rep", axis=1, tiled=True)[0]
+    rows, width = tokens.shape
+    half_width, hidden_width = gate_weight.shape[1:]
+    half_hidden = down_weight.shape[1]
+    total = expert_count * rows
+    own = (gate_weight[0], up_weight[0], down_weight[0])
+    partner = partner_2(own, "rep", 0)
+    weights = [value for pair in zip(own, partner) for value in pair]
     probs = route_weights(expert_ids, gate_probs, expert_count)
-    rows_in = gather_blocks(tokens)
-    rows_dy = gather_blocks(cotangent)
-    gate_pre = jnp.dot(rows_in, gate_mat, preferred_element_type=jnp.float32)
-    up_pre = jnp.dot(rows_in, up_mat, preferred_element_type=jnp.float32)
-    sigma = jax.nn.sigmoid(gate_pre)
-    act = gate_pre * sigma
-    hidden = (act * up_pre).astype(jnp.bfloat16)
-    out_rows = (jnp.dot(hidden, down_mat, preferred_element_type=jnp.float32) * probs).astype(
-        jnp.bfloat16
-    )
-    layer_out = reduce_blocks(out_rows, 2)
-    rows_scaled = (rows_dy.astype(jnp.float32) * probs).astype(jnp.bfloat16)
-    dhidden = contract_cols(rows_scaled, down_mat)
-    dgate = (dhidden * up_pre * sigma * (1.0 + gate_pre * (1.0 - sigma))).astype(jnp.bfloat16)
-    dup = (dhidden * act).astype(jnp.bfloat16)
-    grad_rows = (contract_cols(dgate, gate_mat) + contract_cols(dup, up_mat)).astype(jnp.bfloat16)
-    token_grad = reduce_blocks(grad_rows, 2)
-    half_width = gate_weight.shape[1]
-    half_hidden = down_weight.shape[1]
+    pieces = gather_blocks(jnp.concatenate([tokens, cotangent], axis=0))
+    which = replica.astype(jnp.int32).reshape(1)
+    bf16, f32 = jnp.bfloat16, jnp.float32
+    out_keep, out_send, gate_pre, up_pre, hidden, rows_in = expert_call(
+        functools.partial(forward_kernel, rows, expert_count),
+        [
+            ((total // 2, width), bf16),
+            ((total // 2, width), bf16),
+            ((total, hidden_width), f32),
+            ((total, hidden_width), f32),
+            ((total, hidden_width), bf16),
+            ((total, width), bf16),
+        ],
+        width, hidden_width, expert_count, total, 3,
+        [which, probs, *pieces, *weights],
+        [SMEM, VMEM] + [ANY] * (expert_count + 6),
+    )
+    layer_out = reduce_blocks(out_keep, [out_send], rows)
+    grad_keep, grad_near, grad_far, dgate, dup, rows_scaled = expert_call(
+        functools.partial(backward_kernel, rows, expert_count),
+        [
+            ((total // 2, width), bf16),
+            ((total // 4, width), bf16),
+            ((total // 4, width), bf16),
+            ((total, hidden_width), bf16),
+            ((total, hidden_width), bf16),
+            ((total, width), bf16),
+        ],
+        width, hidden_width, expert_count, total, 3,
+        [which, probs, gate_pre, up_pre, *pieces, *weights],
+        [SMEM, VMEM, VMEM, VMEM] + [ANY] * (expert_count + 6),
+    )
+    token_grad = reduce_blocks(grad_keep, [grad_near, grad_far], rows)
 
     def half(value, which, size):
         return lax.dynamic_slice_in_dim(value, which * size, size, 1)
 
     other = 1 - replica
     sent = (
-        contract_rows(half(rows_in, other, half_width), dgate).astype(jnp.bfloat16),
-        contract_rows(half(rows_in, other, half_width), dup).astype(jnp.bfloat16),
-        contract_rows(half(hidden, other, half_hidden), rows_scaled).astype(jnp.bfloat16),
-    )
-    partner = partner_2(sent, "rep", 0)
-    gate_out = add_bf16(contract_rows(half(rows_in, replica, half_width), dgate), partner[0])
-    up_out = add_bf16(contract_rows(half(rows_in, replica, half_width), dup), partner[1])
-    down_out = add_bf16(contract_rows(half(hidden, replica, half_hidden), rows_scaled), partner[2])
+        contract_rows(half(rows_in, other, half_width), dgate).astype(bf16),
+        contract_rows(half(rows_in, other, half_width), dup).astype(bf16),
+        contract_rows(half(hidden, other, half_hidden), rows_scaled).astype(bf16),
+    )
+    back = partner_2(sent, "rep", 0)
+    gate_out = add_bf16(contract_rows(half(rows_in, replica, half_width), dgate), back[0])
+    up_out = add_bf16(contract_rows(half(rows_in, replica, half_width), dup), back[1])
+    down_out = add_bf16(contract_rows(half(hidden, replica, half_hidden), rows_scaled), back[2])
     return layer_out, token_grad, gate_out[None], up_out[None], down_out[None]
 
 

time: 177 us -> 160 us (0.904)
  Pallas kernels: 0 us -> 30.6 us
  matrix products: 31.7 us -> 11.2 us
  between operations: 14.2 us -> 0.94 us
  waiting for transfers between devices: 70.2 us -> 59.5 us
  local copies, waits for them, and re-layouts: 11.3 us -> 5.33 us
  starting transfers between devices: 46.2 us -> 48.7 us
    pallas_call x0 -> x2, Pallas kernels: none -> 30.6 us  [expert_call(): pl.pallas_call(kernel, out_shape=[jax.ShapeDtypeStruct(shape, dtype) for...]
    dot_general x6 -> x0, matrix products: 21.7 us -> none  [the longest x3 8.52 us: contract_cols(): lax.dot_general(left, right, (((1,), (1,)), ((), ())), preferred_element_...]
    unnamed x46 -> x37, local copies, waits for them, and re-layouts: 10.2 us -> 3.29 us
    all_to_all x1, waiting for transfers between devices: 5.42 us -> 0.01 us  [route_weights(): lax.all_to_all(dense, ('grp', 'exp'), split_axis=0, concat_axis=0, tiled=...]
    unnamed x3 -> x0, waiting for transfers between devices: 2.06 us -> none
    ppermute x32 -> x18, starting transfers between devices: 25 us -> 26.9 us  [swap_inner(): return lax.ppermute(value, ('exp', 'rep'), pairs)]
    ppermute x12 -> x9, waiting for transfers between devices: 15.3 us -> 13.7 us  [shift_group(): lax.ppermute(value, 'grp', [(i, (i + step) % count) for i in range(count)])]
    ppermute x32 -> x18, waiting for transfers between devices: 47.4 us -> 45.8 us  [swap_inner(): return lax.ppermute(value, ('exp', 'rep'), pairs)]
  transfers between devices with their start and end apart: 51 -> 34, of which waited for: 25 -> 15; matrix products, arithmetic and copies ran while one was open for 20% -> 10% of each run, Pallas kernels for 0% -> 0%
where the time goes in v2:
time: 160 us
  waiting for transfers between devices  59.5 us (37%)
  starting transfers between devices  48.7 us (30%)
  Pallas kernels  30.6 us (19%)
  matrix products  11.2 us (7%)
  local copies, waits for them, and re-layouts  5.33 us (3%)
  other arithmetic  3.82 us (2%)
    ppermute x18, waiting for transfers between devices, swap_inner(): return lax.ppermute(value, ('exp', 'rep'), pairs)  45.8 us
    pallas_call x2, Pallas kernels, expert_call(): pl.pallas_call(kernel, out_shape=[jax.ShapeDtypeStruct(shape, dtype) for...  30.6 us
    ppermute x18, starting transfers between devices, swap_inner(): return lax.ppermute(value, ('exp', 'rep'), pairs)  26.9 us
    ppermute x9, starting transfers between devices, shift_group(): lax.ppermute(value, 'grp', [(i, (i + step) % count) for i in range(count)])  17.2 us
    ppermute x9, waiting for transfers between devices, shift_group(): lax.ppermute(value, 'grp', [(i, (i + step) % count) for i in range(count)])  13.7 us
    dot_general x6, matrix products, contract_rows(): lax.dot_general(left, right, (((0,), (0,)), ((), ())), preferred_element_...  11.2 us
    all_to_all x1, starting transfers between devices, route_weights(): lax.all_to_all(dense, ('grp', 'exp'), split_axis=0, concat_axis=0, tiled=...  3.47 us
    unnamed x37, local copies, waits for them, and re-layouts  3.29 us
  transfers between devices with their start and end apart: 34, of which 15 were waited for; matrix products, arithmetic and copies ran while one was open for 10% of the time, Pallas kernels for 0%

profile of v2, /device:TPU:0, one launch (start us, length us, event | category | flops | bytes accessed | tf_op | source)
XLA Modules:
  0.0 160.1 jit_solution(14084445260517609531)
XLA Ops:
  2.5 3.1 %collective-permute-start = (bf16[64,2048]{1,0:T(8,128)(2,1)S(1)}, bf16[64,2048]{1,0:T(8,128)(2,1)S(1)}, u32[]{:S(2)}, u32[]{:S(2)}) collective-permute-start(bf16[64,2048]{1,0:T(8,128)(2,1)S(1)} %constant_dynamic-update-slice_fusion.refs_3_), channel_id=1, source_target_pairs={{0,8},{8,16},{16,24},{24,0},{1,9},{9,17},{17,25},{25,1},{2,10},{10... | collective-permute-start | bytes 786440 | tf_op jit(solution)/shard_map/ppermute | solution.py:157
  5.6 2.1 %collective-permute-start.2 = (bf16[64,2048]{1,0:T(8,128)(2,1)S(1)}, bf16[64,2048]{1,0:T(8,128)(2,1)S(1)}, u32[]{:S(2)}, u32[]{:S(2)}) collective-permute-start(bf16[64,2048]{1,0:T(8,128)(2,1)S(1)} %constant_dynamic-update-slice_fusion.refs_3_), channel_id=1, source_target_pairs={{0,24},{8,0},{16,8},{24,16},{1,25},{9,1},{17,9},{25,17},{2,26},{10... | collective-permute-start | bytes 786440 | tf_op jit(solution)/shard_map/ppermute | solution.py:157
  10.8 3.9 %collective-permute-done.refs_0_ = bf16[64,2048]{1,0:T(8,128)(2,1)S(1)} collective-permute-done((bf16[64,2048]{1,0:T(8,128)(2,1)S(1)}, bf16[64,2048]{1,0:T(8,128)(2,1)S(1)}, u32[]{:S(2)}, u32[]{:S(2)}) %collective-permute-start) | collective-permute-done | bytes 262176 | tf_op jit(solution)/shard_map/ppermute | solution.py:157
  14.8 4.4 %collective-permute-done.2.refs_2_ = bf16[64,2048]{1,0:T(8,128)(2,1)S(1)} collective-permute-done((bf16[64,2048]{1,0:T(8,128)(2,1)S(1)}, bf16[64,2048]{1,0:T(8,128)(2,1)S(1)}, u32[]{:S(2)}, u32[]{:S(2)}) %collective-permute-start.2) | collective-permute-done | bytes 262176 | tf_op jit(solution)/shard_map/ppermute | solution.py:157
  21.4 3.8 %collective-permute-done.1.refs_1_ = bf16[64,2048]{1,0:T(8,128)(2,1)} collective-permute-done((bf16[64,2048]{1,0:T(8,128)(2,1)S(1)}, bf16[64,2048]{1,0:T(8,128)(2,1)}, u32[]{:S(2)}, u32[]{:S(2)}) %collective-permute-start.1) | collective-permute-done | bytes 262176 | tf_op jit(solution)/shard_map/ppermute | solution.py:157
  28.3 6.1 %collective-permute-done.5.refs_6_ = bf16[64,2048]{1,0:T(8,128)(2,1)S(1)} collective-permute-done((bf16[64,2048]{1,0:T(8,128)(2,1)S(1)}, bf16[64,2048]{1,0:T(8,128)(2,1)S(1)}, u32[]{:S(2)}, u32[]{:S(2)}) %collective-permute-start.5) | collective-permute-done | bytes 262176 | tf_op jit(solution)/shard_map/ppermute | solution.py:165
  36.5 5.2 %collective-permute-done.9.refs_10_ = bf16[64,2048]{1,0:T(8,128)(2,1)S(1)} collective-permute-done((bf16[64,2048]{1,0:T(8,128)(2,1)S(1)}, bf16[64,2048]{1,0:T(8,128)(2,1)S(1)}, u32[]{:S(2)}, u32[]{:S(2)}) %collective-permute-start.9) | collective-permute-done | bytes 262176 | tf_op jit(solution)/shard_map/ppermute | solution.py:165
  45.1 3.5 %all-to-all-start = ((f32[16,1,32]{2,1,0:T(1,128)}), f32[16,1,32]{2,1,0:T(1,128)S(1)}, u32[]{:S(2)}, u32[]{:S(2)}) async-start(f32[16,1,32]{2,1,0:T(1,128)} %bitcast.5), calls=%async_computation | async-start | bytes 16384 | tf_op jit(solution)/shard_map/all_to_all | solution.py:210
  48.6 1.9 %collective-permute-start.8 = (bf16[64,2048]{1,0:T(8,128)(2,1)}, bf16[64,2048]{1,0:T(8,128)(2,1)}, u32[]{:S(2)}, u32[]{:S(2)}) collective-permute-start(bf16[64,2048]{1,0:T(8,128)(2,1)} %collective-permute-done.1.refs_1_), channel_id=1, source_target_pairs={{0,4},{1,3},{2,6},{3,1},{4,0},{5,7},{6,2},{7,5},{8,12},{9,11},{10,... | collective-permute-start | bytes 786440 | tf_op jit(solution)/shard_map/ppermute | solution.py:165
  52.6 2.8 %collective-permute-done.8.refs_9_ = bf16[64,2048]{1,0:T(8,128)(2,1)} collective-permute-done((bf16[64,2048]{1,0:T(8,128)(2,1)}, bf16[64,2048]{1,0:T(8,128)(2,1)}, u32[]{:S(2)}, u32[]{:S(2)}) %collective-permute-start.8) | collective-permute-done | bytes 262176 | tf_op jit(solution)/shard_map/ppermute | solution.py:165
  62.1 2.8 %collective-permute-done.12.refs_13_ = bf16[64,2048]{1,0:T(8,128)(2,1)} collective-permute-done((bf16[64,2048]{1,0:T(8,128)(2,1)}, bf16[64,2048]{1,0:T(8,128)(2,1)}, u32[]{:S(2)}, u32[]{:S(2)}) %collective-permute-start.12) | collective-permute-done | bytes 262176 | tf_op jit(solution)/shard_map/ppermute | solution.py:165
  66.6 14.9 %shard_map.110 = (bf16[256,2048]{1,0:T(8,128)(2,1)}, bf16[256,2048]{1,0:T(8,128)(2,1)}, f32[512,768]{1,0:T(8,128)}, f32[512,768]{1,0:T(8,128)}, bf16[512,768]{1,0:T(8,128)(2,1)}, /*index=5*/bf16[512,2048]{1,0:T(8,128)(2,1)}) custom-call(s32[1]{0:T(128)} %bitcast.replica_ref, f32[512,1]{1,0:T(8,128)} %reshape.154.probs_ref, bf16[64,2048]{1,0:T(8,128)(2,1)} %copy-done.6, ...), custom_call_target="tpu_custom_call" | custom-call | flops 4831838208 | bytes 17825792 | tf_op jit(solution)/shard_map/pallas_call | solution.py:335
  81.5 15.7 %shard_map.111 = (bf16[256,2048]{1,0:T(8,128)(2,1)}, bf16[128,2048]{1,0:T(8,128)(2,1)}, bf16[128,2048]{1,0:T(8,128)(2,1)}, bf16[512,768]{1,0:T(8,128)(2,1)}, bf1...) custom-call(s32[1]{0:T(128)} %bitcast.replica_ref, f32[512,1]{1,0:T(8,128)} %reshape.154.probs_ref, ...), custom_call_target="tpu_custom_call" | custom-call | flops 4831838208 | bytes 17825792 | tf_op jit(solution)/shard_map/pallas_call | solution.py:335
  101.1 2.6 %convolution_convert_fusion.2 = bf16[1024,768]{1,0:T(8,128)(2,1)S(1)} fusion(bf16[512,768]{1,0:T(8,128)(2,1)} %get-tuple-element.25, bf16[512,2048]{1,0:T(8,128)(2,1)} %get-tuple-element.24, s32[]{:T(128)S(6)} %select_n.55), kind=kOutput, calls=%fused_computation.6 | convolution fusion | flops 806092800 | bytes 3407876 | tf_op jit(solution)/shard_map/dot_general | solution.py:20
  103.8 3.4 %collective-permute-done.25 = bf16[128,2048]{1,0:T(8,128)(2,1)S(1)} collective-permute-done((bf16[128,2048]{1,0:T(8,128)(2,1)}, bf16[128,2048]{1,0:T(8,128)(2,1)S(1)}, u32[]{:S(2)}, u32[]{:S(2)}) %collective-permute-start.25) | collective-permute-done | bytes 524320 | tf_op jit(solution)/shard_map/ppermute | solution.py:165
  109.6 18.7 %collective-permute-done.23 = bf16[128,2048]{1,0:T(8,128)(2,1)S(1)} collective-permute-done((bf16[128,2048]{1,0:T(8,128)(2,1)}, bf16[128,2048]{1,0:T(8,128)(2,1)S(1)}, u32[]{:S(2)}, u32[]{:S(2)}) %collective-permute-start.23) | collective-permute-done | bytes 524320 | tf_op jit(solution)/shard_map/ppermute | solution.py:165
  128.5 2.3 %collective-permute-start.24 = (bf16[64,2048]{1,0:T(8,128)(2,1)S(1)}, bf16[64,2048]{1,0:T(8,128)(2,1)S(1)}, u32[]{:S(2)}, u32[]{:S(2)}) collective-permute-start(bf16[64,2048]{1,0:T(8,128)(2,1)S(1)} %get-tuple-element.30), channel_id=1, source_target_pairs={{0,2},{1,5},{2,0},{3,7},{4,6},{5,1},{6,4},{7,3},{8,10},{9,13},{10,... | collective-permute-start | bytes 786440 | tf_op jit(solution)/shard_map/ppermute | solution.py:165
  130.9 2.8 %collective-permute-start.28 = (bf16[32,2048]{1,0:T(8,128)(2,1)S(1)}, bf16[32,2048]{1,0:T(8,128)(2,1)S(1)}, u32[]{:S(2)}, u32[]{:S(2)}) collective-permute-start(bf16[32,2048]{1,0:T(8,128)(2,1)S(1)} %get-tuple-element.35), channel_id=1, source_target_pairs={{0,16},{8,24},{16,0},{24,8},{1,17},{9,25},{17,1},{25,9},{2,18},{10... | collective-permute-start | bytes 393224 | tf_op jit(solution)/shard_map/ppermute | solution.py:157
  135.3 2.4 %collective-permute-start.29 = (bf16[32,2048]{1,0:T(8,128)(2,1)S(1)}, bf16[32,2048]{1,0:T(8,128)(2,1)S(1)}, u32[]{:S(2)}, u32[]{:S(2)}) collective-permute-start(bf16[32,2048]{1,0:T(8,128)(2,1)S(1)} %slice.111), channel_id=1, source_target_pairs={{0,8},{8,16},{16,24},{24,0},{1,9},{9,17},{17,25},{25,1},{2,10},{10... | collective-permute-start | bytes 393224 | tf_op jit(solution)/shard_map/ppermute | solution.py:157
  143.3 3.9 %collective-permute-done.19 = bf16[128,2048]{1,0:T(8,128)(2,1)S(1)} collective-permute-done((bf16[128,2048]{1,0:T(8,128)(2,1)S(1)}, bf16[128,2048]{1,0:T(8,128)(2,1)S(1)}, u32[]{:S(2)}, u32[]{:S(2)}) %collective-permute-start.19) | collective-permute-done | bytes 524320 | tf_op jit(solution)/shard_map/ppermute | solution.py:165
  149.9 2.8 %collective-permute-start.20 = (bf16[32,2048]{1,0:T(8,128)(2,1)S(1)}, bf16[32,2048]{1,0:T(8,128)(2,1)S(1)}, u32[]{:S(2)}, u32[]{:S(2)}) collective-permute-start(bf16[32,2048]{1,0:T(8,128)(2,1)S(1)} %get-tuple-element.31), channel_id=1, source_target_pairs={{0,24},{8,0},{16,8},{24,16},{1,25},{9,1},{17,9},{25,17},{2,26},{10... | collective-permute-start | bytes 393224 | tf_op jit(solution)/shard_map/ppermute | solution.py:157
  152.8 2.2 %fusion.1 = bf16[1,1024,768]{2,1,0:T(8,128)(2,1)} fusion(bf16[1024,768]{1,0:T(8,128)(2,1)S(1)} %collective-permute-done.30, bf16[512,768]{1,0:T(8,128)(2,1)S(1)} %copy-done.16, bf16[512,2048]{1,0:T(8,128)(2,1)S(1)} %copy-done.14, s32[]{:T(128)S(6)} %select_n.54), kind=kOutput, calls=%fused_computation.7 | convolution fusion | flops 807665664 | bytes 4980740 | tf_op jit(solution)/shard_map/dot_general | solution.py:20
  155.0 2.2 %fusion = bf16[1,384,2048]{2,1,0:T(8,128)(2,1)} fusion(bf16[384,2048]{1,0:T(8,128)(2,1)S(1)} %collective-permute-done.32, bf16[512,2048]{1,0:T(8,128)(2,1)S(1)} %copy-done.13, bf16[512,768]{1,0:T(8,128)(2,1)S(1)} %copy-done.17, s32[]{:T(128)S(6)} %select_n.56), kind=kOutput, calls=%fused_computation.4 | convolution fusion | flops 807665664 | bytes 5636100 | tf_op jit(solution)/shard_map/dot_general | solution.py:20
  157.2 2.2 %fusion.2 = bf16[1,1024,768]{2,1,0:T(8,128)(2,1)} fusion(bf16[1024,768]{1,0:T(8,128)(2,1)S(1)} %collective-permute-done.31, bf16[512,768]{1,0:T(8,128)(2,1)S(1)} %copy-done.15, bf16[512,2048]{1,0:T(8,128)(2,1)S(1)} %copy-done.14, s32[]{:T(128)S(6)} %select_n.54), kind=kOutput, calls=%fused_computation.8 | convolution fusion | flops 807665664 | bytes 4980740 | tf_op jit(solution)/shard_map/dot_general | solution.py:20
  (107 shorter events, 43.5 us)
Async XLA Ops:
  2.5 12.3 %collective-permute-start = (bf16[64,2048]{1,0:T(8,128)(2,1)S(1)}, bf16[64,2048]{1,0:T(8,128)(2,1)S(1)}, u32[]{:S(2)}, u32[]{:S(2)}) collective-permute-start(bf16[64,2048]{1,0:T(8,128)(2,1)S(1)} %constant_dynamic-update-slice_fusion.refs_3_), channel_id=1, source_target_pairs={{0,8},{8,16},{16,24},{24,0},{1,9},{9,17},{17,25},{25,1},{2,10},{10... | collective-permute-start | bytes 786440 | tf_op jit(solution)/shard_map/ppermute | solution.py:157
  5.6 13.6 %collective-permute-start.2 = (bf16[64,2048]{1,0:T(8,128)(2,1)S(1)}, bf16[64,2048]{1,0:T(8,128)(2,1)S(1)}, u32[]{:S(2)}, u32[]{:S(2)}) collective-permute-start(bf16[64,2048]{1,0:T(8,128)(2,1)S(1)} %constant_dynamic-update-slice_fusion.refs_3_), channel_id=1, source_target_pairs={{0,24},{8,0},{16,8},{24,16},{1,25},{9,1},{17,9},{25,17},{2,26},{10... | collective-permute-start | bytes 786440 | tf_op jit(solution)/shard_map/ppermute | solution.py:157
  7.6 11.5 %collective-permute-start.6 = (bf16[64,2048]{1,0:T(8,128)(2,1)S(1)}, bf16[64,2048]{1,0:T(8,128)(2,1)}, u32[]{:S(2)}, u32[]{:S(2)}) collective-permute-start(bf16[64,2048]{1,0:T(8,128)(2,1)S(1)} %constant_dynamic-update-slice_fusion.refs_3_), channel_id=1, source_target_pairs={{0,2},{1,5},{2,0},{3,7},{4,6},{5,1},{6,4},{7,3},{8,10},{9,13},{10,... | collective-permute-start | bytes 786440 | tf_op jit(solution)/shard_map/ppermute | solution.py:165
  9.3 10.4 %collective-permute-start.10 = (bf16[64,2048]{1,0:T(8,128)(2,1)S(1)}, bf16[64,2048]{1,0:T(8,128)(2,1)S(1)}, u32[]{:S(2)}, u32[]{:S(2)}) collective-permute-start(bf16[64,2048]{1,0:T(8,128)(2,1)S(1)} %constant_dynamic-update-slice_fusion.refs_3_), channel_id=1, source_target_pairs={{0,4},{1,3},{2,6},{3,1},{4,0},{5,7},{6,2},{7,5},{8,12},{9,11},{10,... | collective-permute-start | bytes 786440 | tf_op jit(solution)/shard_map/ppermute | solution.py:165
  14.8 10.5 %collective-permute-start.1 = (bf16[64,2048]{1,0:T(8,128)(2,1)S(1)}, bf16[64,2048]{1,0:T(8,128)(2,1)}, u32[]{:S(2)}, u32[]{:S(2)}) collective-permute-start(bf16[64,2048]{1,0:T(8,128)(2,1)S(1)} %collective-permute-done.refs_0_), channel_id=1, source_target_pairs={{0,8},{8,16},{16,24},{24,0},{1,9},{9,17},{17,25},{25,1},{2,10},{10... | collective-permute-start | bytes 786440 | tf_op jit(solution)/shard_map/ppermute | solution.py:157
  14.8 50.2 %collective-permute-start.15 = (bf16[1024,768]{1,0:T(8,128)(2,1)}, bf16[1024,768]{1,0:T(8,128)(2,1)S(1)}, u32[]{:S(2)}, u32[]{:S(2)}) collective-permute-start(bf16[1024,768]{1,0:T(8,128)(2,1)} %bitcast.48), channel_id=1, source_target_pairs={{0,1},{1,0},{2,3},{3,2},{4,5},{5,4},{6,7},{7,6},{8,9},{9,8},{10,11... | collective-permute-start | bytes 4718600 | tf_op jit(solution)/shard_map/ppermute | solution.py:16
  19.2 45.8 %collective-permute-start.16 = (bf16[1024,768]{1,0:T(8,128)(2,1)}, bf16[1024,768]{1,0:T(8,128)(2,1)S(1)}, u32[]{:S(2)}, u32[]{:S(2)}) collective-permute-start(bf16[1024,768]{1,0:T(8,128)(2,1)} %bitcast.51), channel_id=1, source_target_pairs={{0,1},{1,0},{2,3},{3,2},{4,5},{5,4},{6,7},{7,6},{8,9},{9,8},{10,11... | collective-permute-start | bytes 4718600 | tf_op jit(solution)/shard_map/ppermute | solution.py:16
  19.2 45.8 %collective-permute-start.17 = (bf16[384,2048]{1,0:T(8,128)(2,1)}, bf16[384,2048]{1,0:T(8,128)(2,1)}, u32[]{:S(2)}, u32[]{:S(2)}) collective-permute-start(bf16[384,2048]{1,0:T(8,128)(2,1)} %bitcast.54), channel_id=1, source_target_pairs={{0,1},{1,0},{2,3},{3,2},{4,5},{5,4},{6,7},{7,6},{8,9},{9,8},{10,11... | collective-permute-start | bytes 4718600 | tf_op jit(solution)/shard_map/ppermute | solution.py:16
  25.3 9.2 %collective-permute-start.5 = (bf16[64,2048]{1,0:T(8,128)(2,1)S(1)}, bf16[64,2048]{1,0:T(8,128)(2,1)S(1)}, u32[]{:S(2)}, u32[]{:S(2)}) collective-permute-start(bf16[64,2048]{1,0:T(8,128)(2,1)S(1)} %collective-permute-done.2.refs_2_), channel_id=1, source_target_pairs={{0,2},{1,5},{2,0},{3,7},{4,6},{5,1},{6,4},{7,3},{8,10},{9,13},{10,... | collective-permute-start | bytes 786440 | tf_op jit(solution)/shard_map/ppermute | solution.py:165
  26.8 9.2 %collective-permute-start.7 = (bf16[64,2048]{1,0:T(8,128)(2,1)S(1)}, bf16[64,2048]{1,0:T(8,128)(2,1)S(1)}, u32[]{:S(2)}, u32[]{:S(2)}) collective-permute-start(bf16[64,2048]{1,0:T(8,128)(2,1)S(1)} %collective-permute-done.refs_0_), channel_id=1, source_target_pairs={{0,4},{1,3},{2,6},{3,1},{4,0},{5,7},{6,2},{7,5},{8,12},{9,11},{10,... | collective-permute-start | bytes 786440 | tf_op jit(solution)/shard_map/ppermute | solution.py:165
  35.9 12.7 %collective-permute-start.14 = (bf16[64,2048]{1,0:T(8,128)(2,1)}, bf16[64,2048]{1,0:T(8,128)(2,1)}, u32[]{:S(2)}, u32[]{:S(2)}) collective-permute-start(bf16[64,2048]{1,0:T(8,128)(2,1)} %collective-permute-done.6.refs_7_), channel_id=1, source_target_pairs={{0,4},{1,3},{2,6},{3,1},{4,0},{5,7},{6,2},{7,5},{8,12},{9,11},{10,... | collective-permute-start | bytes 786440 | tf_op jit(solution)/shard_map/ppermute | solution.py:165
  45.1 15.0 %all-to-all-start = ((f32[16,1,32]{2,1,0:T(1,128)}), f32[16,1,32]{2,1,0:T(1,128)S(1)}, u32[]{:S(2)}, u32[]{:S(2)}) async-start(f32[16,1,32]{2,1,0:T(1,128)} %bitcast.5), calls=%async_computation | async-start | bytes 16384 | tf_op jit(solution)/shard_map/all_to_all | solution.py:210
  97.2 9.9 %collective-permute-start.25 = (bf16[128,2048]{1,0:T(8,128)(2,1)}, bf16[128,2048]{1,0:T(8,128)(2,1)S(1)}, u32[]{:S(2)}, u32[]{:S(2)}) collective-permute-start(bf16[128,2048]{1,0:T(8,128)(2,1)} %get-tuple-element.23), channel_id=1, source_target_pairs={{0,4},{1,3},{2,6},{3,1},{4,0},{5,7},{6,2},{7,5},{8,12},{9,11},{10,... | collective-permute-start | bytes 1572872 | tf_op jit(solution)/shard_map/ppermute | solution.py:165
  99.0 38.7 %collective-permute-start.18 = (bf16[256,2048]{1,0:T(8,128)(2,1)S(1)}, bf16[256,2048]{1,0:T(8,128)(2,1)S(1)}, u32[]{:S(2)}, u32[]{:S(2)}) collective-permute-start(bf16[256,2048]{1,0:T(8,128)(2,1)S(1)} %copy-done.5), channel_id=1, source_target_pairs={{0,4},{1,3},{2,6},{3,1},{4,0},{5,7},{6,2},{7,5},{8,12},{9,11},{10,... | collective-permute-start | bytes 3145736 | tf_op jit(solution)/shard_map/ppermute | solution.py:165
  99.3 29.0 %collective-permute-start.23 = (bf16[128,2048]{1,0:T(8,128)(2,1)}, bf16[128,2048]{1,0:T(8,128)(2,1)S(1)}, u32[]{:S(2)}, u32[]{:S(2)}) collective-permute-start(bf16[128,2048]{1,0:T(8,128)(2,1)} %get-tuple-element.22), channel_id=1, source_target_pairs={{0,4},{1,3},{2,6},{3,1},{4,0},{5,7},{6,2},{7,5},{8,12},{9,11},{10,... | collective-permute-start | bytes 1572872 | tf_op jit(solution)/shard_map/ppermute | solution.py:165
  103.7 46.3 %collective-permute-start.30 = (bf16[1024,768]{1,0:T(8,128)(2,1)S(1)}, bf16[1024,768]{1,0:T(8,128)(2,1)S(1)}, u32[]{:S(2)}, u32[]{:S(2)}) collective-permute-start(bf16[1024,768]{1,0:T(8,128)(2,1)S(1)} %convolution_convert_fusion.2), channel_id=1, source_target_pairs={{0,1},{1,0},{2,3},{3,2},{4,5},{5,4},{6,7},{7,6},{8,9},{9,8},{10,11... | collective-permute-start | bytes 4718600 | tf_op jit(solution)/shard_map/ppermute | solution.py:16
  107.2 21.1 %collective-permute-start.26 = (bf16[64,2048]{1,0:T(8,128)(2,1)S(1)}, bf16[64,2048]{1,0:T(8,128)(2,1)S(1)}, u32[]{:S(2)}, u32[]{:S(2)}) collective-permute-start(bf16[64,2048]{1,0:T(8,128)(2,1)S(1)} %fusion.7), channel_id=1, source_target_pairs={{0,2},{1,5},{2,0},{3,7},{4,6},{5,1},{6,4},{7,3},{8,10},{9,13},{10,... | collective-permute-start | bytes 786440 | tf_op jit(solution)/shard_map/ppermute | solution.py:165
  130.9 9.6 %collective-permute-start.28 = (bf16[32,2048]{1,0:T(8,128)(2,1)S(1)}, bf16[32,2048]{1,0:T(8,128)(2,1)S(1)}, u32[]{:S(2)}, u32[]{:S(2)}) collective-permute-start(bf16[32,2048]{1,0:T(8,128)(2,1)S(1)} %get-tuple-element.35), channel_id=1, source_target_pairs={{0,16},{8,24},{16,0},{24,8},{1,17},{9,25},{17,1},{25,9},{2,18},{10... | collective-permute-start | bytes 393224 | tf_op jit(solution)/shard_map/ppermute | solution.py:157
  137.9 9.2 %collective-permute-start.19 = (bf16[128,2048]{1,0:T(8,128)(2,1)S(1)}, bf16[128,2048]{1,0:T(8,128)(2,1)S(1)}, u32[]{:S(2)}, u32[]{:S(2)}) collective-permute-start(bf16[128,2048]{1,0:T(8,128)(2,1)S(1)} %add_convert_fusion.4), channel_id=1, source_target_pairs={{0,2},{1,5},{2,0},{3,7},{4,6},{5,1},{6,4},{7,3},{8,10},{9,13},{10,... | collective-permute-start | bytes 1572872 | tf_op jit(solution)/shard_map/ppermute | solution.py:165
  140.5 16.7 %collective-permute-start.31 = (bf16[1024,768]{1,0:T(8,128)(2,1)S(1)}, bf16[1024,768]{1,0:T(8,128)(2,1)S(1)}, u32[]{:S(2)}, u32[]{:S(2)}) collective-permute-start(bf16[1024,768]{1,0:T(8,128)(2,1)S(1)} %convolution_convert_fusion.1), channel_id=1, source_target_pairs={{0,1},{1,0},{2,3},{3,2},{4,5},{5,4},{6,7},{7,6},{8,9},{9,8},{10,11... | collective-permute-start | bytes 4718600 | tf_op jit(solution)/shard_map/ppermute | solution.py:16
  140.5 14.5 %collective-permute-start.32 = (bf16[384,2048]{1,0:T(8,128)(2,1)S(1)}, bf16[384,2048]{1,0:T(8,128)(2,1)S(1)}, u32[]{:S(2)}, u32[]{:S(2)}) collective-permute-start(bf16[384,2048]{1,0:T(8,128)(2,1)S(1)} %convolution_convert_fusion), channel_id=1, source_target_pairs={{0,1},{1,0},{2,3},{3,2},{4,5},{5,4},{6,7},{7,6},{8,9},{9,8},{10,11... | collective-permute-start | bytes 4718600 | tf_op jit(solution)/shard_map/ppermute | solution.py:16
  147.4 12.0 %collective-permute-start.22 = (bf16[32,2048]{1,0:T(8,128)(2,1)S(1)}, bf16[32,2048]{1,0:T(8,128)(2,1)S(1)}, u32[]{:S(2)}, u32[]{:S(2)}) collective-permute-start(bf16[32,2048]{1,0:T(8,128)(2,1)S(1)} %get-tuple-element.32), channel_id=1, source_target_pairs={{0,8},{8,16},{16,24},{24,0},{1,9},{9,17},{17,25},{25,1},{2,10},{10... | collective-permute-start | bytes 393224 | tf_op jit(solution)/shard_map/ppermute | solution.py:157
  148.9 10.4 %collective-permute-start.21 = (bf16[32,2048]{1,0:T(8,128)(2,1)S(1)}, bf16[32,2048]{1,0:T(8,128)(2,1)S(1)}, u32[]{:S(2)}, u32[]{:S(2)}) collective-permute-start(bf16[32,2048]{1,0:T(8,128)(2,1)S(1)} %get-tuple-element.33), channel_id=1, source_target_pairs={{0,16},{8,24},{16,0},{24,8},{1,17},{9,25},{17,1},{25,9},{2,18},{10... | collective-permute-start | bytes 393224 | tf_op jit(solution)/shard_map/ppermute | solution.py:157
  149.9 9.4 %collective-permute-start.20 = (bf16[32,2048]{1,0:T(8,128)(2,1)S(1)}, bf16[32,2048]{1,0:T(8,128)(2,1)S(1)}, u32[]{:S(2)}, u32[]{:S(2)}) collective-permute-start(bf16[32,2048]{1,0:T(8,128)(2,1)S(1)} %get-tuple-element.31), channel_id=1, source_target_pairs={{0,24},{8,0},{16,8},{24,16},{1,25},{9,1},{17,9},{25,17},{2,26},{10... | collective-permute-start | bytes 393224 | tf_op jit(solution)/shard_map/ppermute | solution.py:157
  (28 other events, 317.1 us)

commit v3 on v0

--- a/solution.py
+++ b/solution.py
@@ -1,6 +1,10 @@
+import functools
+
 import jax
 import jax.numpy as jnp
 from jax import lax
+from jax.experimental import pallas as pl
+from jax.experimental.pallas import tpu as pltpu
 from jax.sharding import PartitionSpec as P
 
 TOP = 8
@@ -30,7 +34,7 @@
     return left_part.astype(jnp.float32) + right_part.astype(jnp.float32)
 
 
-def local(tokens, cotangent, expert_ids, gate_probs, gate_weight, up_weight, down_weight):
+def routed_local(tokens, cotangent, expert_ids, gate_probs, gate_weight, up_weight, down_weight):
     group_count = lax.axis_size("grp")
     inner_count = lax.axis_size("exp")
     expert_count = group_count * inner_count
@@ -141,6 +145,324 @@
     )
 
 
+FIRST, SECOND = (1, 2), (2, 1)
+tie = lax.optimization_barrier
+VMEM_LIMIT = 56 * 2**20
+ANY = pl.BlockSpec(memory_space=pl.ANY)
+SMEM = pl.BlockSpec(memory_space=pltpu.SMEM)
+
+
+def swap_group(value, mask):
+    count = lax.axis_size("grp")
+    return lax.ppermute(value, "grp", [(i, i ^ mask) for i in range(count)])
+
+
+def swap_inner(value, masks):
+    inner, reps = lax.axis_size("exp"), lax.axis_size("rep")
+    pairs = [
+        (e * reps + r, (e ^ masks[r]) * reps + r) for e in range(inner) for r in range(reps)
+    ]
+    return lax.ppermute(value, ("exp", "rep"), pairs)
+
+
+def steps_of(count):
+    steps = [0]
+    while len(steps) < count:
+        steps = [2 * step for step in steps] + [2 * step + 1 for step in steps]
+    return steps
+
+
+def gather_blocks(block, beside):
+    count = lax.axis_size("grp")
+    beside, waiting = list(beside), list(range(len(beside)))
+    moved, first, second, both = {0: block}, {}, {}, {}
+    mask = 1
+    while mask < count:
+        moved[mask] = swap_group(block, mask)
+        mask *= 2
+    for k in range(count + 1):
+        due = [
+            (part, step)
+            for part, step in ((moved, k), (first, k - 1), (second, k - 2), (both, k - 3))
+            if k > 0 and step in part
+        ]
+        if k > 1 and waiting:
+            due.append((beside, waiting.pop(0)))
+        if due:
+            for (part, step), value in zip(due, tie([part[step] for part, step in due])):
+                part[step] = value
+        if k < count:
+            mask = 1
+            while mask < (k & -k):
+                moved[k | mask] = swap_group(moved[k], mask)
+                mask *= 2
+            first[k] = swap_inner(moved[k], FIRST)
+            second[k] = swap_inner(moved[k], SECOND)
+        if k > 0:
+            both[k - 1] = swap_inner(first[k - 1], SECOND)
+    pieces = [part[step] for part in (moved, first, second, both) for step in steps_of(count)]
+    return pieces, beside
+
+
+def add_bf16(left, right):
+    return (left.astype(jnp.float32) + right.astype(jnp.float32)).astype(jnp.bfloat16)
+
+
+def reduce_part(here, came):
+    came = came.reshape(here.shape)
+    passed = swap_inner(add_bf16(here[1], came[1]), FIRST)
+    return add_bf16(here[0].astype(jnp.float32) + came[0].astype(jnp.float32), passed)
+
+
+def reduce_column(column, beside=()):
+    count = lax.axis_size("grp")
+    rows = column.shape[0] // count
+    came = [
+        swap_group(column[q * rows : (q + 1) * rows], step)
+        for q, step in enumerate(steps_of(count))
+        if step
+    ]
+    came[0], *beside = tie((came[0], *beside)) if beside else came[:1]
+    total = column[:rows].astype(jnp.float32)
+    for value in came:
+        total = total + value.astype(jnp.float32)
+    return total.astype(jnp.bfloat16), beside
+
+
+def token_block(tokens, cotangent, expert_ids, gate_probs, expert_count):
+    named = expert_ids[:, :, None] == jnp.arange(expert_count, dtype=jnp.int32)
+    rest = jnp.sum(jnp.where(named, gate_probs[:, :, None], 0.0), axis=1)
+    terms = []
+    for _ in range(3):
+        terms.append(lax.reduce_precision(rest, exponent_bits=8, mantissa_bits=7))
+        rest = rest - terms[-1]
+    terms = jnp.concatenate(terms, axis=1).astype(jnp.bfloat16)
+    rows, side = tokens.shape[0], side_width(expert_count)
+    terms = jnp.pad(terms, ((0, rows), (0, side - terms.shape[1])))
+    return jnp.concatenate([jnp.concatenate([tokens, cotangent], axis=0), terms], axis=1)
+
+
+def side_width(expert_count):
+    return -(-3 * expert_count // 128) * 128
+
+
+def start_halves(halves, whole, sems, first_sem, replica):
+    own, partner = halves
+    size = own.shape[0]
+    copies = []
+    for k, (half, which) in enumerate(((own, replica), (partner, 1 - replica))):
+        place = pl.ds(pl.multiple_of(which * size, size), size)
+        copies.append(pltpu.make_async_copy(half, whole.at[place, :], sems.at[first_sem + k]))
+        copies[-1].start()
+    return copies
+
+
+def start_rows(pieces, whole, offset, rows, first_col, sems):
+    copies = []
+    for k, piece in enumerate(pieces):
+        part = piece.at[pl.ds(offset, rows), pl.ds(first_col, whole.shape[1])]
+        copies.append(pltpu.make_async_copy(part, whole.at[pl.ds(k * rows, rows), :], sems.at[k]))
+        copies[-1].start()
+    return copies
+
+
+def start_out(sources_and_places, sems, first_sem):
+    copies = []
+    for k, (source, place) in enumerate(sources_and_places):
+        copies.append(pltpu.make_async_copy(source, place, sems.at[first_sem + k]))
+        copies[-1].start()
+    return copies
+
+
+def wait_all(copies):
+    for copy in copies:
+        copy.wait()
+
+
+def weights_of(side_ref, expert, expert_count):
+    lane = lax.broadcasted_iota(jnp.int32, side_ref.shape, 1)
+    mine = (lane == expert) | (lane == expert + expert_count) | (lane == expert + 2 * expert_count)
+    return jnp.sum(jnp.where(mine, side_ref[...].astype(jnp.float32), 0.0), axis=1, keepdims=True)
+
+
+def halves_of(whole, cols, keep, send):
+    half = keep.shape[0]
+    return [
+        (whole.at[pl.ds(0, half), cols], keep.at[:, cols]),
+        (whole.at[pl.ds(half, half), cols], send.at[:, cols]),
+    ]
+
+
+def tiles(size, count):
+    return [pl.ds(i * size // count, size // count) for i in range(count)]
+
+
+def forward_kernel(rows, count, where_ref, *refs):
+    pieces, refs = refs[:count], refs[count:]
+    gate, up, down = refs[0:2], refs[2:4], refs[4:6]
+    keep, send, gate_pre_out, up_pre_out, hidden_out, rows_out = refs[6:12]
+    rows_in, side, gate_all, up_all, down_all, gate_pre, up_pre, hidden, out = refs[12:21]
+    row_sems, side_sems, weight_sems, out_sems = refs[21:]
+    width = rows_in.shape[1]
+    row_copies = start_rows(pieces, rows_in, 0, rows, 0, row_sems)
+    gate_copies = start_halves(gate, gate_all, weight_sems, 0, where_ref[0])
+    up_copies = start_halves(up, up_all, weight_sems, 2, where_ref[0])
+    side_copies = start_rows(pieces, side, 0, rows, width, side_sems)
+    down_copies = start_halves(down, down_all, weight_sems, 4, where_ref[0])
+    wait_all(row_copies)
+    outs = start_out([(rows_in, rows_out)], out_sems, 0)
+    wait_all(gate_copies)
+    gate_pre[...] = jnp.dot(rows_in[...], gate_all[...], preferred_element_type=jnp.float32)
+    outs += start_out([(gate_pre, gate_pre_out)], out_sems, 1)
+    wait_all(up_copies)
+    up_pre[...] = jnp.dot(rows_in[...], up_all[...], preferred_element_type=jnp.float32)
+    outs += start_out([(up_pre, up_pre_out)], out_sems, 2)
+    act = gate_pre[...] * jax.nn.sigmoid(gate_pre[...])
+    hidden[...] = (act * up_pre[...]).astype(jnp.bfloat16)
+    outs += start_out([(hidden, hidden_out)], out_sems, 3)
+    wait_all(side_copies)
+    probs = weights_of(side, where_ref[1], count)
+    wait_all(down_copies)
+    for t, cols in enumerate(tiles(width, 2)):
+        part = jnp.dot(hidden[...], down_all[:, cols], preferred_element_type=jnp.float32)
+        out[:, cols] = (part * probs).astype(jnp.bfloat16)
+        outs += start_out(halves_of(out, cols, keep, send), out_sems, 4 + 2 * t)
+    wait_all(outs)
+
+
+def backward_kernel(rows, count, where_ref, gate_pre_in, up_pre_in, *refs):
+    pieces, refs = refs[:count], refs[count:]
+    gate, up, down = refs[0:2], refs[2:4], refs[4:6]
+    keep, send, dgate_out, dup_out, scaled_out = refs[6:11]
+    scaled, side, gate_all, up_all, down_all, gate_pre, up_pre, dgate, dup, grad = refs[11:21]
+    row_sems, side_sems, weight_sems, pre_sems, out_sems = refs[21:]
+    width = scaled.shape[1]
+    row_copies = start_rows(pieces, scaled, rows, rows, 0, row_sems)
+    side_copies = start_rows(pieces, side, 0, rows, width, side_sems)
+    down_copies = start_halves(down, down_all, weight_sems, 4, where_ref[0])
+    pre_copies = start_out([(gate_pre_in, gate_pre), (up_pre_in, up_pre)], pre_sems, 0)
+    gate_copies = start_halves(gate, gate_all, weight_sems, 0, where_ref[0])
+    up_copies = start_halves(up, up_all, weight_sems, 2, where_ref[0])
+    wait_all(row_copies + side_copies)
+    probs = weights_of(side, where_ref[1], count)
+    scaled[...] = (scaled[...].astype(jnp.float32) * probs).astype(jnp.bfloat16)
+    outs = start_out([(scaled, scaled_out)], out_sems, 0)
+    wait_all(down_copies)
+    dhidden = contract_cols(scaled[...], down_all[...])
+    wait_all(pre_copies)
+    sigma = jax.nn.sigmoid(gate_pre[...])
+    dgate[...] = (
+        dhidden * up_pre[...] * sigma * (1.0 + gate_pre[...] * (1.0 - sigma))
+    ).astype(jnp.bfloat16)
+    dup[...] = (dhidden * (gate_pre[...] * sigma)).astype(jnp.bfloat16)
+    outs += start_out([(dgate, dgate_out), (dup, dup_out)], out_sems, 1)
+    wait_all(gate_copies + up_copies)
+    for t, cols in enumerate(tiles(width, 2)):
+        part = contract_cols(dgate[...], gate_all[cols, :])
+        grad[:, cols] = (part + contract_cols(dup[...], up_all[cols, :])).astype(jnp.bfloat16)
+        outs += start_out(halves_of(grad, cols, keep, send), out_sems, 3 + 2 * t)
+    wait_all(outs)
+
+
+def expert_call(kernel, outs, scratch, sems, flops, inputs):
+    return pl.pallas_call(
+        kernel,
+        out_shape=[jax.ShapeDtypeStruct(shape, dtype) for shape, dtype in outs],
+        in_specs=[SMEM] + [ANY] * (len(inputs) - 1),
+        out_specs=[ANY] * len(outs),
+        scratch_shapes=[pltpu.VMEM(shape, dtype) for shape, dtype in scratch]
+        + [pltpu.SemaphoreType.DMA((n,)) for n in sems],
+        compiler_params=pltpu.CompilerParams(vmem_limit_bytes=VMEM_LIMIT),
+        cost_estimate=pl.CostEstimate(
+            flops=flops,
+            bytes_accessed=sum(2 * value.size for value in inputs),
+            transcendentals=0,
+        ),
+    )(*inputs)
+
+
+def partner_in_turn(values):
+    came, values = [], list(values)
+    for k in range(len(values)):
+        came.append(partner_2(values[k], "rep", 0))
+        if k + 1 < len(values):
+            came[k], values[k + 1] = tie((came[k], values[k + 1]))
+    return came
+
+
+def dense_local(tokens, cotangent, expert_ids, gate_probs, gate_weight, up_weight, down_weight):
+    expert_count = lax.axis_size("grp") * lax.axis_size("exp")
+    replica = lax.axis_index("rep")
+    rows, width = tokens.shape
+    half_width, hidden_width = gate_weight.shape[1:]
+    half_hidden = down_weight.shape[1]
+    total = expert_count * rows
+    own = (gate_weight[0], up_weight[0], down_weight[0])
+    partner = partner_in_turn(own)
+    block = token_block(tokens, cotangent, expert_ids, gate_probs, expert_count)
+    pieces, partner = gather_blocks(block, partner)
+    weights = [value for pair in zip(own, partner) for value in pair]
+    expert = lax.axis_index("grp") * lax.axis_size("exp") + lax.axis_index("exp")
+    where = jnp.stack([replica, expert]).astype(jnp.int32)
+    bf16, f32 = jnp.bfloat16, jnp.float32
+    wide, narrow, pre = ((total, width), bf16), ((total, hidden_width), bf16), ((total, hidden_width), f32)
+    half_wide = ((total // 2, width), bf16)
+    held = [
+        wide,
+        ((total, side_width(expert_count)), bf16),
+        ((width, hidden_width), bf16),
+        ((width, hidden_width), bf16),
+        ((hidden_width, width), bf16),
+        pre,
+        pre,
+    ]
+    flops = 6 * total * width * hidden_width
+    out_keep, out_send, gate_pre, up_pre, hidden, rows_in = expert_call(
+        functools.partial(forward_kernel, rows, expert_count),
+        [half_wide, half_wide, pre, pre, narrow, wide],
+        held + [narrow, wide],
+        [expert_count, expert_count, 6, 8],
+        flops,
+        [where, *pieces, *weights],
+    )
+    out_came = swap_inner(out_send, SECOND)
+    grad_keep, grad_send, dgate, dup, rows_scaled = expert_call(
+        functools.partial(backward_kernel, rows, expert_count),
+        [half_wide, half_wide, narrow, narrow, wide],
+        held + [narrow, narrow, wide],
+        [expert_count, expert_count, 6, 2, 7],
+        flops,
+        [where, gate_pre, up_pre, *pieces, *weights],
+    )
+    out_came, grad_keep, grad_send, dgate, dup, rows_scaled = tie(
+        (out_came, grad_keep, grad_send, dgate, dup, rows_scaled)
+    )
+    grad_came = swap_inner(grad_send, SECOND)
+    out_column = reduce_part(out_keep.reshape(2, -1, width), out_came)
+    grad_came, out_column, dgate, dup, rows_scaled, hidden, rows_in = tie(
+        (grad_came, out_column, dgate, dup, rows_scaled, hidden, rows_in)
+    )
+
+    def half(value, which, size):
+        return lax.dynamic_slice_in_dim(value, which * size, size, 1)
+
+    other = 1 - replica
+    sent = (
+        contract_rows(half(rows_in, other, half_width), dgate).astype(bf16),
+        contract_rows(half(rows_in, other, half_width), dup).astype(bf16),
+        contract_rows(half(hidden, other, half_hidden), rows_scaled).astype(bf16),
+    )
+    back = partner_2(sent, "rep", 0)
+    gate_out = add_bf16(contract_rows(half(rows_in, replica, half_width), dgate), back[0])
+    up_out = add_bf16(contract_rows(half(rows_in, replica, half_width), dup), back[1])
+    down_out = add_bf16(contract_rows(half(hidden, replica, half_hidden), rows_scaled), back[2])
+    layer_out, _ = reduce_column(out_column)
+    token_grad, (gate_out, up_out, down_out) = reduce_column(
+        reduce_part(grad_keep.reshape(2, -1, width), grad_came), (gate_out, up_out, down_out)
+    )
+    return layer_out, token_grad, gate_out[None], up_out[None], down_out[None]
+
+
 def solution(mesh):
     in_specs = (
         P(("grp", "exp", "rep"), None),
@@ -158,4 +480,8 @@
         P(("grp", "exp"), "rep", None),
         P(("grp", "exp"), "rep", None),
     )
+    sizes = dict(mesh.shape)
+    group_bits = sizes["grp"] & (sizes["grp"] - 1) == 0
+    whole_blocks = sizes["exp"] == 4 and sizes["rep"] == 2 and group_bits and sizes["grp"] * sizes["exp"] <= 2 * TOP
+    local = dense_local if whole_blocks else routed_local
     return jax.shard_map(local, mesh=mesh, in_specs=in_specs, out_specs=out_specs, check_vma=False)

time: 200 us -> 140 us (0.70); the launches traced: 197 us -> 140 us
  waiting for transfers between devices: 98.4 us -> 46.5 us
  matrix products: 44.9 us -> 11 us
  Pallas kernels: 0 us -> 25.8 us
  starting transfers between devices: 31.9 us -> 48.6 us
  between operations: 14 us -> 0.84 us
  local copies, waits for them, and re-layouts: 2.79 us -> 0.27 us
    all_to_all x4 -> x0, waiting for transfers between devices: 96.3 us -> none  [the longest x1 31.5 us: local(): lax.all_to_all(send_scaled.reshape(expert_count, capacity, model_width),...]
    ppermute x0 -> x25, starting transfers between devices: none -> 46.7 us  [the longest x16 30.8 us: swap_inner(): return lax.ppermute(value, ('exp', 'rep'), pairs)]
    ppermute x0 -> x25, waiting for transfers between devices: none -> 41 us  [the longest x16 25.9 us: swap_inner(): return lax.ppermute(value, ('exp', 'rep'), pairs)]
    all_to_all x4 -> x0, starting transfers between devices: 30.6 us -> none  [the longest x1 8.36 us: local(): lax.all_to_all(send_scaled.reshape(expert_count, capacity, model_width),...]
    dot_general x12 -> x0, matrix products: 30 us -> none  [the longest x3 11.2 us: contract_cols(): lax.dot_general(left, right, (((1,), (1,)), ((), ())), preferred_element_...]
    pallas_call x0 -> x2, Pallas kernels: none -> 25.8 us  [expert_call(): pl.pallas_call(kernel, out_shape=[jax.ShapeDtypeStruct(shape, dtype) for...]
    ppermute x5 -> x6, waiting for transfers between devices: 0.01 us -> 5.53 us  [partner_2(): return lax.ppermute(value, axis, pairs)]
    dot_general x6, matrix products: 15 us -> 11 us  [contract_rows(): lax.dot_general(left, right, (((0,), (0,)), ((), ())), preferred_element_...]
  transfers between devices with their start and end apart: 12 -> 31, of which waited for: 4 -> 15; matrix products, arithmetic and copies ran while one was open for 22% -> 11% of each run, Pallas kernels for 0% -> 9%
where the time goes in v3:
time: 140 us
  starting transfers between devices  48.6 us (35%)
  waiting for transfers between devices  46.5 us (33%)
  Pallas kernels  25.8 us (18%)
  matrix products  11 us (8%)
  other arithmetic  6.83 us (5%)
    ppermute x16, starting transfers between devices, swap_inner(): return lax.ppermute(value, ('exp', 'rep'), pairs)  30.8 us
    ppermute x16, waiting for transfers between devices, swap_inner(): return lax.ppermute(value, ('exp', 'rep'), pairs)  25.9 us
    pallas_call x2, Pallas kernels, expert_call(): pl.pallas_call(kernel, out_shape=[jax.ShapeDtypeStruct(shape, dtype) for...  25.8 us
    ppermute x9, starting transfers between devices, swap_group(): return lax.ppermute(value, 'grp', [(i, i ^ mask) for i in range(count)])  16 us
    ppermute x9, waiting for transfers between devices, swap_group(): return lax.ppermute(value, 'grp', [(i, i ^ mask) for i in range(count)])  15.1 us
    dot_general x6, matrix products, contract_rows(): lax.dot_general(left, right, (((0,), (0,)), ((), ())), preferred_element_...  11 us
    ppermute x6, waiting for transfers between devices, partner_2(): return lax.ppermute(value, axis, pairs)  5.53 us
  transfers between devices with their start and end apart: 31, of which 15 were waited for; matrix products, arithmetic and copies ran while one was open for 11% of the time, Pallas kernels for 9%

profile of v3, /device:TPU:0, one launch (start us, length us, event | category | flops | bytes accessed | tf_op | source)
XLA Modules:
  0.0 139.8 jit_solution(13575145556100545570)
XLA Ops:
  1.1 3.2 %collective-permute-done.5.refs_17_ = bf16[1024,768]{1,0:T(8,128)(2,1)S(1)} collective-permute-done((bf16[1024,768]{1,0:T(8,128)(2,1)}, bf16[1024,768]{1,0:T(8,128)(2,1)S(1)}, u32[]{:S(2)}, u32[]{:S(2)}) %collective-permute-start.5) | collective-permute-done | bytes 1572896 | tf_op jit(solution)/shard_map/ppermute | solution.py:16
  5.8 2.3 %collective-permute-done.10.refs_19_ = bf16[1024,768]{1,0:T(8,128)(2,1)S(1)} collective-permute-done((bf16[1024,768]{1,0:T(8,128)(2,1)}, bf16[1024,768]{1,0:T(8,128)(2,1)S(1)}, u32[]{:S(2)}, u32[]{:S(2)}) %collective-permute-start.10) | collective-permute-done | bytes 1572896 | tf_op jit(solution)/shard_map/ppermute | solution.py:16
  9.6 3.0 %collective-permute-start.1 = (bf16[64,2176]{1,0:T(8,128)(2,1)S(1)}, bf16[64,2176]{1,0:T(8,128)(2,1)S(1)}, u32[]{:S(2)}, u32[]{:S(2)}) collective-permute-start(bf16[64,2176]{1,0:T(8,128)(2,1)S(1)} %pad_maximum_fusion.refs_0_), channel_id=1, source_target_pairs={{0,8},{8,0},{16,24},{24,16},{1,9},{9,1},{17,25},{25,17},{2,10},{10... | collective-permute-start | bytes 835592 | tf_op jit(solution)/shard_map/ppermute | solution.py:157
  14.1 2.6 %collective-permute-start = (bf16[64,2176]{1,0:T(8,128)(2,1)S(1)}, bf16[64,2176]{1,0:T(8,128)(2,1)S(1)}, u32[]{:S(2)}, u32[]{:S(2)}) collective-permute-start(bf16[64,2176]{1,0:T(8,128)(2,1)S(1)} %pad_maximum_fusion.refs_0_), channel_id=1, source_target_pairs={{0,16},{8,24},{16,0},{24,8},{1,17},{9,25},{17,1},{25,9},{2,18},{10... | collective-permute-start | bytes 835592 | tf_op jit(solution)/shard_map/ppermute | solution.py:157
  18.2 6.0 %collective-permute-done.1.refs_2_ = bf16[64,2176]{1,0:T(8,128)(2,1)S(1)} collective-permute-done((bf16[64,2176]{1,0:T(8,128)(2,1)S(1)}, bf16[64,2176]{1,0:T(8,128)(2,1)S(1)}, u32[]{:S(2)}, u32[]{:S(2)}) %collective-permute-start.1) | collective-permute-done | bytes 278560 | tf_op jit(solution)/shard_map/ppermute | solution.py:157
  25.9 2.5 %collective-permute-start.8 = (bf16[64,2176]{1,0:T(8,128)(2,1)S(1)}, bf16[64,2176]{1,0:T(8,128)(2,1)S(1)}, u32[]{:S(2)}, u32[]{:S(2)}) collective-permute-start(bf16[64,2176]{1,0:T(8,128)(2,1)S(1)} %collective-permute-done.1.refs_2_), channel_id=1, source_target_pairs={{0,4},{1,3},{2,6},{3,1},{4,0},{5,7},{6,2},{7,5},{8,12},{9,11},{10,... | collective-permute-start | bytes 835592 | tf_op jit(solution)/shard_map/ppermute | solution.py:165
  29.7 3.4 %collective-permute-done.3.refs_6_ = bf16[64,2176]{1,0:T(8,128)(2,1)S(1)} collective-permute-done((bf16[64,2176]{1,0:T(8,128)(2,1)S(1)}, bf16[64,2176]{1,0:T(8,128)(2,1)S(1)}, u32[]{:S(2)}, u32[]{:S(2)}) %collective-permute-start.3) | collective-permute-done | bytes 278560 | tf_op jit(solution)/shard_map/ppermute | solution.py:165
  34.9 3.2 %collective-permute-start.12 = (bf16[64,2176]{1,0:T(8,128)(2,1)S(1)}, bf16[64,2176]{1,0:T(8,128)(2,1)S(1)}, u32[]{:S(2)}, u32[]{:S(2)}) collective-permute-start(bf16[64,2176]{1,0:T(8,128)(2,1)S(1)} %collective-permute-done.refs_1_), channel_id=1, source_target_pairs={{0,4},{1,3},{2,6},{3,1},{4,0},{5,7},{6,2},{7,5},{8,12},{9,11},{10,... | collective-permute-start | bytes 835592 | tf_op jit(solution)/shard_map/ppermute | solution.py:165
  44.6 3.1 %collective-permute-start.15 = (bf16[64,2176]{1,0:T(8,128)(2,1)}, bf16[64,2176]{1,0:T(8,128)(2,1)}, u32[]{:S(2)}, u32[]{:S(2)}) collective-permute-start(bf16[64,2176]{1,0:T(8,128)(2,1)} %collective-permute-done.6.refs_3_), channel_id=1, source_target_pairs={{0,4},{1,3},{2,6},{3,1},{4,0},{5,7},{6,2},{7,5},{8,12},{9,11},{10,... | collective-permute-start | bytes 835592 | tf_op jit(solution)/shard_map/ppermute | solution.py:165
  48.6 4.1 %collective-permute-done.11.refs_7_ = bf16[64,2176]{1,0:T(8,128)(2,1)} collective-permute-done((bf16[64,2176]{1,0:T(8,128)(2,1)}, bf16[64,2176]{1,0:T(8,128)(2,1)}, u32[]{:S(2)}, u32[]{:S(2)}) %collective-permute-start.11) | collective-permute-done | bytes 278560 | tf_op jit(solution)/shard_map/ppermute | solution.py:165
  52.7 3.6 %collective-permute-start.17 = (bf16[64,2176]{1,0:T(8,128)(2,1)}, bf16[64,2176]{1,0:T(8,128)(2,1)}, u32[]{:S(2)}, u32[]{:S(2)}) collective-permute-start(bf16[64,2176]{1,0:T(8,128)(2,1)} %collective-permute-done.11.refs_7_), channel_id=1, source_target_pairs={{0,4},{1,3},{2,6},{3,1},{4,0},{5,7},{6,2},{7,5},{8,12},{9,11},{10,... | collective-permute-start | bytes 835592 | tf_op jit(solution)/shard_map/ppermute | solution.py:165
  56.9 4.2 %collective-permute-done.17.refs_15_ = bf16[64,2176]{1,0:T(8,128)(2,1)} collective-permute-done((bf16[64,2176]{1,0:T(8,128)(2,1)}, bf16[64,2176]{1,0:T(8,128)(2,1)}, u32[]{:S(2)}, u32[]{:S(2)}) %collective-permute-start.17) | collective-permute-done | bytes 278560 | tf_op jit(solution)/shard_map/ppermute | solution.py:165
  61.1 12.7 %shard_map.110 = (bf16[256,2048]{1,0:T(8,128)(2,1)}, bf16[256,2048]{1,0:T(8,128)(2,1)}, f32[512,768]{1,0:T(8,128)}, f32[512,768]{1,0:T(8,128)}, bf16[512,768]{1,0:T(8,128)(2,1)}, /*index=5*/bf16[512,2048]{1,0:T(8,128)(2,1)}) custom-call(s32[2]{0:T(128)} %pad_add_fusion.where_ref, bf16[64,2176]{1,0:T(8,128)(2,1)} %copy-done.2, bf16[64,2176]{1,0:T(8,128)(2,1)} %copy-done.7, ...), custom_call_target="tpu_custom_call" | custom-call | flops 4831838208 | bytes 13893636 | tf_op jit(solution)/shard_map/pallas_call | solution.py:368
  75.9 13.1 %shard_map.111 = (bf16[256,2048]{1,0:T(8,128)(2,1)}, bf16[256,2048]{1,0:T(8,128)(2,1)}, bf16[512,768]{1,0:T(8,128)(2,1)}, bf16[512,768]{1,0:T(8,128)(2,1)}, bf16[512,2048]{1,0:T(8,128)(2,1)}) custom-call(s32[2]{0:T(128)} %pad_add_fusion.where_ref, f32[512,768]{1,0:T(8,128)} %get-tuple-element.72.gate_pre_in, f32[512,768]{1,0:T(8,128)} %get-tuple-element.73.up_pre_in, ...), custom_call_target="tpu_custom_call" | custom-call | flops 4831838208 | bytes 15466500 | tf_op jit(solution)/shard_map/pallas_call | solution.py:368
  92.1 2.2 %collective-permute-start.20 = (bf16[128,2048]{1,0:T(8,128)(2,1)}, bf16[128,2048]{1,0:T(8,128)(2,1)}, u32[]{:S(2)}, u32[]{:S(2)}) collective-permute-start(bf16[128,2048]{1,0:T(8,128)(2,1)} %add_convert_fusion.6), channel_id=1, source_target_pairs={{0,2},{1,5},{2,0},{3,7},{4,6},{5,1},{6,4},{7,3},{8,10},{9,13},{10,... | collective-permute-start | bytes 1572872 | tf_op jit(solution)/shard_map/ppermute | solution.py:165
  94.3 10.4 %collective-permute-done.20 = bf16[128,2048]{1,0:T(8,128)(2,1)} collective-permute-done((bf16[128,2048]{1,0:T(8,128)(2,1)}, bf16[128,2048]{1,0:T(8,128)(2,1)}, u32[]{:S(2)}, u32[]{:S(2)}) %collective-permute-start.20) | collective-permute-done | bytes 524320 | tf_op jit(solution)/shard_map/ppermute | solution.py:165
  106.5 2.3 %convolution_convert_fusion.1 = bf16[1024,768]{1,0:T(8,128)(2,1)S(1)} fusion(bf16[512,768]{1,0:T(8,128)(2,1)} %get-tuple-element.92, bf16[512,2048]{1,0:T(8,128)(2,1)S(1)} %copy-done.15, s32[]{:T(128)S(6)} %select_n.20), kind=kOutput, calls=%fused_computation.4 | convolution fusion | flops 806092800 | bytes 3407876 | tf_op jit(solution)/shard_map/dot_general | solution.py:20
  110.1 4.2 %collective-permute-start.21 = (bf16[32,2048]{1,0:T(8,128)(2,1)S(1)}, bf16[32,2048]{1,0:T(8,128)(2,1)S(1)}, u32[]{:S(2)}, u32[]{:S(2)}) collective-permute-start(bf16[32,2048]{1,0:T(8,128)(2,1)S(1)} %get-tuple-element.102), channel_id=1, source_target_pairs={{0,16},{8,24},{16,0},{24,8},{1,17},{9,25},{17,1},{25,9},{2,18},{10... | collective-permute-start | bytes 393224 | tf_op jit(solution)/shard_map/ppermute | solution.py:157
  117.9 3.9 %collective-permute-done.21 = bf16[32,2048]{1,0:T(8,128)(2,1)S(1)} collective-permute-done((bf16[32,2048]{1,0:T(8,128)(2,1)S(1)}, bf16[32,2048]{1,0:T(8,128)(2,1)S(1)}, u32[]{:S(2)}, u32[]{:S(2)}) %collective-permute-start.21) | collective-permute-done | bytes 131104 | tf_op jit(solution)/shard_map/ppermute | solution.py:157
  122.3 2.5 %collective-permute-done.23 = bf16[32,2048]{1,0:T(8,128)(2,1)S(1)} collective-permute-done((bf16[32,2048]{1,0:T(8,128)(2,1)S(1)}, bf16[32,2048]{1,0:T(8,128)(2,1)S(1)}, u32[]{:S(2)}, u32[]{:S(2)}) %collective-permute-start.23) | collective-permute-done | bytes 131104 | tf_op jit(solution)/shard_map/ppermute | solution.py:157
  125.8 2.2 %collective-permute-start.25 = (bf16[32,2048]{1,0:T(8,128)(2,1)S(1)}, bf16[32,2048]{1,0:T(8,128)(2,1)S(1)}, u32[]{:S(2)}, u32[]{:S(2)}) collective-permute-start(bf16[32,2048]{1,0:T(8,128)(2,1)S(1)} %get-tuple-element.99), channel_id=1, source_target_pairs={{0,16},{8,24},{16,0},{24,8},{1,17},{9,25},{17,1},{25,9},{2,18},{10... | collective-permute-start | bytes 393224 | tf_op jit(solution)/shard_map/ppermute | solution.py:157
  130.5 2.2 %add_convert_fusion.1 = bf16[1024,768]{1,0:T(8,128)(2,1)} fusion(bf16[1024,768]{1,0:T(8,128)(2,1)S(1)} %collective-permute-done.27, bf16[512,768]{1,0:T(8,128)(2,1)S(1)} %copy-done.17, bf16[512,2048]{1,0:T(8,128)(2,1)S(1)} %copy-done.15, s32[]{:T(128)S(6)} %select_n.19), kind=kOutput, calls=%fused_computation.1 | convolution fusion | flops 807665664 | bytes 4980740 | tf_op jit(solution)/shard_map/dot_general | solution.py:20
  132.7 2.2 %add_convert_fusion = bf16[384,2048]{1,0:T(8,128)(2,1)} fusion(bf16[384,2048]{1,0:T(8,128)(2,1)S(1)} %collective-permute-done.28, bf16[512,2048]{1,0:T(8,128)(2,1)S(1)} %copy-done.14, bf16[512,768]{1,0:T(8,128)(2,1)S(1)} %copy-done.18, s32[]{:T(128)S(6)} %select_n.21), kind=kOutput, calls=%fused_computation | convolution fusion | flops 807665664 | bytes 5636100 | tf_op jit(solution)/shard_map/dot_general | solution.py:20
  134.8 2.2 %add_convert_fusion.2 = bf16[1024,768]{1,0:T(8,128)(2,1)} fusion(bf16[1024,768]{1,0:T(8,128)(2,1)S(1)} %collective-permute-done.26, bf16[512,768]{1,0:T(8,128)(2,1)S(1)} %copy-done.16, bf16[512,2048]{1,0:T(8,128)(2,1)S(1)} %copy-done.15, s32[]{:T(128)S(6)} %select_n.19), kind=kOutput, calls=%fused_computation.2 | convolution fusion | flops 807665664 | bytes 4980740 | tf_op jit(solution)/shard_map/dot_general | solution.py:20
  (100 shorter events, 37.7 us)
Async XLA Ops:
  8.0 44.6 %collective-permute-start.14 = (bf16[384,2048]{1,0:T(8,128)(2,1)}, bf16[384,2048]{1,0:T(8,128)(2,1)}, u32[]{:S(2)}, u32[]{:S(2)}) collective-permute-start(bf16[384,2048]{1,0:T(8,128)(2,1)} %bitcast.20), channel_id=1, source_target_pairs={{0,1},{1,0},{2,3},{3,2},{4,5},{5,4},{6,7},{7,6},{8,9},{9,8},{10,11... | collective-permute-start | bytes 4718600 | tf_op jit(solution)/shard_map/ppermute | solution.py:16
  9.6 14.6 %collective-permute-start.1 = (bf16[64,2176]{1,0:T(8,128)(2,1)S(1)}, bf16[64,2176]{1,0:T(8,128)(2,1)S(1)}, u32[]{:S(2)}, u32[]{:S(2)}) collective-permute-start(bf16[64,2176]{1,0:T(8,128)(2,1)S(1)} %pad_maximum_fusion.refs_0_), channel_id=1, source_target_pairs={{0,8},{8,0},{16,24},{24,16},{1,9},{9,1},{17,25},{25,17},{2,10},{10... | collective-permute-start | bytes 835592 | tf_op jit(solution)/shard_map/ppermute | solution.py:157
  12.6 11.6 %collective-permute-start.2 = (bf16[64,2176]{1,0:T(8,128)(2,1)S(1)}, bf16[64,2176]{1,0:T(8,128)(2,1)S(1)}, u32[]{:S(2)}, u32[]{:S(2)}) collective-permute-start(bf16[64,2176]{1,0:T(8,128)(2,1)S(1)} %pad_maximum_fusion.refs_0_), channel_id=1, source_target_pairs={{0,2},{1,5},{2,0},{3,7},{4,6},{5,1},{6,4},{7,3},{8,10},{9,13},{10,... | collective-permute-start | bytes 835592 | tf_op jit(solution)/shard_map/ppermute | solution.py:165
  14.1 15.1 %collective-permute-start = (bf16[64,2176]{1,0:T(8,128)(2,1)S(1)}, bf16[64,2176]{1,0:T(8,128)(2,1)S(1)}, u32[]{:S(2)}, u32[]{:S(2)}) collective-permute-start(bf16[64,2176]{1,0:T(8,128)(2,1)S(1)} %pad_maximum_fusion.refs_0_), channel_id=1, source_target_pairs={{0,16},{8,24},{16,0},{24,8},{1,17},{9,25},{17,1},{25,9},{2,18},{10... | collective-permute-start | bytes 835592 | tf_op jit(solution)/shard_map/ppermute | solution.py:157
  16.7 13.0 %collective-permute-start.4 = (bf16[64,2176]{1,0:T(8,128)(2,1)S(1)}, bf16[64,2176]{1,0:T(8,128)(2,1)S(1)}, u32[]{:S(2)}, u32[]{:S(2)}) collective-permute-start(bf16[64,2176]{1,0:T(8,128)(2,1)S(1)} %pad_maximum_fusion.refs_0_), channel_id=1, source_target_pairs={{0,4},{1,3},{2,6},{3,1},{4,0},{5,7},{6,2},{7,5},{8,12},{9,11},{10,... | collective-permute-start | bytes 835592 | tf_op jit(solution)/shard_map/ppermute | solution.py:165
  29.2 9.9 %collective-permute-start.9 = (bf16[64,2176]{1,0:T(8,128)(2,1)S(1)}, bf16[64,2176]{1,0:T(8,128)(2,1)S(1)}, u32[]{:S(2)}, u32[]{:S(2)}) collective-permute-start(bf16[64,2176]{1,0:T(8,128)(2,1)S(1)} %collective-permute-done.2.refs_4_), channel_id=1, source_target_pairs={{0,4},{1,3},{2,6},{3,1},{4,0},{5,7},{6,2},{7,5},{8,12},{9,11},{10,... | collective-permute-start | bytes 835592 | tf_op jit(solution)/shard_map/ppermute | solution.py:165
  33.0 9.7 %collective-permute-start.7 = (bf16[64,2176]{1,0:T(8,128)(2,1)S(1)}, bf16[64,2176]{1,0:T(8,128)(2,1)}, u32[]{:S(2)}, u32[]{:S(2)}) collective-permute-start(bf16[64,2176]{1,0:T(8,128)(2,1)S(1)} %collective-permute-done.refs_1_), channel_id=1, source_target_pairs={{0,2},{1,5},{2,0},{3,7},{4,6},{5,1},{6,4},{7,3},{8,10},{9,13},{10,... | collective-permute-start | bytes 835592 | tf_op jit(solution)/shard_map/ppermute | solution.py:165
  34.9 12.8 %collective-permute-start.12 = (bf16[64,2176]{1,0:T(8,128)(2,1)S(1)}, bf16[64,2176]{1,0:T(8,128)(2,1)S(1)}, u32[]{:S(2)}, u32[]{:S(2)}) collective-permute-start(bf16[64,2176]{1,0:T(8,128)(2,1)S(1)} %collective-permute-done.refs_1_), channel_id=1, source_target_pairs={{0,4},{1,3},{2,6},{3,1},{4,0},{5,7},{6,2},{7,5},{8,12},{9,11},{10,... | collective-permute-start | bytes 835592 | tf_op jit(solution)/shard_map/ppermute | solution.py:165
  39.0 9.6 %collective-permute-start.13 = (bf16[64,2176]{1,0:T(8,128)(2,1)S(1)}, bf16[64,2176]{1,0:T(8,128)(2,1)S(1)}, u32[]{:S(2)}, u32[]{:S(2)}) collective-permute-start(bf16[64,2176]{1,0:T(8,128)(2,1)S(1)} %collective-permute-done.3.refs_6_), channel_id=1, source_target_pairs={{0,4},{1,3},{2,6},{3,1},{4,0},{5,7},{6,2},{7,5},{8,12},{9,11},{10,... | collective-permute-start | bytes 835592 | tf_op jit(solution)/shard_map/ppermute | solution.py:165
  42.7 9.9 %collective-permute-start.11 = (bf16[64,2176]{1,0:T(8,128)(2,1)}, bf16[64,2176]{1,0:T(8,128)(2,1)}, u32[]{:S(2)}, u32[]{:S(2)}) collective-permute-start(bf16[64,2176]{1,0:T(8,128)(2,1)} %collective-permute-done.6.refs_3_), channel_id=1, source_target_pairs={{0,2},{1,5},{2,0},{3,7},{4,6},{5,1},{6,4},{7,3},{8,10},{9,13},{10,... | collective-permute-start | bytes 835592 | tf_op jit(solution)/shard_map/ppermute | solution.py:165
  44.6 12.3 %collective-permute-start.15 = (bf16[64,2176]{1,0:T(8,128)(2,1)}, bf16[64,2176]{1,0:T(8,128)(2,1)}, u32[]{:S(2)}, u32[]{:S(2)}) collective-permute-start(bf16[64,2176]{1,0:T(8,128)(2,1)} %collective-permute-done.6.refs_3_), channel_id=1, source_target_pairs={{0,4},{1,3},{2,6},{3,1},{4,0},{5,7},{6,2},{7,5},{8,12},{9,11},{10,... | collective-permute-start | bytes 835592 | tf_op jit(solution)/shard_map/ppermute | solution.py:165
  47.7 9.2 %collective-permute-start.16 = (bf16[64,2176]{1,0:T(8,128)(2,1)}, bf16[64,2176]{1,0:T(8,128)(2,1)}, u32[]{:S(2)}, u32[]{:S(2)}) collective-permute-start(bf16[64,2176]{1,0:T(8,128)(2,1)} %collective-permute-done.7.refs_5_), channel_id=1, source_target_pairs={{0,4},{1,3},{2,6},{3,1},{4,0},{5,7},{6,2},{7,5},{8,12},{9,11},{10,... | collective-permute-start | bytes 835592 | tf_op jit(solution)/shard_map/ppermute | solution.py:165
  73.8 15.2 %collective-permute-start.18 = (bf16[256,2048]{1,0:T(8,128)(2,1)}, bf16[256,2048]{1,0:T(8,128)(2,1)S(1)}, u32[]{:S(2)}, u32[]{:S(2)}) collective-permute-start(bf16[256,2048]{1,0:T(8,128)(2,1)} %get-tuple-element.71), channel_id=1, source_target_pairs={{0,4},{1,3},{2,6},{3,1},{4,0},{5,7},{6,2},{7,5},{8,12},{9,11},{10,... | collective-permute-start | bytes 3145736 | tf_op jit(solution)/shard_map/ppermute | solution.py:165
  89.0 17.5 %collective-permute-start.19 = (bf16[256,2048]{1,0:T(8,128)(2,1)}, bf16[256,2048]{1,0:T(8,128)(2,1)S(1)}, u32[]{:S(2)}, u32[]{:S(2)}) collective-permute-start(bf16[256,2048]{1,0:T(8,128)(2,1)} %get-tuple-element.79), channel_id=1, source_target_pairs={{0,4},{1,3},{2,6},{3,1},{4,0},{5,7},{6,2},{7,5},{8,12},{9,11},{10,... | collective-permute-start | bytes 3145736 | tf_op jit(solution)/shard_map/ppermute | solution.py:165
  92.1 12.6 %collective-permute-start.20 = (bf16[128,2048]{1,0:T(8,128)(2,1)}, bf16[128,2048]{1,0:T(8,128)(2,1)}, u32[]{:S(2)}, u32[]{:S(2)}) collective-permute-start(bf16[128,2048]{1,0:T(8,128)(2,1)} %add_convert_fusion.6), channel_id=1, source_target_pairs={{0,2},{1,5},{2,0},{3,7},{4,6},{5,1},{6,4},{7,3},{8,10},{9,13},{10,... | collective-permute-start | bytes 1572872 | tf_op jit(solution)/shard_map/ppermute | solution.py:165
  108.8 20.2 %collective-permute-start.27 = (bf16[1024,768]{1,0:T(8,128)(2,1)S(1)}, bf16[1024,768]{1,0:T(8,128)(2,1)S(1)}, u32[]{:S(2)}, u32[]{:S(2)}) collective-permute-start(bf16[1024,768]{1,0:T(8,128)(2,1)S(1)} %convolution_convert_fusion.1), channel_id=1, source_target_pairs={{0,1},{1,0},{2,3},{3,2},{4,5},{5,4},{6,7},{7,6},{8,9},{9,8},{10,11... | collective-permute-start | bytes 4718600 | tf_op jit(solution)/shard_map/ppermute | solution.py:16
  109.0 16.5 %collective-permute-start.24 = (bf16[128,2048]{1,0:T(8,128)(2,1)S(1)}, bf16[128,2048]{1,0:T(8,128)(2,1)S(1)}, u32[]{:S(2)}, u32[]{:S(2)}) collective-permute-start(bf16[128,2048]{1,0:T(8,128)(2,1)S(1)} %add_convert_fusion.4), channel_id=1, source_target_pairs={{0,2},{1,5},{2,0},{3,7},{4,6},{5,1},{6,4},{7,3},{8,10},{9,13},{10,... | collective-permute-start | bytes 1572872 | tf_op jit(solution)/shard_map/ppermute | solution.py:165
  110.1 11.7 %collective-permute-start.21 = (bf16[32,2048]{1,0:T(8,128)(2,1)S(1)}, bf16[32,2048]{1,0:T(8,128)(2,1)S(1)}, u32[]{:S(2)}, u32[]{:S(2)}) collective-permute-start(bf16[32,2048]{1,0:T(8,128)(2,1)S(1)} %get-tuple-element.102), channel_id=1, source_target_pairs={{0,16},{8,24},{16,0},{24,8},{1,17},{9,25},{17,1},{25,9},{2,18},{10... | collective-permute-start | bytes 393224 | tf_op jit(solution)/shard_map/ppermute | solution.py:157
  114.3 10.5 %collective-permute-start.23 = (bf16[32,2048]{1,0:T(8,128)(2,1)S(1)}, bf16[32,2048]{1,0:T(8,128)(2,1)S(1)}, u32[]{:S(2)}, u32[]{:S(2)}) collective-permute-start(bf16[32,2048]{1,0:T(8,128)(2,1)S(1)} %get-tuple-element.103), channel_id=1, source_target_pairs={{0,24},{8,16},{16,8},{24,0},{1,25},{9,17},{17,9},{25,1},{2,26},{10... | collective-permute-start | bytes 393224 | tf_op jit(solution)/shard_map/ppermute | solution.py:157
  121.8 10.9 %collective-permute-start.28 = (bf16[384,2048]{1,0:T(8,128)(2,1)S(1)}, bf16[384,2048]{1,0:T(8,128)(2,1)S(1)}, u32[]{:S(2)}, u32[]{:S(2)}) collective-permute-start(bf16[384,2048]{1,0:T(8,128)(2,1)S(1)} %convolution_convert_fusion), channel_id=1, source_target_pairs={{0,1},{1,0},{2,3},{3,2},{4,5},{5,4},{6,7},{7,6},{8,9},{9,8},{10,11... | collective-permute-start | bytes 4718600 | tf_op jit(solution)/shard_map/ppermute | solution.py:16
  121.8 13.0 %collective-permute-start.26 = (bf16[1024,768]{1,0:T(8,128)(2,1)S(1)}, bf16[1024,768]{1,0:T(8,128)(2,1)S(1)}, u32[]{:S(2)}, u32[]{:S(2)}) collective-permute-start(bf16[1024,768]{1,0:T(8,128)(2,1)S(1)} %convolution_convert_fusion.2), channel_id=1, source_target_pairs={{0,1},{1,0},{2,3},{3,2},{4,5},{5,4},{6,7},{7,6},{8,9},{9,8},{10,11... | collective-permute-start | bytes 4718600 | tf_op jit(solution)/shard_map/ppermute | solution.py:16
  125.8 11.2 %collective-permute-start.25 = (bf16[32,2048]{1,0:T(8,128)(2,1)S(1)}, bf16[32,2048]{1,0:T(8,128)(2,1)S(1)}, u32[]{:S(2)}, u32[]{:S(2)}) collective-permute-start(bf16[32,2048]{1,0:T(8,128)(2,1)S(1)} %get-tuple-element.99), channel_id=1, source_target_pairs={{0,16},{8,24},{16,0},{24,8},{1,17},{9,25},{17,1},{25,9},{2,18},{10... | collective-permute-start | bytes 393224 | tf_op jit(solution)/shard_map/ppermute | solution.py:157
  128.0 9.0 %collective-permute-start.29 = (bf16[32,2048]{1,0:T(8,128)(2,1)S(1)}, bf16[32,2048]{1,0:T(8,128)(2,1)S(1)}, u32[]{:S(2)}, u32[]{:S(2)}) collective-permute-start(bf16[32,2048]{1,0:T(8,128)(2,1)S(1)} %get-tuple-element.101), channel_id=1, source_target_pairs={{0,8},{8,0},{16,24},{24,16},{1,9},{9,1},{17,25},{25,17},{2,10},{10... | collective-permute-start | bytes 393224 | tf_op jit(solution)/shard_map/ppermute | solution.py:157
  129.0 10.1 %collective-permute-start.30 = (bf16[32,2048]{1,0:T(8,128)(2,1)S(1)}, bf16[32,2048]{1,0:T(8,128)(2,1)S(1)}, u32[]{:S(2)}, u32[]{:S(2)}) collective-permute-start(bf16[32,2048]{1,0:T(8,128)(2,1)S(1)} %get-tuple-element.100), channel_id=1, source_target_pairs={{0,24},{8,16},{16,8},{24,0},{1,25},{9,17},{17,9},{25,1},{2,26},{10... | collective-permute-start | bytes 393224 | tf_op jit(solution)/shard_map/ppermute | solution.py:157
  (26 other events, 370.5 us)

commit v4 on v3

--- a/solution.py
+++ b/solution.py
@@ -174,23 +174,21 @@
 
 def gather_blocks(block, beside):
     count = lax.axis_size("grp")
-    beside, waiting = list(beside), list(range(len(beside)))
-    moved, first, second, both = {0: block}, {}, {}, {}
-    mask = 1
-    while mask < count:
-        moved[mask] = swap_group(block, mask)
-        mask *= 2
+    moved, first, second, both = {0: block, 1: swap_group(block, 1)}, {}, {}, {}
     for k in range(count + 1):
         due = [
             (part, step)
-            for part, step in ((moved, k), (first, k - 1), (second, k - 2), (both, k - 3))
+            for part, step in ((moved, k), (first, k - 1), (second, k - 1), (both, k - 3))
             if k > 0 and step in part
         ]
-        if k > 1 and waiting:
-            due.append((beside, waiting.pop(0)))
-        if due:
-            for (part, step), value in zip(due, tie([part[step] for part, step in due])):
-                part[step] = value
+        values = beside(k, [part[step] for part, step in due])
+        for (part, step), value in zip(due, values):
+            part[step] = value
+        if k == 0:
+            mask = 2
+            while mask < count:
+                moved[mask] = swap_group(moved[0], mask)
+                mask *= 2
         if k < count:
             mask = 1
             while mask < (k & -k):
@@ -200,8 +198,7 @@
             second[k] = swap_inner(moved[k], SECOND)
         if k > 0:
             both[k - 1] = swap_inner(first[k - 1], SECOND)
-    pieces = [part[step] for part in (moved, first, second, both) for step in steps_of(count)]
-    return pieces, beside
+    return [part[step] for part in (moved, first, second, both) for step in steps_of(count)]
 
 
 def add_bf16(left, right):
@@ -214,19 +211,28 @@
     return add_bf16(here[0].astype(jnp.float32) + came[0].astype(jnp.float32), passed)
 
 
-def reduce_column(column, beside=()):
+def send_column(column):
     count = lax.axis_size("grp")
     rows = column.shape[0] // count
-    came = [
-        swap_group(column[q * rows : (q + 1) * rows], step)
+    return [
+        column[q * rows : (q + 1) * rows] if step == 0
+        else swap_group(column[q * rows : (q + 1) * rows], step)
         for q, step in enumerate(steps_of(count))
-        if step
     ]
-    came[0], *beside = tie((came[0], *beside)) if beside else came[:1]
-    total = column[:rows].astype(jnp.float32)
-    for value in came:
+
+
+def halve_column(column, masks):
+    for mask in masks:
+        half = column.shape[0] // 2
+        column = add_bf16(column[:half], swap_group(column[half:], mask))
+    return column
+
+
+def add_all(values):
+    total = values[0].astype(jnp.float32)
+    for value in values[1:]:
         total = total + value.astype(jnp.float32)
-    return total.astype(jnp.bfloat16), beside
+    return total.astype(jnp.bfloat16)
 
 
 def token_block(tokens, cotangent, expert_ids, gate_probs, expert_count):
@@ -274,6 +280,12 @@
     return copies
 
 
+def start_parts(parts, whole, sems, first_sem):
+    size = parts[0].shape[0]
+    places = [whole.at[pl.ds(k * size, size), :] for k in range(len(parts))]
+    return start_out(list(zip(parts, places)), sems, first_sem)
+
+
 def wait_all(copies):
     for copy in copies:
         copy.wait()
@@ -297,40 +309,50 @@
     return [pl.ds(i * size // count, size // count) for i in range(count)]
 
 
-def forward_kernel(rows, count, where_ref, *refs):
+def assemble_kernel(rows, count, *refs):
+    pieces, halves, refs = refs[:count], refs[count : count + 2], refs[count + 2 :]
+    whole_out, hidden_out, whole, hidden, sems, half_sems, out_sems = refs
+    copies = start_rows(pieces, whole, 0, rows, 0, sems)
+    wait_all(copies + start_parts(halves, hidden, half_sems, 0))
+    wait_all(start_out([(whole, whole_out), (hidden, hidden_out)], out_sems, 0))
+
+
+def forward_kernel(rows, count, expert_count, where_ref, *refs):
     pieces, refs = refs[:count], refs[count:]
     gate, up, down = refs[0:2], refs[2:4], refs[4:6]
-    keep, send, gate_pre_out, up_pre_out, hidden_out, rows_out = refs[6:12]
-    rows_in, side, gate_all, up_all, down_all, gate_pre, up_pre, hidden, out = refs[12:21]
-    row_sems, side_sems, weight_sems, out_sems = refs[21:]
+    whole_out, gate_pre_out, up_pre_out, hidden_out = refs[6:10]
+    rows_in, side, gate_all, up_all, down_all, gate_pre, up_pre, hidden, out = refs[10:19]
+    row_sems, side_sems, weight_sems, out_sems = refs[19:]
     width = rows_in.shape[1]
     row_copies = start_rows(pieces, rows_in, 0, rows, 0, row_sems)
     gate_copies = start_halves(gate, gate_all, weight_sems, 0, where_ref[0])
+    wait_all(row_copies)
     up_copies = start_halves(up, up_all, weight_sems, 2, where_ref[0])
+    wait_all(gate_copies)
     side_copies = start_rows(pieces, side, 0, rows, width, side_sems)
     down_copies = start_halves(down, down_all, weight_sems, 4, where_ref[0])
-    wait_all(row_copies)
-    outs = start_out([(rows_in, rows_out)], out_sems, 0)
-    wait_all(gate_copies)
-    gate_pre[...] = jnp.dot(rows_in[...], gate_all[...], preferred_element_type=jnp.float32)
-    outs += start_out([(gate_pre, gate_pre_out)], out_sems, 1)
+    pre = jnp.dot(rows_in[...], gate_all[...], preferred_element_type=jnp.float32)
+    gate_pre[...] = pre.astype(gate_pre.dtype)
+    act = pre * jax.nn.sigmoid(pre)
     wait_all(up_copies)
-    up_pre[...] = jnp.dot(rows_in[...], up_all[...], preferred_element_type=jnp.float32)
-    outs += start_out([(up_pre, up_pre_out)], out_sems, 2)
-    act = gate_pre[...] * jax.nn.sigmoid(gate_pre[...])
-    hidden[...] = (act * up_pre[...]).astype(jnp.bfloat16)
-    outs += start_out([(hidden, hidden_out)], out_sems, 3)
+    pre = jnp.dot(rows_in[...], up_all[...], preferred_element_type=jnp.float32)
+    up_pre[...] = pre.astype(up_pre.dtype)
+    hidden[...] = (act * pre).astype(jnp.bfloat16)
+    outs = start_out(
+        [(gate_pre, gate_pre_out), (up_pre, up_pre_out), (hidden, hidden_out)], out_sems, 0
+    )
     wait_all(side_copies)
-    probs = weights_of(side, where_ref[1], count)
+    probs = weights_of(side, where_ref[1], expert_count)
     wait_all(down_copies)
     for t, cols in enumerate(tiles(width, 2)):
         part = jnp.dot(hidden[...], down_all[:, cols], preferred_element_type=jnp.float32)
         out[:, cols] = (part * probs).astype(jnp.bfloat16)
-        outs += start_out(halves_of(out, cols, keep, send), out_sems, 4 + 2 * t)
+        outs += start_out([(out.at[:, cols], whole_out.at[:, cols])], out_sems, 3 + t)
     wait_all(outs)
 
 
-def backward_kernel(rows, count, where_ref, gate_pre_in, up_pre_in, *refs):
+def backward_kernel(rows, count, where_ref, *refs):
+    gate_pre_in, up_pre_in, refs = refs[0:2], refs[2:4], refs[4:]
     pieces, refs = refs[:count], refs[count:]
     gate, up, down = refs[0:2], refs[2:4], refs[4:6]
     keep, send, dgate_out, dup_out, scaled_out = refs[6:11]
@@ -340,21 +362,21 @@
     row_copies = start_rows(pieces, scaled, rows, rows, 0, row_sems)
     side_copies = start_rows(pieces, side, 0, rows, width, side_sems)
     down_copies = start_halves(down, down_all, weight_sems, 4, where_ref[0])
-    pre_copies = start_out([(gate_pre_in, gate_pre), (up_pre_in, up_pre)], pre_sems, 0)
+    pre_copies = start_parts(gate_pre_in, gate_pre, pre_sems, 0)
+    pre_copies += start_parts(up_pre_in, up_pre, pre_sems, 2)
+    wait_all(row_copies + side_copies)
     gate_copies = start_halves(gate, gate_all, weight_sems, 0, where_ref[0])
     up_copies = start_halves(up, up_all, weight_sems, 2, where_ref[0])
-    wait_all(row_copies + side_copies)
     probs = weights_of(side, where_ref[1], count)
     scaled[...] = (scaled[...].astype(jnp.float32) * probs).astype(jnp.bfloat16)
     outs = start_out([(scaled, scaled_out)], out_sems, 0)
     wait_all(down_copies)
     dhidden = contract_cols(scaled[...], down_all[...])
     wait_all(pre_copies)
-    sigma = jax.nn.sigmoid(gate_pre[...])
-    dgate[...] = (
-        dhidden * up_pre[...] * sigma * (1.0 + gate_pre[...] * (1.0 - sigma))
-    ).astype(jnp.bfloat16)
-    dup[...] = (dhidden * (gate_pre[...] * sigma)).astype(jnp.bfloat16)
+    pre, gain = gate_pre[...].astype(jnp.float32), up_pre[...].astype(jnp.float32)
+    sigma = jax.nn.sigmoid(pre)
+    dgate[...] = (dhidden * gain * sigma * (1.0 + pre * (1.0 - sigma))).astype(jnp.bfloat16)
+    dup[...] = (dhidden * (pre * sigma)).astype(jnp.bfloat16)
     outs += start_out([(dgate, dgate_out), (dup, dup_out)], out_sems, 1)
     wait_all(gate_copies + up_copies)
     for t, cols in enumerate(tiles(width, 2)):
@@ -381,13 +403,21 @@
     )(*inputs)
 
 
-def partner_in_turn(values):
-    came, values = [], list(values)
-    for k in range(len(values)):
-        came.append(partner_2(values[k], "rep", 0))
-        if k + 1 < len(values):
-            came[k], values[k + 1] = tie((came[k], values[k + 1]))
-    return came
+class PartnerWeights:
+    def __init__(self, own):
+        self.own, self.came = list(own), []
+
+    def __call__(self, step, values):
+        if not values:
+            return values
+        k = len(self.came)
+        old, new = self.came[k - 1 :] if k > 1 else [], self.own[k : k + 1]
+        values = list(tie((*values, *old, *new)))
+        if new:
+            self.came.append(partner_2(values.pop(), "rep", 0))
+        if old:
+            self.came[k - 1] = values.pop()
+        return values
 
 
 def dense_local(tokens, cotangent, expert_ids, gate_probs, gate_weight, up_weight, down_weight):
@@ -398,41 +428,63 @@
     half_hidden = down_weight.shape[1]
     total = expert_count * rows
     own = (gate_weight[0], up_weight[0], down_weight[0])
-    partner = partner_in_turn(own)
+    partner = PartnerWeights(own)
     block = token_block(tokens, cotangent, expert_ids, gate_probs, expert_count)
-    pieces, partner = gather_blocks(block, partner)
+    pieces = gather_blocks(block, partner)
+    partner = partner.came
     weights = [value for pair in zip(own, partner) for value in pair]
     expert = lax.axis_index("grp") * lax.axis_size("exp") + lax.axis_index("exp")
     where = jnp.stack([replica, expert]).astype(jnp.int32)
-    bf16, f32 = jnp.bfloat16, jnp.float32
-    wide, narrow, pre = ((total, width), bf16), ((total, hidden_width), bf16), ((total, hidden_width), f32)
+    bf16 = jnp.bfloat16
+    wide, narrow = ((total, width), bf16), ((total, hidden_width), bf16)
     half_wide = ((total // 2, width), bf16)
-    held = [
-        wide,
-        ((total, side_width(expert_count)), bf16),
+    half_narrow = ((total // 2, hidden_width), bf16)
+    mats = [
         ((width, hidden_width), bf16),
         ((width, hidden_width), bf16),
         ((hidden_width, width), bf16),
-        pre,
-        pre,
     ]
+    side = side_width(expert_count)
     flops = 6 * total * width * hidden_width
-    out_keep, out_send, gate_pre, up_pre, hidden, rows_in = expert_call(
-        functools.partial(forward_kernel, rows, expert_count),
-        [half_wide, half_wide, pre, pre, narrow, wide],
-        held + [narrow, wide],
-        [expert_count, expert_count, 6, 8],
-        flops,
-        [where, *pieces, *weights],
-    )
+    half_count = expert_count // 2
+    forward, waiting = [], pieces[half_count:]
+    for half_pieces in (pieces[:half_count], None):
+        forward.append(
+            list(expert_call(
+                functools.partial(forward_kernel, rows, half_count, expert_count),
+                [half_wide] + [half_narrow] * 3,
+                [half_wide, ((total // 2, side), bf16), *mats] + [half_narrow] * 3 + [half_wide],
+                [half_count, half_count, 6, 5],
+                flops // 2,
+                [where, *(half_pieces or waiting), *weights],
+            ))
+        )
+        if half_pieces:
+            forward[0][0], waiting = tie((forward[0][0], waiting))
+    (out_keep, out_send), gate_pre, up_pre, hidden = zip(*forward)
+    held = [wide, ((total, side), bf16), *mats, narrow, narrow]
     out_came = swap_inner(out_send, SECOND)
+    rows_in, hidden = pl.pallas_call(
+        functools.partial(assemble_kernel, rows, expert_count),
+        out_shape=[jax.ShapeDtypeStruct(*wide), jax.ShapeDtypeStruct(*narrow)],
+        in_specs=[ANY] * (expert_count + 2),
+        out_specs=[ANY, ANY],
+        scratch_shapes=[
+            pltpu.VMEM(*wide),
+            pltpu.VMEM(*narrow),
+            pltpu.SemaphoreType.DMA((expert_count,)),
+            pltpu.SemaphoreType.DMA((2,)),
+            pltpu.SemaphoreType.DMA((2,)),
+        ],
+        compiler_params=pltpu.CompilerParams(vmem_limit_bytes=VMEM_LIMIT // 4),
+    )(*pieces, *hidden)
     grad_keep, grad_send, dgate, dup, rows_scaled = expert_call(
         functools.partial(backward_kernel, rows, expert_count),
         [half_wide, half_wide, narrow, narrow, wide],
         held + [narrow, narrow, wide],
-        [expert_count, expert_count, 6, 2, 7],
+        [expert_count, expert_count, 6, 4, 7],
         flops,
-        [where, gate_pre, up_pre, *pieces, *weights],
+        [where, *gate_pre, *up_pre, *pieces, *weights],
     )
     out_came, grad_keep, grad_send, dgate, dup, rows_scaled = tie(
         (out_came, grad_keep, grad_send, dgate, dup, rows_scaled)
@@ -456,10 +508,16 @@
     gate_out = add_bf16(contract_rows(half(rows_in, replica, half_width), dgate), back[0])
     up_out = add_bf16(contract_rows(half(rows_in, replica, half_width), dup), back[1])
     down_out = add_bf16(contract_rows(half(hidden, replica, half_hidden), rows_scaled), back[2])
-    layer_out, _ = reduce_column(out_column)
-    token_grad, (gate_out, up_out, down_out) = reduce_column(
-        reduce_part(grad_keep.reshape(2, -1, width), grad_came), (gate_out, up_out, down_out)
-    )
+    masks = [2**bit for bit in range(lax.axis_size("grp").bit_length() - 1)]
+    out_column = halve_column(out_column, masks[:-1])
+    half = out_column.shape[0] // 2
+    out_terms = [out_column[:half], swap_group(out_column[half:], masks[-1])]
+    grad_column = reduce_part(grad_keep.reshape(2, -1, width), grad_came)
+    grad_terms = send_column(grad_column)
+    out_terms, grad_terms[1], gate_out, up_out, down_out = tie(
+        (out_terms, grad_terms[1], gate_out, up_out, down_out)
+    )
+    layer_out, token_grad = add_all(out_terms), add_all(grad_terms)
     return layer_out, token_grad, gate_out[None], up_out[None], down_out[None]
 
 

time: 140 us -> 132 us (0.943)
  starting transfers between devices: 48.6 us -> 37.2 us
  waiting for transfers between devices: 46.5 us -> 40.5 us
  local copies, waits for them, and re-layouts: 0.27 us -> 5.04 us
  Pallas kernels: 25.8 us -> 29.8 us
  other arithmetic: 6.83 us -> 8.52 us
    ppermute x16, starting transfers between devices: 30.8 us -> 22.9 us  [swap_inner(): return lax.ppermute(value, ('exp', 'rep'), pairs)]
    ppermute x6, waiting for transfers between devices: 5.53 us -> 0.02 us  [partner_2(): return lax.ppermute(value, axis, pairs)]
    unnamed x38 -> x78, local copies, waits for them, and re-layouts: 0.07 us -> 4.82 us
    ppermute x9 -> x8, starting transfers between devices: 16 us -> 12.7 us  [swap_group(): return lax.ppermute(value, 'grp', [(i, i ^ mask) for i in range(count)])]
    ppermute x9 -> x8, waiting for transfers between devices: 15.1 us -> 12.8 us  [swap_group(): return lax.ppermute(value, 'grp', [(i, i ^ mask) for i in range(count)])]
    pallas_call x2 -> x3, Pallas kernels: 25.8 us -> 27.8 us  [expert_call(): pl.pallas_call(kernel, out_shape=[jax.ShapeDtypeStruct(shape, dtype) for...]
    pallas_call x0 -> x1, Pallas kernels: none -> 1.98 us  [dense_local(): pl.pallas_call(functools.partial(assemble_kernel, rows, expert_count), ou...]
    convert_element_type x4 -> x5, other arithmetic: 2.75 us -> 4.71 us  [add_bf16(): (left.astype(jnp.float32) + right.astype(jnp.float32)).astype(jnp.bfloat16)]
  transfers between devices with their start and end apart: 31 -> 30, of which waited for: 15 -> 18; matrix products, arithmetic and copies ran while one was open for 11% -> 12% of each run, Pallas kernels for 9% -> 17%
where the time goes in v4:
time: 132 us
  waiting for transfers between devices  40.5 us (31%)
  starting transfers between devices  37.2 us (28%)
  Pallas kernels  29.8 us (23%)
  matrix products  9.68 us (7%)
  other arithmetic  8.52 us (6%)
  local copies, waits for them, and re-layouts  5.04 us (4%)
    pallas_call x3, Pallas kernels, expert_call(): pl.pallas_call(kernel, out_shape=[jax.ShapeDtypeStruct(shape, dtype) for...  27.8 us
    ppermute x16, waiting for transfers between devices, swap_inner(): return lax.ppermute(value, ('exp', 'rep'), pairs)  27.7 us
    ppermute x16, starting transfers between devices, swap_inner(): return lax.ppermute(value, ('exp', 'rep'), pairs)  22.9 us
    ppermute x8, waiting for transfers between devices, swap_group(): return lax.ppermute(value, 'grp', [(i, i ^ mask) for i in range(count)])  12.8 us
    ppermute x8, starting transfers between devices, swap_group(): return lax.ppermute(value, 'grp', [(i, i ^ mask) for i in range(count)])  12.7 us
    dot_general x6, matrix products, contract_rows(): lax.dot_general(left, right, (((0,), (0,)), ((), ())), preferred_element_...  9.68 us
    unnamed x78, local copies, waits for them, and re-layouts  4.82 us
    convert_element_type x5, other arithmetic, add_bf16(): (left.astype(jnp.float32) + right.astype(jnp.float32)).astype(jnp.bfloat16)  4.71 us
  transfers between devices with their start and end apart: 30, of which 18 were waited for; matrix products, arithmetic and copies ran while one was open for 12% of the time, Pallas kernels for 17%

profile of v4, /device:TPU:0, one launch (start us, length us, event | category | flops | bytes accessed | tf_op | source)
XLA Modules:
  0.0 131.8 jit_solution(7863498585684633635)
XLA Ops:
  2.6 3.1 %collective-permute-start.1 = (bf16[64,2176]{1,0:T(8,128)(2,1)S(1)}, bf16[64,2176]{1,0:T(8,128)(2,1)S(1)}, u32[]{:S(2)}, u32[]{:S(2)}) collective-permute-start(bf16[64,2176]{1,0:T(8,128)(2,1)S(1)} %pad_maximum_fusion.refs_0_.refs_4_), channel_id=1, source_target_pairs={{0,8},{8,0},{16,24},{24,16},{1,9},{9,1},{17,25},{25,17},{2,10},{10... | collective-permute-start | bytes 835592 | tf_op jit(solution)/shard_map/ppermute | solution.py:157
  8.7 2.6 %collective-permute-start = (bf16[64,2176]{1,0:T(8,128)(2,1)S(1)}, bf16[64,2176]{1,0:T(8,128)(2,1)S(1)}, u32[]{:S(2)}, u32[]{:S(2)}) collective-permute-start(bf16[64,2176]{1,0:T(8,128)(2,1)S(1)} %pad_maximum_fusion.refs_0_.refs_4_), channel_id=1, source_target_pairs={{0,16},{8,24},{16,0},{24,8},{1,17},{9,25},{17,1},{25,9},{2,18},{10... | collective-permute-start | bytes 835592 | tf_op jit(solution)/shard_map/ppermute | solution.py:157
  11.3 4.3 %collective-permute-done.1.refs_2_.refs_6_ = bf16[64,2176]{1,0:T(8,128)(2,1)S(1)} collective-permute-done((bf16[64,2176]{1,0:T(8,128)(2,1)S(1)}, bf16[64,2176]{1,0:T(8,128)(2,1)S(1)}, u32[]{:S(2)}, u32[]{:S(2)}) %collective-permute-start.1) | collective-permute-done | bytes 278560 | tf_op jit(solution)/shard_map/ppermute | solution.py:157
  15.7 2.8 %collective-permute-start.4 = (bf16[64,2176]{1,0:T(8,128)(2,1)S(1)}, bf16[64,2176]{1,0:T(8,128)(2,1)S(1)}, u32[]{:S(2)}, u32[]{:S(2)}) collective-permute-start(bf16[64,2176]{1,0:T(8,128)(2,1)S(1)} %collective-permute-done.1.refs_2_.refs_6_), channel_id=1, source_target_pairs={{0,2},{1,5},{2,0},{3,7},{4,6},{5,1},{6,4},{7,3},{8,10},{9,13},{10,... | collective-permute-start | bytes 835592 | tf_op jit(solution)/shard_map/ppermute | solution.py:165
  18.5 2.5 %collective-permute-start.5 = (bf16[64,2176]{1,0:T(8,128)(2,1)S(1)}, bf16[64,2176]{1,0:T(8,128)(2,1)S(1)}, u32[]{:S(2)}, u32[]{:S(2)}) collective-permute-start(bf16[64,2176]{1,0:T(8,128)(2,1)S(1)} %collective-permute-done.1.refs_2_.refs_6_), channel_id=1, source_target_pairs={{0,4},{1,3},{2,6},{3,1},{4,0},{5,7},{6,2},{7,5},{8,12},{9,11},{10,... | collective-permute-start | bytes 835592 | tf_op jit(solution)/shard_map/ppermute | solution.py:165
  21.0 2.2 %collective-permute-done.refs_1_.refs_5_ = bf16[64,2176]{1,0:T(8,128)(2,1)S(1)} collective-permute-done((bf16[64,2176]{1,0:T(8,128)(2,1)S(1)}, bf16[64,2176]{1,0:T(8,128)(2,1)S(1)}, u32[]{:S(2)}, u32[]{:S(2)}) %collective-permute-start) | collective-permute-done | bytes 278560 | tf_op jit(solution)/shard_map/ppermute | solution.py:157
  23.2 2.3 %collective-permute-done.4.refs_6_.refs_10_ = bf16[64,2176]{1,0:T(8,128)(2,1)S(1)} collective-permute-done((bf16[64,2176]{1,0:T(8,128)(2,1)S(1)}, bf16[64,2176]{1,0:T(8,128)(2,1)S(1)}, u32[]{:S(2)}, u32[]{:S(2)}) %collective-permute-start.4) | collective-permute-done | bytes 278560 | tf_op jit(solution)/shard_map/ppermute | solution.py:165
  29.9 4.4 %collective-permute-done.9.refs_4_.refs_16_.refs_12_ = bf16[64,2176]{1,0:T(8,128)(2,1)S(1)} collective-permute-done((bf16[64,2176]{1,0:T(8,128)(2,1)S(1)}, bf16[64,2176]{1,0:T(8,128)(2,1)S(1)}, u32[]{:S(2)}, u32[]{:S(2)}) %collective-permute-start.9) | collective-permute-done | bytes 278560 | tf_op jit(solution)/shard_map/ppermute | solution.py:165
  34.3 2.3 %collective-permute-done.6.refs_3_.refs_7_ = bf16[64,2176]{1,0:T(8,128)(2,1)S(1)} collective-permute-done((bf16[64,2176]{1,0:T(8,128)(2,1)S(1)}, bf16[64,2176]{1,0:T(8,128)(2,1)S(1)}, u32[]{:S(2)}, u32[]{:S(2)}) %collective-permute-start.6) | collective-permute-done | bytes 278560 | tf_op jit(solution)/shard_map/ppermute | solution.py:157
  42.5 5.6 %collective-permute-done.13.refs_6_.refs_18_.refs_14_ = bf16[64,2176]{1,0:T(8,128)(2,1)S(1)} collective-permute-done((bf16[64,2176]{1,0:T(8,128)(2,1)S(1)}, bf16[64,2176]{1,0:T(8,128)(2,1)S(1)}, u32[]{:S(2)}, u32[]{:S(2)}) %collective-permute-start.13) | collective-permute-done | bytes 278560 | tf_op jit(solution)/shard_map/ppermute | solution.py:165
  48.1 2.1 %collective-permute-start.16 = (bf16[64,2176]{1,0:T(8,128)(2,1)S(1)}, bf16[64,2176]{1,0:T(8,128)(2,1)S(1)}, u32[]{:S(2)}, u32[]{:S(2)}) collective-permute-start(bf16[64,2176]{1,0:T(8,128)(2,1)S(1)} %collective-permute-done.7.refs_5_.refs_9_), channel_id=1, source_target_pairs={{0,4},{1,3},{2,6},{3,1},{4,0},{5,7},{6,2},{7,5},{8,12},{9,11},{10,... | collective-permute-start | bytes 835592 | tf_op jit(solution)/shard_map/ppermute | solution.py:165
  51.5 1.7 %collective-permute-start.17 = (bf16[64,2176]{1,0:T(8,128)(2,1)}, bf16[64,2176]{1,0:T(8,128)(2,1)S(1)}, u32[]{:S(2)}, u32[]{:S(2)}) collective-permute-start(bf16[64,2176]{1,0:T(8,128)(2,1)} %collective-permute-done.11.refs_7_.refs_11_), channel_id=1, source_target_pairs={{0,4},{1,3},{2,6},{3,1},{4,0},{5,7},{6,2},{7,5},{8,12},{9,11},{10,... | collective-permute-start | bytes 835592 | tf_op jit(solution)/shard_map/ppermute | solution.py:165
  53.9 7.6 %shard_map.110 = (bf16[256,2048]{1,0:T(8,128)(2,1)}, bf16[256,768]{1,0:T(8,128)(2,1)}, bf16[256,768]{1,0:T(8,128)(2,1)}, bf16[256,768]{1,0:T(8,128)(2,1)}) custom-call(s32[2]{0:T(128)} %pad_add_fusion.where_ref, bf16[64,2176]{1,0:T(8,128)(2,1)} %copy-done, bf16[64,2176]{1,0:T(8,128)(2,1)} %copy-done.8, bf16[64,2176]{1,0:T(8,128)(2,1)} %copy-done.2, ...), custom_call_target="tpu_custom_call" | custom-call | flops 2415919104 | bytes 11665412 | tf_op jit(solution)/shard_map/pallas_call | solution.py:390
  62.5 7.6 %shard_map.111 = (bf16[256,2048]{1,0:T(8,128)(2,1)}, bf16[256,768]{1,0:T(8,128)(2,1)}, bf16[256,768]{1,0:T(8,128)(2,1)}, bf16[256,768]{1,0:T(8,128)(2,1)}) custom-call(s32[2]{0:T(128)} %pad_add_fusion.where_ref, bf16[64,2176]{1,0:T(8,128)(2,1)} %copy-done.6, bf16[64,2176]{1,0:T(8,128)(2,1)} %copy-done.20, bf16[64,2176]{1,0:T(8,128)(2,1)} %copy-done.12, ...), custom_call_target="tpu_custom_call" | custom-call | flops 2415919104 | bytes 11665412 | tf_op jit(solution)/shard_map/pallas_call | solution.py:390
  70.5 12.6 %shard_map.112 = (bf16[256,2048]{1,0:T(8,128)(2,1)}, bf16[256,2048]{1,0:T(8,128)(2,1)}, bf16[512,768]{1,0:T(8,128)(2,1)}, bf16[512,768]{1,0:T(8,128)(2,1)}, bf16[512,2048]{1,0:T(8,128)(2,1)}) custom-call(s32[2]{0:T(128)} %pad_add_fusion.where_ref, bf16[256,768]{1,0:T(8,128)(2,1)} %get-tuple-element.94.refs_0_, bf16[256,768]{1,0:T(8,128)(2,1)} %get-tuple-element.95.refs_1_, ...), custom_call_target="tpu_custom_call" | custom-call | flops 4831838208 | bytes 15466500 | tf_op jit(solution)/shard_map/pallas_call | solution.py:390
  83.1 2.1 %collective-permute-done.18 = bf16[256,2048]{1,0:T(8,128)(2,1)S(1)} collective-permute-done((bf16[256,2048]{1,0:T(8,128)(2,1)}, bf16[256,2048]{1,0:T(8,128)(2,1)S(1)}, u32[]{:S(2)}, u32[]{:S(2)}) %collective-permute-start.18) | collective-permute-done | bytes 1048608 | tf_op jit(solution)/shard_map/ppermute | solution.py:165
  91.7 2.0 %shard_map.113 = (bf16[512,2048]{1,0:T(8,128)(2,1)S(1)}, bf16[512,768]{1,0:T(8,128)(2,1)S(1)}) custom-call(bf16[64,2176]{1,0:T(8,128)(2,1)S(1)} %copy-done.1, bf16[64,2176]{1,0:T(8,128)(2,1)S(1)} %copy-done.9, bf16[64,2176]{1,0:T(8,128)(2,1)S(1)} %copy-done.3, bf16[64,2176]{1,0:T(8,128)(2,1)S(1)} %copy-done.17, bf16[64,2176]{1,0:T(8,128)(2,1)S(1)} %copy-done.5, ...), custom_call_target="tpu_custom_call" | custom-call | tf_op jit(solution)/shard_map/pallas_call | solution.py:467
  93.7 7.8 %collective-permute-done.20 = bf16[128,2048]{1,0:T(8,128)(2,1)} collective-permute-done((bf16[128,2048]{1,0:T(8,128)(2,1)}, bf16[128,2048]{1,0:T(8,128)(2,1)}, u32[]{:S(2)}, u32[]{:S(2)}) %collective-permute-start.20) | collective-permute-done | bytes 524320 | tf_op jit(solution)/shard_map/ppermute | solution.py:165
  111.4 2.5 %collective-permute-start.22 = (bf16[32,2048]{1,0:T(8,128)(2,1)S(1)}, bf16[32,2048]{1,0:T(8,128)(2,1)S(1)}, u32[]{:S(2)}, u32[]{:S(2)}) collective-permute-start(bf16[32,2048]{1,0:T(8,128)(2,1)S(1)} %get-tuple-element.130), channel_id=1, source_target_pairs={{0,16},{8,24},{16,0},{24,8},{1,17},{9,25},{17,1},{25,9},{2,18},{10... | collective-permute-start | bytes 393224 | tf_op jit(solution)/shard_map/ppermute | solution.py:157
  116.4 2.5 %collective-permute-start.24 = (bf16[32,2048]{1,0:T(8,128)(2,1)S(1)}, bf16[32,2048]{1,0:T(8,128)(2,1)S(1)}, u32[]{:S(2)}, u32[]{:S(2)}) collective-permute-start(bf16[32,2048]{1,0:T(8,128)(2,1)S(1)} %get-tuple-element.129), channel_id=1, source_target_pairs={{0,16},{8,24},{16,0},{24,8},{1,17},{9,25},{17,1},{25,9},{2,18},{10... | collective-permute-start | bytes 393224 | tf_op jit(solution)/shard_map/ppermute | solution.py:157
  120.3 2.2 %add_convert_fusion.2 = bf16[1024,768]{1,0:T(8,128)(2,1)} fusion(bf16[1024,768]{1,0:T(8,128)(2,1)S(1)} %collective-permute-done.25, bf16[512,768]{1,0:T(8,128)(2,1)S(1)} %copy-done.38, bf16[512,2048]{1,0:T(8,128)(2,1)S(1)} %get-tuple-element.116, s32[]{:T(128)S(6)} %select_n.19), kind=kOutput, calls=%fused_computation.2 | convolution fusion | flops 807665664 | bytes 4980740 | tf_op jit(solution)/shard_map/dot_general | solution.py:20
  122.5 2.2 %add_convert_fusion = bf16[384,2048]{1,0:T(8,128)(2,1)} fusion(bf16[384,2048]{1,0:T(8,128)(2,1)S(1)} %collective-permute-done.27, bf16[512,2048]{1,0:T(8,128)(2,1)S(1)} %copy-done.36, bf16[512,768]{1,0:T(8,128)(2,1)S(1)} %get-tuple-element.119, s32[]{:T(128)S(6)} %select_n.21), kind=kOutput, calls=%fused_computation | convolution fusion | flops 807665664 | bytes 5636100 | tf_op jit(solution)/shard_map/dot_general | solution.py:20
  124.7 2.2 %add_convert_fusion.1 = bf16[1024,768]{1,0:T(8,128)(2,1)} fusion(bf16[1024,768]{1,0:T(8,128)(2,1)S(1)} %collective-permute-done.26, bf16[512,768]{1,0:T(8,128)(2,1)S(1)} %copy-done.37, bf16[512,2048]{1,0:T(8,128)(2,1)S(1)} %get-tuple-element.116, s32[]{:T(128)S(6)} %select_n.19), kind=kOutput, calls=%fused_computation.1 | convolution fusion | flops 807665664 | bytes 4980740 | tf_op jit(solution)/shard_map/dot_general | solution.py:20
  127.2 2.8 %collective-permute-done.24 = bf16[32,2048]{1,0:T(8,128)(2,1)S(1)} collective-permute-done((bf16[32,2048]{1,0:T(8,128)(2,1)S(1)}, bf16[32,2048]{1,0:T(8,128)(2,1)S(1)}, u32[]{:S(2)}, u32[]{:S(2)}) %collective-permute-start.24) | collective-permute-done | bytes 131104 | tf_op jit(solution)/shard_map/ppermute | solution.py:157
  (142 shorter events, 40.6 us)
Async XLA Ops:
  2.6 13.0 %collective-permute-start.1 = (bf16[64,2176]{1,0:T(8,128)(2,1)S(1)}, bf16[64,2176]{1,0:T(8,128)(2,1)S(1)}, u32[]{:S(2)}, u32[]{:S(2)}) collective-permute-start(bf16[64,2176]{1,0:T(8,128)(2,1)S(1)} %pad_maximum_fusion.refs_0_.refs_4_), channel_id=1, source_target_pairs={{0,8},{8,0},{16,24},{24,16},{1,9},{9,1},{17,25},{25,17},{2,10},{10... | collective-permute-start | bytes 835592 | tf_op jit(solution)/shard_map/ppermute | solution.py:157
  5.7 9.9 %collective-permute-start.2 = (bf16[64,2176]{1,0:T(8,128)(2,1)S(1)}, bf16[64,2176]{1,0:T(8,128)(2,1)S(1)}, u32[]{:S(2)}, u32[]{:S(2)}) collective-permute-start(bf16[64,2176]{1,0:T(8,128)(2,1)S(1)} %pad_maximum_fusion.refs_0_.refs_4_), channel_id=1, source_target_pairs={{0,2},{1,5},{2,0},{3,7},{4,6},{5,1},{6,4},{7,3},{8,10},{9,13},{10,... | collective-permute-start | bytes 835592 | tf_op jit(solution)/shard_map/ppermute | solution.py:165
  8.7 14.5 %collective-permute-start = (bf16[64,2176]{1,0:T(8,128)(2,1)S(1)}, bf16[64,2176]{1,0:T(8,128)(2,1)S(1)}, u32[]{:S(2)}, u32[]{:S(2)}) collective-permute-start(bf16[64,2176]{1,0:T(8,128)(2,1)S(1)} %pad_maximum_fusion.refs_0_.refs_4_), channel_id=1, source_target_pairs={{0,16},{8,24},{16,0},{24,8},{1,17},{9,25},{17,1},{25,9},{2,18},{10... | collective-permute-start | bytes 835592 | tf_op jit(solution)/shard_map/ppermute | solution.py:157
  15.7 9.9 %collective-permute-start.4 = (bf16[64,2176]{1,0:T(8,128)(2,1)S(1)}, bf16[64,2176]{1,0:T(8,128)(2,1)S(1)}, u32[]{:S(2)}, u32[]{:S(2)}) collective-permute-start(bf16[64,2176]{1,0:T(8,128)(2,1)S(1)} %collective-permute-done.1.refs_2_.refs_6_), channel_id=1, source_target_pairs={{0,2},{1,5},{2,0},{3,7},{4,6},{5,1},{6,4},{7,3},{8,10},{9,13},{10,... | collective-permute-start | bytes 835592 | tf_op jit(solution)/shard_map/ppermute | solution.py:165
  25.5 12.8 %collective-permute-start.10 = (bf16[1024,768]{1,0:T(8,128)(2,1)}, bf16[1024,768]{1,0:T(8,128)(2,1)S(1)}, u32[]{:S(2)}, u32[]{:S(2)}) collective-permute-start(bf16[1024,768]{1,0:T(8,128)(2,1)} %bitcast.18), channel_id=1, source_target_pairs={{0,1},{1,0},{2,3},{3,2},{4,5},{5,4},{6,7},{7,6},{8,9},{9,8},{10,11... | collective-permute-start | bytes 4718600 | tf_op jit(solution)/shard_map/ppermute | solution.py:16
  27.5 9.6 %collective-permute-start.7 = (bf16[64,2176]{1,0:T(8,128)(2,1)S(1)}, bf16[64,2176]{1,0:T(8,128)(2,1)S(1)}, u32[]{:S(2)}, u32[]{:S(2)}) collective-permute-start(bf16[64,2176]{1,0:T(8,128)(2,1)S(1)} %collective-permute-done.refs_1_.refs_5_), channel_id=1, source_target_pairs={{0,2},{1,5},{2,0},{3,7},{4,6},{5,1},{6,4},{7,3},{8,10},{9,13},{10,... | collective-permute-start | bytes 835592 | tf_op jit(solution)/shard_map/ppermute | solution.py:165
  28.7 9.6 %collective-permute-start.8 = (bf16[64,2176]{1,0:T(8,128)(2,1)S(1)}, bf16[64,2176]{1,0:T(8,128)(2,1)S(1)}, u32[]{:S(2)}, u32[]{:S(2)}) collective-permute-start(bf16[64,2176]{1,0:T(8,128)(2,1)S(1)} %collective-permute-done.refs_1_.refs_5_), channel_id=1, source_target_pairs={{0,4},{1,3},{2,6},{3,1},{4,0},{5,7},{6,2},{7,5},{8,12},{9,11},{10,... | collective-permute-start | bytes 835592 | tf_op jit(solution)/shard_map/ppermute | solution.py:165
  38.3 13.2 %collective-permute-start.14 = (bf16[384,2048]{1,0:T(8,128)(2,1)}, bf16[384,2048]{1,0:T(8,128)(2,1)}, u32[]{:S(2)}, u32[]{:S(2)}) collective-permute-start(bf16[384,2048]{1,0:T(8,128)(2,1)} %bitcast.22), channel_id=1, source_target_pairs={{0,1},{1,0},{2,3},{3,2},{4,5},{5,4},{6,7},{7,6},{8,9},{9,8},{10,11... | collective-permute-start | bytes 4718600 | tf_op jit(solution)/shard_map/ppermute | solution.py:16
  38.4 15.5 %collective-permute-start.15 = (bf16[1024,768]{1,0:T(8,128)(2,1)}, bf16[1024,768]{1,0:T(8,128)(2,1)}, u32[]{:S(2)}, u32[]{:S(2)}) collective-permute-start(bf16[1024,768]{1,0:T(8,128)(2,1)} %bitcast.14), channel_id=1, source_target_pairs={{0,1},{1,0},{2,3},{3,2},{4,5},{5,4},{6,7},{7,6},{8,9},{9,8},{10,11... | collective-permute-start | bytes 4718600 | tf_op jit(solution)/shard_map/ppermute | solution.py:16
  38.9 9.2 %collective-permute-start.13 = (bf16[64,2176]{1,0:T(8,128)(2,1)S(1)}, bf16[64,2176]{1,0:T(8,128)(2,1)S(1)}, u32[]{:S(2)}, u32[]{:S(2)}) collective-permute-start(bf16[64,2176]{1,0:T(8,128)(2,1)S(1)} %collective-permute-done.4.refs_6_.refs_10_), channel_id=1, source_target_pairs={{0,4},{1,3},{2,6},{3,1},{4,0},{5,7},{6,2},{7,5},{8,12},{9,11},{10,... | collective-permute-start | bytes 835592 | tf_op jit(solution)/shard_map/ppermute | solution.py:165
  40.6 9.7 %collective-permute-start.11 = (bf16[64,2176]{1,0:T(8,128)(2,1)S(1)}, bf16[64,2176]{1,0:T(8,128)(2,1)}, u32[]{:S(2)}, u32[]{:S(2)}) collective-permute-start(bf16[64,2176]{1,0:T(8,128)(2,1)S(1)} %collective-permute-done.6.refs_3_.refs_7_), channel_id=1, source_target_pairs={{0,2},{1,5},{2,0},{3,7},{4,6},{5,1},{6,4},{7,3},{8,10},{9,13},{10,... | collective-permute-start | bytes 835592 | tf_op jit(solution)/shard_map/ppermute | solution.py:165
  41.8 9.7 %collective-permute-start.12 = (bf16[64,2176]{1,0:T(8,128)(2,1)S(1)}, bf16[64,2176]{1,0:T(8,128)(2,1)}, u32[]{:S(2)}, u32[]{:S(2)}) collective-permute-start(bf16[64,2176]{1,0:T(8,128)(2,1)S(1)} %collective-permute-done.6.refs_3_.refs_7_), channel_id=1, source_target_pairs={{0,4},{1,3},{2,6},{3,1},{4,0},{5,7},{6,2},{7,5},{8,12},{9,11},{10,... | collective-permute-start | bytes 835592 | tf_op jit(solution)/shard_map/ppermute | solution.py:165
  48.1 13.5 %collective-permute-start.16 = (bf16[64,2176]{1,0:T(8,128)(2,1)S(1)}, bf16[64,2176]{1,0:T(8,128)(2,1)S(1)}, u32[]{:S(2)}, u32[]{:S(2)}) collective-permute-start(bf16[64,2176]{1,0:T(8,128)(2,1)S(1)} %collective-permute-done.7.refs_5_.refs_9_), channel_id=1, source_target_pairs={{0,4},{1,3},{2,6},{3,1},{4,0},{5,7},{6,2},{7,5},{8,12},{9,11},{10,... | collective-permute-start | bytes 835592 | tf_op jit(solution)/shard_map/ppermute | solution.py:165
  51.5 10.1 %collective-permute-start.17 = (bf16[64,2176]{1,0:T(8,128)(2,1)}, bf16[64,2176]{1,0:T(8,128)(2,1)S(1)}, u32[]{:S(2)}, u32[]{:S(2)}) collective-permute-start(bf16[64,2176]{1,0:T(8,128)(2,1)} %collective-permute-done.11.refs_7_.refs_11_), channel_id=1, source_target_pairs={{0,4},{1,3},{2,6},{3,1},{4,0},{5,7},{6,2},{7,5},{8,12},{9,11},{10,... | collective-permute-start | bytes 835592 | tf_op jit(solution)/shard_map/ppermute | solution.py:165
  70.1 15.1 %collective-permute-start.18 = (bf16[256,2048]{1,0:T(8,128)(2,1)}, bf16[256,2048]{1,0:T(8,128)(2,1)S(1)}, u32[]{:S(2)}, u32[]{:S(2)}) collective-permute-start(bf16[256,2048]{1,0:T(8,128)(2,1)} %get-tuple-element.93), channel_id=1, source_target_pairs={{0,4},{1,3},{2,6},{3,1},{4,0},{5,7},{6,2},{7,5},{8,12},{9,11},{10,... | collective-permute-start | bytes 3145736 | tf_op jit(solution)/shard_map/ppermute | solution.py:165
  85.2 18.8 %collective-permute-start.19 = (bf16[256,2048]{1,0:T(8,128)(2,1)}, bf16[256,2048]{1,0:T(8,128)(2,1)}, u32[]{:S(2)}, u32[]{:S(2)}) collective-permute-start(bf16[256,2048]{1,0:T(8,128)(2,1)} %get-tuple-element.103), channel_id=1, source_target_pairs={{0,4},{1,3},{2,6},{3,1},{4,0},{5,7},{6,2},{7,5},{8,12},{9,11},{10,... | collective-permute-start | bytes 3145736 | tf_op jit(solution)/shard_map/ppermute | solution.py:165
  86.4 15.2 %collective-permute-start.20 = (bf16[128,2048]{1,0:T(8,128)(2,1)}, bf16[128,2048]{1,0:T(8,128)(2,1)}, u32[]{:S(2)}, u32[]{:S(2)}) collective-permute-start(bf16[128,2048]{1,0:T(8,128)(2,1)} %add_convert_fusion.6), channel_id=1, source_target_pairs={{0,2},{1,5},{2,0},{3,7},{4,6},{5,1},{6,4},{7,3},{8,10},{9,13},{10,... | collective-permute-start | bytes 1572872 | tf_op jit(solution)/shard_map/ppermute | solution.py:165
  105.8 9.2 %collective-permute-start.23 = (bf16[128,2048]{1,0:T(8,128)(2,1)S(1)}, bf16[128,2048]{1,0:T(8,128)(2,1)S(1)}, u32[]{:S(2)}, u32[]{:S(2)}) collective-permute-start(bf16[128,2048]{1,0:T(8,128)(2,1)S(1)} %add_convert_fusion.4), channel_id=1, source_target_pairs={{0,2},{1,5},{2,0},{3,7},{4,6},{5,1},{6,4},{7,3},{8,10},{9,13},{10,... | collective-permute-start | bytes 1572872 | tf_op jit(solution)/shard_map/ppermute | solution.py:165
  108.0 11.0 %collective-permute-start.25 = (bf16[1024,768]{1,0:T(8,128)(2,1)S(1)}, bf16[1024,768]{1,0:T(8,128)(2,1)S(1)}, u32[]{:S(2)}, u32[]{:S(2)}) collective-permute-start(bf16[1024,768]{1,0:T(8,128)(2,1)S(1)} %convolution_convert_fusion.2), channel_id=1, source_target_pairs={{0,1},{1,0},{2,3},{3,2},{4,5},{5,4},{6,7},{7,6},{8,9},{9,8},{10,11... | collective-permute-start | bytes 4718600 | tf_op jit(solution)/shard_map/ppermute | solution.py:16
  109.1 15.6 %collective-permute-start.26 = (bf16[1024,768]{1,0:T(8,128)(2,1)S(1)}, bf16[1024,768]{1,0:T(8,128)(2,1)S(1)}, u32[]{:S(2)}, u32[]{:S(2)}) collective-permute-start(bf16[1024,768]{1,0:T(8,128)(2,1)S(1)} %convolution_convert_fusion.1), channel_id=1, source_target_pairs={{0,1},{1,0},{2,3},{3,2},{4,5},{5,4},{6,7},{7,6},{8,9},{9,8},{10,11... | collective-permute-start | bytes 4718600 | tf_op jit(solution)/shard_map/ppermute | solution.py:16
  110.7 11.8 %collective-permute-start.27 = (bf16[384,2048]{1,0:T(8,128)(2,1)S(1)}, bf16[384,2048]{1,0:T(8,128)(2,1)S(1)}, u32[]{:S(2)}, u32[]{:S(2)}) collective-permute-start(bf16[384,2048]{1,0:T(8,128)(2,1)S(1)} %convolution_convert_fusion), channel_id=1, source_target_pairs={{0,1},{1,0},{2,3},{3,2},{4,5},{5,4},{6,7},{7,6},{8,9},{9,8},{10,11... | collective-permute-start | bytes 4718600 | tf_op jit(solution)/shard_map/ppermute | solution.py:16
  111.4 15.8 %collective-permute-start.22 = (bf16[32,2048]{1,0:T(8,128)(2,1)S(1)}, bf16[32,2048]{1,0:T(8,128)(2,1)S(1)}, u32[]{:S(2)}, u32[]{:S(2)}) collective-permute-start(bf16[32,2048]{1,0:T(8,128)(2,1)S(1)} %get-tuple-element.130), channel_id=1, source_target_pairs={{0,16},{8,24},{16,0},{24,8},{1,17},{9,25},{17,1},{25,9},{2,18},{10... | collective-permute-start | bytes 393224 | tf_op jit(solution)/shard_map/ppermute | solution.py:157
  116.4 13.5 %collective-permute-start.24 = (bf16[32,2048]{1,0:T(8,128)(2,1)S(1)}, bf16[32,2048]{1,0:T(8,128)(2,1)S(1)}, u32[]{:S(2)}, u32[]{:S(2)}) collective-permute-start(bf16[32,2048]{1,0:T(8,128)(2,1)S(1)} %get-tuple-element.129), channel_id=1, source_target_pairs={{0,16},{8,24},{16,0},{24,8},{1,17},{9,25},{17,1},{25,9},{2,18},{10... | collective-permute-start | bytes 393224 | tf_op jit(solution)/shard_map/ppermute | solution.py:157
  118.9 11.7 %collective-permute-start.29 = (bf16[32,2048]{1,0:T(8,128)(2,1)S(1)}, bf16[32,2048]{1,0:T(8,128)(2,1)S(1)}, u32[]{:S(2)}, u32[]{:S(2)}) collective-permute-start(bf16[32,2048]{1,0:T(8,128)(2,1)S(1)} %get-tuple-element.128), channel_id=1, source_target_pairs={{0,24},{8,16},{16,8},{24,0},{1,25},{9,17},{17,9},{25,1},{2,26},{10... | collective-permute-start | bytes 393224 | tf_op jit(solution)/shard_map/ppermute | solution.py:157
  (45 other events, 694.8 us)

commit v5 on v4

--- a/solution.py
+++ b/solution.py
@@ -195,8 +195,10 @@
                 moved[k | mask] = swap_group(moved[k], mask)
                 mask *= 2
             first[k] = swap_inner(moved[k], FIRST)
-            second[k] = swap_inner(moved[k], SECOND)
-        if k > 0:
+            second[k] = swap_group(second[k - 1], 1) if k in (3,) else swap_inner(moved[k], SECOND)
+        if k - 1 in ():
+            both[k - 1] = swap_group(both[k - 2], 1)
+        elif k > 0:
             both[k - 1] = swap_inner(first[k - 1], SECOND)
     return [part[step] for part in (moved, first, second, both) for step in steps_of(count)]
 

time: 132 us -> 129 us (0.977)
  waiting for transfers between devices: 40.5 us -> 37.5 us
    ppermute x16 -> x15, waiting for transfers between devices: 27.7 us -> 25.8 us  [swap_inner(): return lax.ppermute(value, ('exp', 'rep'), pairs)]
    ppermute x8 -> x9, waiting for transfers between devices: 12.8 us -> 11.7 us  [swap_group(): return lax.ppermute(value, 'grp', [(i, i ^ mask) for i in range(count)])]
    ppermute x16 -> x15, starting transfers between devices: 22.9 us -> 23 us  [swap_inner(): return lax.ppermute(value, ('exp', 'rep'), pairs)]
    ppermute x8 -> x9, starting transfers between devices: 12.7 us -> 12.8 us  [swap_group(): return lax.ppermute(value, 'grp', [(i, i ^ mask) for i in range(count)])]
  transfers between devices with their start and end apart: 30 -> 30, of which waited for: 18 -> 15; matrix products, arithmetic and copies ran while one was open for 12% -> 12% of each run, Pallas kernels for 17% -> 17%
where the time goes in v5:
time: 129 us
  waiting for transfers between devices  37.5 us (29%)
  starting transfers between devices  37.3 us (29%)
  Pallas kernels  29.8 us (23%)
  matrix products  9.68 us (8%)
  other arithmetic  8.52 us (7%)
  local copies, waits for them, and re-layouts  5.04 us (4%)
    pallas_call x3, Pallas kernels, expert_call(): pl.pallas_call(kernel, out_shape=[jax.ShapeDtypeStruct(shape, dtype) for...  27.8 us
    ppermute x15, waiting for transfers between devices, swap_inner(): return lax.ppermute(value, ('exp', 'rep'), pairs)  25.8 us
    ppermute x15, starting transfers between devices, swap_inner(): return lax.ppermute(value, ('exp', 'rep'), pairs)  23 us
    ppermute x9, starting transfers between devices, swap_group(): return lax.ppermute(value, 'grp', [(i, i ^ mask) for i in range(count)])  12.8 us
    ppermute x9, waiting for transfers between devices, swap_group(): return lax.ppermute(value, 'grp', [(i, i ^ mask) for i in range(count)])  11.7 us
    dot_general x6, matrix products, contract_rows(): lax.dot_general(left, right, (((0,), (0,)), ((), ())), preferred_element_...  9.68 us
    unnamed x78, local copies, waits for them, and re-layouts  4.82 us
    convert_element_type x5, other arithmetic, add_bf16(): (left.astype(jnp.float32) + right.astype(jnp.float32)).astype(jnp.bfloat16)  4.71 us
  transfers between devices with their start and end apart: 30, of which 15 were waited for; matrix products, arithmetic and copies ran while one was open for 12% of the time, Pallas kernels for 17%

profile of v5, /device:TPU:0, one launch (start us, length us, event | category | flops | bytes accessed | tf_op | source)
XLA Modules:
  0.0 128.9 jit_solution(9655213211846901038)
XLA Ops:
  2.6 3.1 %collective-permute-start.1 = (bf16[64,2176]{1,0:T(8,128)(2,1)S(1)}, bf16[64,2176]{1,0:T(8,128)(2,1)S(1)}, u32[]{:S(2)}, u32[]{:S(2)}) collective-permute-start(bf16[64,2176]{1,0:T(8,128)(2,1)S(1)} %pad_maximum_fusion.refs_0_.refs_4_), channel_id=1, source_target_pairs={{0,8},{8,0},{16,24},{24,16},{1,9},{9,1},{17,25},{25,17},{2,10},{10... | collective-permute-start | bytes 835592 | tf_op jit(solution)/shard_map/ppermute | solution.py:157
  8.7 2.6 %collective-permute-start = (bf16[64,2176]{1,0:T(8,128)(2,1)S(1)}, bf16[64,2176]{1,0:T(8,128)(2,1)S(1)}, u32[]{:S(2)}, u32[]{:S(2)}) collective-permute-start(bf16[64,2176]{1,0:T(8,128)(2,1)S(1)} %pad_maximum_fusion.refs_0_.refs_4_), channel_id=1, source_target_pairs={{0,16},{8,24},{16,0},{24,8},{1,17},{9,25},{17,1},{25,9},{2,18},{10... | collective-permute-start | bytes 835592 | tf_op jit(solution)/shard_map/ppermute | solution.py:157
  11.3 4.3 %collective-permute-done.1.refs_2_.refs_6_ = bf16[64,2176]{1,0:T(8,128)(2,1)S(1)} collective-permute-done((bf16[64,2176]{1,0:T(8,128)(2,1)S(1)}, bf16[64,2176]{1,0:T(8,128)(2,1)S(1)}, u32[]{:S(2)}, u32[]{:S(2)}) %collective-permute-start.1) | collective-permute-done | bytes 278560 | tf_op jit(solution)/shard_map/ppermute | solution.py:157
  15.7 2.8 %collective-permute-start.4 = (bf16[64,2176]{1,0:T(8,128)(2,1)S(1)}, bf16[64,2176]{1,0:T(8,128)(2,1)S(1)}, u32[]{:S(2)}, u32[]{:S(2)}) collective-permute-start(bf16[64,2176]{1,0:T(8,128)(2,1)S(1)} %collective-permute-done.1.refs_2_.refs_6_), channel_id=1, source_target_pairs={{0,2},{1,5},{2,0},{3,7},{4,6},{5,1},{6,4},{7,3},{8,10},{9,13},{10,... | collective-permute-start | bytes 835592 | tf_op jit(solution)/shard_map/ppermute | solution.py:165
  18.5 2.5 %collective-permute-start.5 = (bf16[64,2176]{1,0:T(8,128)(2,1)S(1)}, bf16[64,2176]{1,0:T(8,128)(2,1)S(1)}, u32[]{:S(2)}, u32[]{:S(2)}) collective-permute-start(bf16[64,2176]{1,0:T(8,128)(2,1)S(1)} %collective-permute-done.1.refs_2_.refs_6_), channel_id=1, source_target_pairs={{0,4},{1,3},{2,6},{3,1},{4,0},{5,7},{6,2},{7,5},{8,12},{9,11},{10,... | collective-permute-start | bytes 835592 | tf_op jit(solution)/shard_map/ppermute | solution.py:165
  21.0 2.2 %collective-permute-done.refs_1_.refs_5_ = bf16[64,2176]{1,0:T(8,128)(2,1)S(1)} collective-permute-done((bf16[64,2176]{1,0:T(8,128)(2,1)S(1)}, bf16[64,2176]{1,0:T(8,128)(2,1)S(1)}, u32[]{:S(2)}, u32[]{:S(2)}) %collective-permute-start) | collective-permute-done | bytes 278560 | tf_op jit(solution)/shard_map/ppermute | solution.py:157
  23.2 2.3 %collective-permute-done.4.refs_6_.refs_10_ = bf16[64,2176]{1,0:T(8,128)(2,1)S(1)} collective-permute-done((bf16[64,2176]{1,0:T(8,128)(2,1)S(1)}, bf16[64,2176]{1,0:T(8,128)(2,1)S(1)}, u32[]{:S(2)}, u32[]{:S(2)}) %collective-permute-start.4) | collective-permute-done | bytes 278560 | tf_op jit(solution)/shard_map/ppermute | solution.py:165
  25.8 1.7 %collective-permute-start.9 = (bf16[64,2176]{1,0:T(8,128)(2,1)S(1)}, bf16[64,2176]{1,0:T(8,128)(2,1)S(1)}, u32[]{:S(2)}, u32[]{:S(2)}) collective-permute-start(bf16[64,2176]{1,0:T(8,128)(2,1)S(1)} %collective-permute-done.2.refs_4_.refs_8_), channel_id=1, source_target_pairs={{0,4},{1,3},{2,6},{3,1},{4,0},{5,7},{6,2},{7,5},{8,12},{9,11},{10,... | collective-permute-start | bytes 835592 | tf_op jit(solution)/shard_map/ppermute | solution.py:165
  29.9 4.4 %collective-permute-done.9.refs_4_.refs_16_.refs_12_ = bf16[64,2176]{1,0:T(8,128)(2,1)S(1)} collective-permute-done((bf16[64,2176]{1,0:T(8,128)(2,1)S(1)}, bf16[64,2176]{1,0:T(8,128)(2,1)S(1)}, u32[]{:S(2)}, u32[]{:S(2)}) %collective-permute-start.9) | collective-permute-done | bytes 278560 | tf_op jit(solution)/shard_map/ppermute | solution.py:165
  34.3 2.3 %collective-permute-done.6.refs_3_.refs_7_ = bf16[64,2176]{1,0:T(8,128)(2,1)S(1)} collective-permute-done((bf16[64,2176]{1,0:T(8,128)(2,1)S(1)}, bf16[64,2176]{1,0:T(8,128)(2,1)S(1)}, u32[]{:S(2)}, u32[]{:S(2)}) %collective-permute-start.6) | collective-permute-done | bytes 278560 | tf_op jit(solution)/shard_map/ppermute | solution.py:157
  38.9 1.7 %collective-permute-start.13 = (bf16[64,2176]{1,0:T(8,128)(2,1)S(1)}, bf16[64,2176]{1,0:T(8,128)(2,1)S(1)}, u32[]{:S(2)}, u32[]{:S(2)}) collective-permute-start(bf16[64,2176]{1,0:T(8,128)(2,1)S(1)} %collective-permute-done.4.refs_6_.refs_10_), channel_id=1, source_target_pairs={{0,4},{1,3},{2,6},{3,1},{4,0},{5,7},{6,2},{7,5},{8,12},{9,11},{10,... | collective-permute-start | bytes 835592 | tf_op jit(solution)/shard_map/ppermute | solution.py:165
  41.8 6.2 %collective-permute-done.13.refs_6_.refs_18_.refs_14_ = bf16[64,2176]{1,0:T(8,128)(2,1)S(1)} collective-permute-done((bf16[64,2176]{1,0:T(8,128)(2,1)S(1)}, bf16[64,2176]{1,0:T(8,128)(2,1)S(1)}, u32[]{:S(2)}, u32[]{:S(2)}) %collective-permute-start.13) | collective-permute-done | bytes 278560 | tf_op jit(solution)/shard_map/ppermute | solution.py:165
  48.1 2.1 %collective-permute-start.16 = (bf16[64,2176]{1,0:T(8,128)(2,1)S(1)}, bf16[64,2176]{1,0:T(8,128)(2,1)S(1)}, u32[]{:S(2)}, u32[]{:S(2)}) collective-permute-start(bf16[64,2176]{1,0:T(8,128)(2,1)S(1)} %collective-permute-done.7.refs_5_.refs_9_), channel_id=1, source_target_pairs={{0,4},{1,3},{2,6},{3,1},{4,0},{5,7},{6,2},{7,5},{8,12},{9,11},{10,... | collective-permute-start | bytes 835592 | tf_op jit(solution)/shard_map/ppermute | solution.py:165
  51.4 7.6 %shard_map.110 = (bf16[256,2048]{1,0:T(8,128)(2,1)}, bf16[256,768]{1,0:T(8,128)(2,1)}, bf16[256,768]{1,0:T(8,128)(2,1)}, bf16[256,768]{1,0:T(8,128)(2,1)}) custom-call(s32[2]{0:T(128)} %pad_add_fusion.where_ref, bf16[64,2176]{1,0:T(8,128)(2,1)} %copy-done, bf16[64,2176]{1,0:T(8,128)(2,1)} %copy-done.8, bf16[64,2176]{1,0:T(8,128)(2,1)} %copy-done.2, ...), custom_call_target="tpu_custom_call" | custom-call | flops 2415919104 | bytes 11665412 | tf_op jit(solution)/shard_map/pallas_call | solution.py:392
  59.9 7.6 %shard_map.111 = (bf16[256,2048]{1,0:T(8,128)(2,1)}, bf16[256,768]{1,0:T(8,128)(2,1)}, bf16[256,768]{1,0:T(8,128)(2,1)}, bf16[256,768]{1,0:T(8,128)(2,1)}) custom-call(s32[2]{0:T(128)} %pad_add_fusion.where_ref, bf16[64,2176]{1,0:T(8,128)(2,1)} %copy-done.6, bf16[64,2176]{1,0:T(8,128)(2,1)} %copy-done.20, bf16[64,2176]{1,0:T(8,128)(2,1)} %copy-done.12, ...), custom_call_target="tpu_custom_call" | custom-call | flops 2415919104 | bytes 11665412 | tf_op jit(solution)/shard_map/pallas_call | solution.py:392
  69.2 12.6 %shard_map.112 = (bf16[256,2048]{1,0:T(8,128)(2,1)}, bf16[256,2048]{1,0:T(8,128)(2,1)}, bf16[512,768]{1,0:T(8,128)(2,1)}, bf16[512,768]{1,0:T(8,128)(2,1)}, bf16[512,2048]{1,0:T(8,128)(2,1)}) custom-call(s32[2]{0:T(128)} %pad_add_fusion.where_ref, bf16[256,768]{1,0:T(8,128)(2,1)} %get-tuple-element.94.refs_0_, bf16[256,768]{1,0:T(8,128)(2,1)} %get-tuple-element.95.refs_1_, ...), custom_call_target="tpu_custom_call" | custom-call | flops 4831838208 | bytes 15466500 | tf_op jit(solution)/shard_map/pallas_call | solution.py:392
  90.0 2.0 %shard_map.113 = (bf16[512,2048]{1,0:T(8,128)(2,1)S(1)}, bf16[512,768]{1,0:T(8,128)(2,1)S(1)}) custom-call(bf16[64,2176]{1,0:T(8,128)(2,1)S(1)} %copy-done.1, bf16[64,2176]{1,0:T(8,128)(2,1)S(1)} %copy-done.9, bf16[64,2176]{1,0:T(8,128)(2,1)S(1)} %copy-done.3, bf16[64,2176]{1,0:T(8,128)(2,1)S(1)} %copy-done.17, bf16[64,2176]{1,0:T(8,128)(2,1)S(1)} %copy-done.5, ...), custom_call_target="tpu_custom_call" | custom-call | tf_op jit(solution)/shard_map/pallas_call | solution.py:469
  92.0 8.2 %collective-permute-done.20 = bf16[128,2048]{1,0:T(8,128)(2,1)} collective-permute-done((bf16[128,2048]{1,0:T(8,128)(2,1)}, bf16[128,2048]{1,0:T(8,128)(2,1)}, u32[]{:S(2)}, u32[]{:S(2)}) %collective-permute-start.20) | collective-permute-done | bytes 524320 | tf_op jit(solution)/shard_map/ppermute | solution.py:165
  108.7 2.6 %collective-permute-start.22 = (bf16[32,2048]{1,0:T(8,128)(2,1)S(1)}, bf16[32,2048]{1,0:T(8,128)(2,1)S(1)}, u32[]{:S(2)}, u32[]{:S(2)}) collective-permute-start(bf16[32,2048]{1,0:T(8,128)(2,1)S(1)} %get-tuple-element.130), channel_id=1, source_target_pairs={{0,16},{8,24},{16,0},{24,8},{1,17},{9,25},{17,1},{25,9},{2,18},{10... | collective-permute-start | bytes 393224 | tf_op jit(solution)/shard_map/ppermute | solution.py:157
  114.3 2.5 %collective-permute-start.24 = (bf16[32,2048]{1,0:T(8,128)(2,1)S(1)}, bf16[32,2048]{1,0:T(8,128)(2,1)S(1)}, u32[]{:S(2)}, u32[]{:S(2)}) collective-permute-start(bf16[32,2048]{1,0:T(8,128)(2,1)S(1)} %get-tuple-element.129), channel_id=1, source_target_pairs={{0,16},{8,24},{16,0},{24,8},{1,17},{9,25},{17,1},{25,9},{2,18},{10... | collective-permute-start | bytes 393224 | tf_op jit(solution)/shard_map/ppermute | solution.py:157
  118.2 2.2 %add_convert_fusion.2 = bf16[1024,768]{1,0:T(8,128)(2,1)} fusion(bf16[1024,768]{1,0:T(8,128)(2,1)S(1)} %collective-permute-done.25, bf16[512,768]{1,0:T(8,128)(2,1)S(1)} %copy-done.38, bf16[512,2048]{1,0:T(8,128)(2,1)S(1)} %get-tuple-element.116, s32[]{:T(128)S(6)} %select_n.19), kind=kOutput, calls=%fused_computation.2 | convolution fusion | flops 807665664 | bytes 4980740 | tf_op jit(solution)/shard_map/dot_general | solution.py:20
  120.4 2.2 %add_convert_fusion = bf16[384,2048]{1,0:T(8,128)(2,1)} fusion(bf16[384,2048]{1,0:T(8,128)(2,1)S(1)} %collective-permute-done.27, bf16[512,2048]{1,0:T(8,128)(2,1)S(1)} %copy-done.36, bf16[512,768]{1,0:T(8,128)(2,1)S(1)} %get-tuple-element.119, s32[]{:T(128)S(6)} %select_n.21), kind=kOutput, calls=%fused_computation | convolution fusion | flops 807665664 | bytes 5636100 | tf_op jit(solution)/shard_map/dot_general | solution.py:20
  122.6 2.2 %add_convert_fusion.1 = bf16[1024,768]{1,0:T(8,128)(2,1)} fusion(bf16[1024,768]{1,0:T(8,128)(2,1)S(1)} %collective-permute-done.26, bf16[512,768]{1,0:T(8,128)(2,1)S(1)} %copy-done.37, bf16[512,2048]{1,0:T(8,128)(2,1)S(1)} %get-tuple-element.116, s32[]{:T(128)S(6)} %select_n.19), kind=kOutput, calls=%fused_computation.1 | convolution fusion | flops 807665664 | bytes 4980740 | tf_op jit(solution)/shard_map/dot_general | solution.py:20
  124.8 2.4 %collective-permute-done.24 = bf16[32,2048]{1,0:T(8,128)(2,1)S(1)} collective-permute-done((bf16[32,2048]{1,0:T(8,128)(2,1)S(1)}, bf16[32,2048]{1,0:T(8,128)(2,1)S(1)}, u32[]{:S(2)}, u32[]{:S(2)}) %collective-permute-start.24) | collective-permute-done | bytes 131104 | tf_op jit(solution)/shard_map/ppermute | solution.py:157
  (142 shorter events, 37.3 us)
Async XLA Ops:
  2.6 13.0 %collective-permute-start.1 = (bf16[64,2176]{1,0:T(8,128)(2,1)S(1)}, bf16[64,2176]{1,0:T(8,128)(2,1)S(1)}, u32[]{:S(2)}, u32[]{:S(2)}) collective-permute-start(bf16[64,2176]{1,0:T(8,128)(2,1)S(1)} %pad_maximum_fusion.refs_0_.refs_4_), channel_id=1, source_target_pairs={{0,8},{8,0},{16,24},{24,16},{1,9},{9,1},{17,25},{25,17},{2,10},{10... | collective-permute-start | bytes 835592 | tf_op jit(solution)/shard_map/ppermute | solution.py:157
  5.7 9.9 %collective-permute-start.2 = (bf16[64,2176]{1,0:T(8,128)(2,1)S(1)}, bf16[64,2176]{1,0:T(8,128)(2,1)S(1)}, u32[]{:S(2)}, u32[]{:S(2)}) collective-permute-start(bf16[64,2176]{1,0:T(8,128)(2,1)S(1)} %pad_maximum_fusion.refs_0_.refs_4_), channel_id=1, source_target_pairs={{0,2},{1,5},{2,0},{3,7},{4,6},{5,1},{6,4},{7,3},{8,10},{9,13},{10,... | collective-permute-start | bytes 835592 | tf_op jit(solution)/shard_map/ppermute | solution.py:165
  8.7 14.5 %collective-permute-start = (bf16[64,2176]{1,0:T(8,128)(2,1)S(1)}, bf16[64,2176]{1,0:T(8,128)(2,1)S(1)}, u32[]{:S(2)}, u32[]{:S(2)}) collective-permute-start(bf16[64,2176]{1,0:T(8,128)(2,1)S(1)} %pad_maximum_fusion.refs_0_.refs_4_), channel_id=1, source_target_pairs={{0,16},{8,24},{16,0},{24,8},{1,17},{9,25},{17,1},{25,9},{2,18},{10... | collective-permute-start | bytes 835592 | tf_op jit(solution)/shard_map/ppermute | solution.py:157
  15.7 9.9 %collective-permute-start.4 = (bf16[64,2176]{1,0:T(8,128)(2,1)S(1)}, bf16[64,2176]{1,0:T(8,128)(2,1)S(1)}, u32[]{:S(2)}, u32[]{:S(2)}) collective-permute-start(bf16[64,2176]{1,0:T(8,128)(2,1)S(1)} %collective-permute-done.1.refs_2_.refs_6_), channel_id=1, source_target_pairs={{0,2},{1,5},{2,0},{3,7},{4,6},{5,1},{6,4},{7,3},{8,10},{9,13},{10,... | collective-permute-start | bytes 835592 | tf_op jit(solution)/shard_map/ppermute | solution.py:165
  25.5 12.8 %collective-permute-start.10 = (bf16[1024,768]{1,0:T(8,128)(2,1)}, bf16[1024,768]{1,0:T(8,128)(2,1)S(1)}, u32[]{:S(2)}, u32[]{:S(2)}) collective-permute-start(bf16[1024,768]{1,0:T(8,128)(2,1)} %bitcast.18), channel_id=1, source_target_pairs={{0,1},{1,0},{2,3},{3,2},{4,5},{5,4},{6,7},{7,6},{8,9},{9,8},{10,11... | collective-permute-start | bytes 4718600 | tf_op jit(solution)/shard_map/ppermute | solution.py:16
  27.5 9.1 %collective-permute-start.6 = (bf16[64,2176]{1,0:T(8,128)(2,1)S(1)}, bf16[64,2176]{1,0:T(8,128)(2,1)S(1)}, u32[]{:S(2)}, u32[]{:S(2)}) collective-permute-start(bf16[64,2176]{1,0:T(8,128)(2,1)S(1)} %collective-permute-done.refs_1_.refs_5_), channel_id=1, source_target_pairs={{0,8},{8,0},{16,24},{24,16},{1,9},{9,1},{17,25},{25,17},{2,10},{10... | collective-permute-start | bytes 835592 | tf_op jit(solution)/shard_map/ppermute | solution.py:157
  27.5 9.6 %collective-permute-start.7 = (bf16[64,2176]{1,0:T(8,128)(2,1)S(1)}, bf16[64,2176]{1,0:T(8,128)(2,1)S(1)}, u32[]{:S(2)}, u32[]{:S(2)}) collective-permute-start(bf16[64,2176]{1,0:T(8,128)(2,1)S(1)} %collective-permute-done.refs_1_.refs_5_), channel_id=1, source_target_pairs={{0,2},{1,5},{2,0},{3,7},{4,6},{5,1},{6,4},{7,3},{8,10},{9,13},{10,... | collective-permute-start | bytes 835592 | tf_op jit(solution)/shard_map/ppermute | solution.py:165
  28.7 9.6 %collective-permute-start.8 = (bf16[64,2176]{1,0:T(8,128)(2,1)S(1)}, bf16[64,2176]{1,0:T(8,128)(2,1)S(1)}, u32[]{:S(2)}, u32[]{:S(2)}) collective-permute-start(bf16[64,2176]{1,0:T(8,128)(2,1)S(1)} %collective-permute-done.refs_1_.refs_5_), channel_id=1, source_target_pairs={{0,4},{1,3},{2,6},{3,1},{4,0},{5,7},{6,2},{7,5},{8,12},{9,11},{10,... | collective-permute-start | bytes 835592 | tf_op jit(solution)/shard_map/ppermute | solution.py:165
  38.3 11.8 %collective-permute-start.14 = (bf16[384,2048]{1,0:T(8,128)(2,1)}, bf16[384,2048]{1,0:T(8,128)(2,1)}, u32[]{:S(2)}, u32[]{:S(2)}) collective-permute-start(bf16[384,2048]{1,0:T(8,128)(2,1)} %bitcast.22), channel_id=1, source_target_pairs={{0,1},{1,0},{2,3},{3,2},{4,5},{5,4},{6,7},{7,6},{8,9},{9,8},{10,11... | collective-permute-start | bytes 4718600 | tf_op jit(solution)/shard_map/ppermute | solution.py:16
  38.4 12.9 %collective-permute-start.15 = (bf16[1024,768]{1,0:T(8,128)(2,1)}, bf16[1024,768]{1,0:T(8,128)(2,1)}, u32[]{:S(2)}, u32[]{:S(2)}) collective-permute-start(bf16[1024,768]{1,0:T(8,128)(2,1)} %bitcast.14), channel_id=1, source_target_pairs={{0,1},{1,0},{2,3},{3,2},{4,5},{5,4},{6,7},{7,6},{8,9},{9,8},{10,11... | collective-permute-start | bytes 4718600 | tf_op jit(solution)/shard_map/ppermute | solution.py:16
  38.9 9.2 %collective-permute-start.13 = (bf16[64,2176]{1,0:T(8,128)(2,1)S(1)}, bf16[64,2176]{1,0:T(8,128)(2,1)S(1)}, u32[]{:S(2)}, u32[]{:S(2)}) collective-permute-start(bf16[64,2176]{1,0:T(8,128)(2,1)S(1)} %collective-permute-done.4.refs_6_.refs_10_), channel_id=1, source_target_pairs={{0,4},{1,3},{2,6},{3,1},{4,0},{5,7},{6,2},{7,5},{8,12},{9,11},{10,... | collective-permute-start | bytes 835592 | tf_op jit(solution)/shard_map/ppermute | solution.py:165
  40.6 9.5 %collective-permute-start.11 = (bf16[64,2176]{1,0:T(8,128)(2,1)S(1)}, bf16[64,2176]{1,0:T(8,128)(2,1)}, u32[]{:S(2)}, u32[]{:S(2)}) collective-permute-start(bf16[64,2176]{1,0:T(8,128)(2,1)S(1)} %collective-permute-done.6.refs_3_.refs_7_), channel_id=1, source_target_pairs={{0,2},{1,5},{2,0},{3,7},{4,6},{5,1},{6,4},{7,3},{8,10},{9,13},{10,... | collective-permute-start | bytes 835592 | tf_op jit(solution)/shard_map/ppermute | solution.py:165
  48.1 11.0 %collective-permute-start.16 = (bf16[64,2176]{1,0:T(8,128)(2,1)S(1)}, bf16[64,2176]{1,0:T(8,128)(2,1)S(1)}, u32[]{:S(2)}, u32[]{:S(2)}) collective-permute-start(bf16[64,2176]{1,0:T(8,128)(2,1)S(1)} %collective-permute-done.7.refs_5_.refs_9_), channel_id=1, source_target_pairs={{0,4},{1,3},{2,6},{3,1},{4,0},{5,7},{6,2},{7,5},{8,12},{9,11},{10,... | collective-permute-start | bytes 835592 | tf_op jit(solution)/shard_map/ppermute | solution.py:165
  50.2 8.9 %collective-permute-start.17 = (bf16[64,2176]{1,0:T(8,128)(2,1)}, bf16[64,2176]{1,0:T(8,128)(2,1)S(1)}, u32[]{:S(2)}, u32[]{:S(2)}) collective-permute-start(bf16[64,2176]{1,0:T(8,128)(2,1)} %collective-permute-done.11.refs_7_.refs_11_), channel_id=1, source_target_pairs={{0,4},{1,3},{2,6},{3,1},{4,0},{5,7},{6,2},{7,5},{8,12},{9,11},{10,... | collective-permute-start | bytes 835592 | tf_op jit(solution)/shard_map/ppermute | solution.py:165
  67.5 15.1 %collective-permute-start.18 = (bf16[256,2048]{1,0:T(8,128)(2,1)}, bf16[256,2048]{1,0:T(8,128)(2,1)S(1)}, u32[]{:S(2)}, u32[]{:S(2)}) collective-permute-start(bf16[256,2048]{1,0:T(8,128)(2,1)} %get-tuple-element.93), channel_id=1, source_target_pairs={{0,4},{1,3},{2,6},{3,1},{4,0},{5,7},{6,2},{7,5},{8,12},{9,11},{10,... | collective-permute-start | bytes 3145736 | tf_op jit(solution)/shard_map/ppermute | solution.py:165
  82.6 19.3 %collective-permute-start.19 = (bf16[256,2048]{1,0:T(8,128)(2,1)}, bf16[256,2048]{1,0:T(8,128)(2,1)}, u32[]{:S(2)}, u32[]{:S(2)}) collective-permute-start(bf16[256,2048]{1,0:T(8,128)(2,1)} %get-tuple-element.103), channel_id=1, source_target_pairs={{0,4},{1,3},{2,6},{3,1},{4,0},{5,7},{6,2},{7,5},{8,12},{9,11},{10,... | collective-permute-start | bytes 3145736 | tf_op jit(solution)/shard_map/ppermute | solution.py:165
  85.1 15.1 %collective-permute-start.20 = (bf16[128,2048]{1,0:T(8,128)(2,1)}, bf16[128,2048]{1,0:T(8,128)(2,1)}, u32[]{:S(2)}, u32[]{:S(2)}) collective-permute-start(bf16[128,2048]{1,0:T(8,128)(2,1)} %add_convert_fusion.6), channel_id=1, source_target_pairs={{0,2},{1,5},{2,0},{3,7},{4,6},{5,1},{6,4},{7,3},{8,10},{9,13},{10,... | collective-permute-start | bytes 1572872 | tf_op jit(solution)/shard_map/ppermute | solution.py:165
  103.7 9.2 %collective-permute-start.23 = (bf16[128,2048]{1,0:T(8,128)(2,1)S(1)}, bf16[128,2048]{1,0:T(8,128)(2,1)S(1)}, u32[]{:S(2)}, u32[]{:S(2)}) collective-permute-start(bf16[128,2048]{1,0:T(8,128)(2,1)S(1)} %add_convert_fusion.4), channel_id=1, source_target_pairs={{0,2},{1,5},{2,0},{3,7},{4,6},{5,1},{6,4},{7,3},{8,10},{9,13},{10,... | collective-permute-start | bytes 1572872 | tf_op jit(solution)/shard_map/ppermute | solution.py:165
  105.7 11.2 %collective-permute-start.25 = (bf16[1024,768]{1,0:T(8,128)(2,1)S(1)}, bf16[1024,768]{1,0:T(8,128)(2,1)S(1)}, u32[]{:S(2)}, u32[]{:S(2)}) collective-permute-start(bf16[1024,768]{1,0:T(8,128)(2,1)S(1)} %convolution_convert_fusion.2), channel_id=1, source_target_pairs={{0,1},{1,0},{2,3},{3,2},{4,5},{5,4},{6,7},{7,6},{8,9},{9,8},{10,11... | collective-permute-start | bytes 4718600 | tf_op jit(solution)/shard_map/ppermute | solution.py:16
  106.8 15.8 %collective-permute-start.26 = (bf16[1024,768]{1,0:T(8,128)(2,1)S(1)}, bf16[1024,768]{1,0:T(8,128)(2,1)S(1)}, u32[]{:S(2)}, u32[]{:S(2)}) collective-permute-start(bf16[1024,768]{1,0:T(8,128)(2,1)S(1)} %convolution_convert_fusion.1), channel_id=1, source_target_pairs={{0,1},{1,0},{2,3},{3,2},{4,5},{5,4},{6,7},{7,6},{8,9},{9,8},{10,11... | collective-permute-start | bytes 4718600 | tf_op jit(solution)/shard_map/ppermute | solution.py:16
  108.4 12.0 %collective-permute-start.27 = (bf16[384,2048]{1,0:T(8,128)(2,1)S(1)}, bf16[384,2048]{1,0:T(8,128)(2,1)S(1)}, u32[]{:S(2)}, u32[]{:S(2)}) collective-permute-start(bf16[384,2048]{1,0:T(8,128)(2,1)S(1)} %convolution_convert_fusion), channel_id=1, source_target_pairs={{0,1},{1,0},{2,3},{3,2},{4,5},{5,4},{6,7},{7,6},{8,9},{9,8},{10,11... | collective-permute-start | bytes 4718600 | tf_op jit(solution)/shard_map/ppermute | solution.py:16
  108.7 16.1 %collective-permute-start.22 = (bf16[32,2048]{1,0:T(8,128)(2,1)S(1)}, bf16[32,2048]{1,0:T(8,128)(2,1)S(1)}, u32[]{:S(2)}, u32[]{:S(2)}) collective-permute-start(bf16[32,2048]{1,0:T(8,128)(2,1)S(1)} %get-tuple-element.130), channel_id=1, source_target_pairs={{0,16},{8,24},{16,0},{24,8},{1,17},{9,25},{17,1},{25,9},{2,18},{10... | collective-permute-start | bytes 393224 | tf_op jit(solution)/shard_map/ppermute | solution.py:157
  114.3 12.9 %collective-permute-start.24 = (bf16[32,2048]{1,0:T(8,128)(2,1)S(1)}, bf16[32,2048]{1,0:T(8,128)(2,1)S(1)}, u32[]{:S(2)}, u32[]{:S(2)}) collective-permute-start(bf16[32,2048]{1,0:T(8,128)(2,1)S(1)} %get-tuple-element.129), channel_id=1, source_target_pairs={{0,16},{8,24},{16,0},{24,8},{1,17},{9,25},{17,1},{25,9},{2,18},{10... | collective-permute-start | bytes 393224 | tf_op jit(solution)/shard_map/ppermute | solution.py:157
  116.8 11.1 %collective-permute-start.29 = (bf16[32,2048]{1,0:T(8,128)(2,1)S(1)}, bf16[32,2048]{1,0:T(8,128)(2,1)S(1)}, u32[]{:S(2)}, u32[]{:S(2)}) collective-permute-start(bf16[32,2048]{1,0:T(8,128)(2,1)S(1)} %get-tuple-element.128), channel_id=1, source_target_pairs={{0,24},{8,16},{16,8},{24,0},{1,25},{9,17},{17,9},{25,1},{2,26},{10... | collective-permute-start | bytes 393224 | tf_op jit(solution)/shard_map/ppermute | solution.py:157
  (45 other events, 657.8 us)

commit v6 on v5

--- a/solution.py
+++ b/solution.py
@@ -147,8 +147,9 @@
 
 FIRST, SECOND = (1, 2), (2, 1)
 tie = lax.optimization_barrier
-VMEM_LIMIT = 56 * 2**20
+VMEM_LIMIT = 32 * 2**20
 ANY = pl.BlockSpec(memory_space=pl.ANY)
+VMEM = pl.BlockSpec(memory_space=pltpu.VMEM)
 SMEM = pl.BlockSpec(memory_space=pltpu.SMEM)
 
 
@@ -319,24 +320,29 @@
     wait_all(start_out([(whole, whole_out), (hidden, hidden_out)], out_sems, 0))
 
 
+def weights_kernel(where_ref, *refs):
+    wholes, where_out, sems = refs[6:9], refs[9], refs[10]
+    copies = []
+    for k, whole in enumerate(wholes):
+        copies += start_halves(refs[2 * k : 2 * k + 2], whole, sems, 2 * k, where_ref[0])
+    for k in range(where_out.shape[0]):
+        where_out[k] = where_ref[k]
+    wait_all(copies)
+
+
 def forward_kernel(rows, count, expert_count, where_ref, *refs):
     pieces, refs = refs[:count], refs[count:]
-    gate, up, down = refs[0:2], refs[2:4], refs[4:6]
-    whole_out, gate_pre_out, up_pre_out, hidden_out = refs[6:10]
-    rows_in, side, gate_all, up_all, down_all, gate_pre, up_pre, hidden, out = refs[10:19]
-    row_sems, side_sems, weight_sems, out_sems = refs[19:]
+    gate_all, up_all, down_all = refs[0:3]
+    whole_out, gate_pre_out, up_pre_out, hidden_out = refs[3:7]
+    rows_in, side, gate_pre, up_pre, hidden, out = refs[7:13]
+    row_sems, side_sems, out_sems = refs[13:]
     width = rows_in.shape[1]
     row_copies = start_rows(pieces, rows_in, 0, rows, 0, row_sems)
-    gate_copies = start_halves(gate, gate_all, weight_sems, 0, where_ref[0])
+    side_copies = start_rows(pieces, side, 0, rows, width, side_sems)
     wait_all(row_copies)
-    up_copies = start_halves(up, up_all, weight_sems, 2, where_ref[0])
-    wait_all(gate_copies)
-    side_copies = start_rows(pieces, side, 0, rows, width, side_sems)
-    down_copies = start_halves(down, down_all, weight_sems, 4, where_ref[0])
     pre = jnp.dot(rows_in[...], gate_all[...], preferred_element_type=jnp.float32)
     gate_pre[...] = pre.astype(gate_pre.dtype)
     act = pre * jax.nn.sigmoid(pre)
-    wait_all(up_copies)
     pre = jnp.dot(rows_in[...], up_all[...], preferred_element_type=jnp.float32)
     up_pre[...] = pre.astype(up_pre.dtype)
     hidden[...] = (act * pre).astype(jnp.bfloat16)
@@ -345,7 +351,6 @@
     )
     wait_all(side_copies)
     probs = weights_of(side, where_ref[1], expert_count)
-    wait_all(down_copies)
     for t, cols in enumerate(tiles(width, 2)):
         part = jnp.dot(hidden[...], down_all[:, cols], preferred_element_type=jnp.float32)
         out[:, cols] = (part * probs).astype(jnp.bfloat16)
@@ -356,23 +361,19 @@
 def backward_kernel(rows, count, where_ref, *refs):
     gate_pre_in, up_pre_in, refs = refs[0:2], refs[2:4], refs[4:]
     pieces, refs = refs[:count], refs[count:]
-    gate, up, down = refs[0:2], refs[2:4], refs[4:6]
-    keep, send, dgate_out, dup_out, scaled_out = refs[6:11]
-    scaled, side, gate_all, up_all, down_all, gate_pre, up_pre, dgate, dup, grad = refs[11:21]
-    row_sems, side_sems, weight_sems, pre_sems, out_sems = refs[21:]
+    gate_all, up_all, down_all = refs[0:3]
+    keep, send, dgate_out, dup_out, scaled_out = refs[3:8]
+    scaled, side, gate_pre, up_pre, dgate, dup, grad = refs[8:15]
+    row_sems, side_sems, pre_sems, out_sems = refs[15:]
     width = scaled.shape[1]
     row_copies = start_rows(pieces, scaled, rows, rows, 0, row_sems)
     side_copies = start_rows(pieces, side, 0, rows, width, side_sems)
-    down_copies = start_halves(down, down_all, weight_sems, 4, where_ref[0])
     pre_copies = start_parts(gate_pre_in, gate_pre, pre_sems, 0)
     pre_copies += start_parts(up_pre_in, up_pre, pre_sems, 2)
     wait_all(row_copies + side_copies)
-    gate_copies = start_halves(gate, gate_all, weight_sems, 0, where_ref[0])
-    up_copies = start_halves(up, up_all, weight_sems, 2, where_ref[0])
     probs = weights_of(side, where_ref[1], count)
     scaled[...] = (scaled[...].astype(jnp.float32) * probs).astype(jnp.bfloat16)
     outs = start_out([(scaled, scaled_out)], out_sems, 0)
-    wait_all(down_copies)
     dhidden = contract_cols(scaled[...], down_all[...])
     wait_all(pre_copies)
     pre, gain = gate_pre[...].astype(jnp.float32), up_pre[...].astype(jnp.float32)
@@ -380,7 +381,6 @@
     dgate[...] = (dhidden * gain * sigma * (1.0 + pre * (1.0 - sigma))).astype(jnp.bfloat16)
     dup[...] = (dhidden * (pre * sigma)).astype(jnp.bfloat16)
     outs += start_out([(dgate, dgate_out), (dup, dup_out)], out_sems, 1)
-    wait_all(gate_copies + up_copies)
     for t, cols in enumerate(tiles(width, 2)):
         part = contract_cols(dgate[...], gate_all[cols, :])
         grad[:, cols] = (part + contract_cols(dup[...], up_all[cols, :])).astype(jnp.bfloat16)
@@ -388,11 +388,15 @@
     wait_all(outs)
 
 
+def in_hbm(values):
+    return [pltpu.with_memory_space_constraint(value, pltpu.HBM) for value in values]
+
+
 def expert_call(kernel, outs, scratch, sems, flops, inputs):
     return pl.pallas_call(
         kernel,
-        out_shape=[jax.ShapeDtypeStruct(shape, dtype) for shape, dtype in outs],
-        in_specs=[SMEM] + [ANY] * (len(inputs) - 1),
+        out_shape=[pltpu.HBM(shape, dtype) for shape, dtype in outs],
+        in_specs=[SMEM] + [ANY] * (len(inputs) - 4) + [VMEM] * 3,
         out_specs=[ANY] * len(outs),
         scratch_shapes=[pltpu.VMEM(shape, dtype) for shape, dtype in scratch]
         + [pltpu.SemaphoreType.DMA((n,)) for n in sems],
@@ -402,24 +406,40 @@
             bytes_accessed=sum(2 * value.size for value in inputs),
             transcendentals=0,
         ),
-    )(*inputs)
-
-
-class PartnerWeights:
-    def __init__(self, own):
-        self.own, self.came = list(own), []
+    )(inputs[0], *in_hbm(inputs[1:-3]), *inputs[-3:])
+
+
+class WholeWeights:
+    def __init__(self, own, where):
+        self.own, self.where, self.came, self.whole = list(own), where, [], None
+
+    def load(self):
+        width, hidden_width = 2 * self.own[0].shape[0], self.own[0].shape[1]
+        shapes = [(width, hidden_width), (width, hidden_width), (hidden_width, width)]
+        halves = [value for pair in zip(self.own, self.came) for value in pair]
+        *self.whole, self.where = pl.pallas_call(
+            weights_kernel,
+            out_shape=[pltpu.VMEM(shape, jnp.bfloat16) for shape in shapes]
+            + [jax.ShapeDtypeStruct(self.where.shape, self.where.dtype)],
+            in_specs=[SMEM] + [ANY] * 6,
+            out_specs=[VMEM] * 3 + [SMEM],
+            scratch_shapes=[pltpu.SemaphoreType.DMA((6,))],
+            compiler_params=pltpu.CompilerParams(vmem_limit_bytes=VMEM_LIMIT),
+        )(self.where, *in_hbm(halves))
+        self.whole = [pltpu.with_memory_space_constraint(w, pltpu.VMEM) for w in self.whole]
 
     def __call__(self, step, values):
         if not values:
             return values
-        k = len(self.came)
-        old, new = self.came[k - 1 :] if k > 1 else [], self.own[k : k + 1]
-        values = list(tie((*values, *old, *new)))
-        if new:
-            self.came.append(partner_2(values.pop(), "rep", 0))
-        if old:
-            self.came[k - 1] = values.pop()
-        return values
+        count = len(values)
+        if step <= 2:
+            new = self.own[:1] if step == 1 else self.own[1:]
+            values = list(tie((*values, *new)))
+            self.came += [partner_2(value, "rep", 0) for value in values[count:]]
+        elif self.whole is None:
+            self.load()
+            *values, self.where = tie((*values, self.where))
+        return values[:count]
 
 
 def dense_local(tokens, cotangent, expert_ids, gate_probs, gate_weight, up_weight, down_weight):
@@ -430,22 +450,18 @@
     half_hidden = down_weight.shape[1]
     total = expert_count * rows
     own = (gate_weight[0], up_weight[0], down_weight[0])
-    partner = PartnerWeights(own)
-    block = token_block(tokens, cotangent, expert_ids, gate_probs, expert_count)
-    pieces = gather_blocks(block, partner)
-    partner = partner.came
-    weights = [value for pair in zip(own, partner) for value in pair]
     expert = lax.axis_index("grp") * lax.axis_size("exp") + lax.axis_index("exp")
     where = jnp.stack([replica, expert]).astype(jnp.int32)
+    block = token_block(tokens, cotangent, expert_ids, gate_probs, expert_count)
+    collected = WholeWeights(own, where)
+    pieces = gather_blocks(block, collected)
+    if collected.whole is None:
+        collected.load()
+    weights, where = collected.whole, collected.where
     bf16 = jnp.bfloat16
     wide, narrow = ((total, width), bf16), ((total, hidden_width), bf16)
     half_wide = ((total // 2, width), bf16)
     half_narrow = ((total // 2, hidden_width), bf16)
-    mats = [
-        ((width, hidden_width), bf16),
-        ((width, hidden_width), bf16),
-        ((hidden_width, width), bf16),
-    ]
     side = side_width(expert_count)
     flops = 6 * total * width * hidden_width
     half_count = expert_count // 2
@@ -455,8 +471,8 @@
             list(expert_call(
                 functools.partial(forward_kernel, rows, half_count, expert_count),
                 [half_wide] + [half_narrow] * 3,
-                [half_wide, ((total // 2, side), bf16), *mats] + [half_narrow] * 3 + [half_wide],
-                [half_count, half_count, 6, 5],
+                [half_wide, ((total // 2, side), bf16)] + [half_narrow] * 3 + [half_wide],
+                [half_count, half_count, 5],
                 flops // 2,
                 [where, *(half_pieces or waiting), *weights],
             ))
@@ -464,7 +480,7 @@
         if half_pieces:
             forward[0][0], waiting = tie((forward[0][0], waiting))
     (out_keep, out_send), gate_pre, up_pre, hidden = zip(*forward)
-    held = [wide, ((total, side), bf16), *mats, narrow, narrow]
+    held = [wide, ((total, side), bf16), narrow, narrow]
     out_came = swap_inner(out_send, SECOND)
     rows_in, hidden = pl.pallas_call(
         functools.partial(assemble_kernel, rows, expert_count),
@@ -479,12 +495,12 @@
             pltpu.SemaphoreType.DMA((2,)),
         ],
         compiler_params=pltpu.CompilerParams(vmem_limit_bytes=VMEM_LIMIT // 4),
-    )(*pieces, *hidden)
+    )(*in_hbm(pieces), *in_hbm(hidden))
     grad_keep, grad_send, dgate, dup, rows_scaled = expert_call(
         functools.partial(backward_kernel, rows, expert_count),
         [half_wide, half_wide, narrow, narrow, wide],
         held + [narrow, narrow, wide],
-        [expert_count, expert_count, 6, 4, 7],
+        [expert_count, expert_count, 4, 7],
         flops,
         [where, *gate_pre, *up_pre, *pieces, *weights],
     )

time: 129 us -> 123 us (0.953)
  local copies, waits for them, and re-layouts: 5.04 us -> 1.23 us
  other arithmetic: 8.52 us -> 5.92 us
  waiting for transfers between devices: 37.5 us -> 39.1 us
  Pallas kernels: 29.8 us -> 28.4 us
    unnamed x78 -> x36, local copies, waits for them, and re-layouts: 4.82 us -> 1.01 us
    convert_element_type x5, other arithmetic: 4.71 us -> 2.63 us  [add_bf16(): (left.astype(jnp.float32) + right.astype(jnp.float32)).astype(jnp.bfloat16)]
    ppermute x15, waiting for transfers between devices: 25.8 us -> 27.5 us  [swap_inner(): return lax.ppermute(value, ('exp', 'rep'), pairs)]
    pallas_call x3 -> x4, Pallas kernels: 27.8 us -> 26.2 us  [the longest x3 21.2 us: expert_call(): pl.pallas_call(kernel, out_shape=[pltpu.HBM(shape, dtype) for shape, dtyp...]
  transfers between devices with their start and end apart: 30 -> 30, of which waited for: 15 -> 13; matrix products, arithmetic and copies ran while one was open for 12% -> 11% of each run, Pallas kernels for 17% -> 18%
where the time goes in v6:
time: 123 us
  waiting for transfers between devices  39.1 us (32%)
  starting transfers between devices  37.6 us (31%)
  Pallas kernels  28.4 us (23%)
  matrix products  9.67 us (8%)
  other arithmetic  5.92 us (5%)
  local copies, waits for them, and re-layouts  1.23 us (1%)
    ppermute x15, waiting for transfers between devices, swap_inner(): return lax.ppermute(value, ('exp', 'rep'), pairs)  27.5 us
    ppermute x15, starting transfers between devices, swap_inner(): return lax.ppermute(value, ('exp', 'rep'), pairs)  24 us
    pallas_call x3, Pallas kernels, expert_call(): pl.pallas_call(kernel, out_shape=[pltpu.HBM(shape, dtype) for shape, dtyp...  21.2 us
    ppermute x9, starting transfers between devices, swap_group(): return lax.ppermute(value, 'grp', [(i, i ^ mask) for i in range(count)])  12.4 us
    ppermute x9, waiting for transfers between devices, swap_group(): return lax.ppermute(value, 'grp', [(i, i ^ mask) for i in range(count)])  11.6 us
    dot_general x6, matrix products, contract_rows(): lax.dot_general(left, right, (((0,), (0,)), ((), ())), preferred_element_...  9.67 us
    pallas_call x1, Pallas kernels, load(): pl.pallas_call(weights_kernel, out_shape=[pltpu.VMEM(shape, jnp.bfloat16)...  4.93 us
    convert_element_type x5, other arithmetic, add_bf16(): (left.astype(jnp.float32) + right.astype(jnp.float32)).astype(jnp.bfloat16)  2.63 us
  transfers between devices with their start and end apart: 30, of which 13 were waited for; matrix products, arithmetic and copies ran while one was open for 11% of the time, Pallas kernels for 18%

profile of v6, /device:TPU:0, one launch (start us, length us, event | category | flops | bytes accessed | tf_op | source)
XLA Modules:
  0.0 122.8 jit_solution(6670561954272183915)
XLA Ops:
  2.6 3.1 %collective-permute-start.1 = (bf16[64,2176]{1,0:T(8,128)(2,1)S(1)}, bf16[64,2176]{1,0:T(8,128)(2,1)S(1)}, u32[]{:S(2)}, u32[]{:S(2)}) collective-permute-start(bf16[64,2176]{1,0:T(8,128)(2,1)S(1)} %pad_maximum_fusion.refs_0_.refs_4_), channel_id=1, source_target_pairs={{0,8},{8,0},{16,24},{24,16},{1,9},{9,1},{17,25},{25,17},{2,10},{10... | collective-permute-start | bytes 835592 | tf_op jit(solution)/shard_map/ppermute | solution.py:158
  8.7 2.6 %collective-permute-start = (bf16[64,2176]{1,0:T(8,128)(2,1)S(1)}, bf16[64,2176]{1,0:T(8,128)(2,1)}, u32[]{:S(2)}, u32[]{:S(2)}) collective-permute-start(bf16[64,2176]{1,0:T(8,128)(2,1)S(1)} %pad_maximum_fusion.refs_0_.refs_4_), channel_id=1, source_target_pairs={{0,16},{8,24},{16,0},{24,8},{1,17},{9,25},{17,1},{25,9},{2,18},{10... | collective-permute-start | bytes 835592 | tf_op jit(solution)/shard_map/ppermute | solution.py:158
  11.3 4.3 %collective-permute-done.1.refs_2_.refs_6_ = bf16[64,2176]{1,0:T(8,128)(2,1)S(1)} collective-permute-done((bf16[64,2176]{1,0:T(8,128)(2,1)S(1)}, bf16[64,2176]{1,0:T(8,128)(2,1)S(1)}, u32[]{:S(2)}, u32[]{:S(2)}) %collective-permute-start.1) | collective-permute-done | bytes 278560 | tf_op jit(solution)/shard_map/ppermute | solution.py:158
  15.6 2.8 %collective-permute-start.4 = (bf16[64,2176]{1,0:T(8,128)(2,1)S(1)}, bf16[64,2176]{1,0:T(8,128)(2,1)S(1)}, u32[]{:S(2)}, u32[]{:S(2)}) collective-permute-start(bf16[64,2176]{1,0:T(8,128)(2,1)S(1)} %collective-permute-done.1.refs_2_.refs_6_), channel_id=1, source_target_pairs={{0,2},{1,5},{2,0},{3,7},{4,6},{5,1},{6,4},{7,3},{8,10},{9,13},{10,... | collective-permute-start | bytes 835592 | tf_op jit(solution)/shard_map/ppermute | solution.py:166
  18.5 2.5 %collective-permute-start.5 = (bf16[64,2176]{1,0:T(8,128)(2,1)S(1)}, bf16[64,2176]{1,0:T(8,128)(2,1)S(1)}, u32[]{:S(2)}, u32[]{:S(2)}) collective-permute-start(bf16[64,2176]{1,0:T(8,128)(2,1)S(1)} %collective-permute-done.1.refs_2_.refs_6_), channel_id=1, source_target_pairs={{0,4},{1,3},{2,6},{3,1},{4,0},{5,7},{6,2},{7,5},{8,12},{9,11},{10,... | collective-permute-start | bytes 835592 | tf_op jit(solution)/shard_map/ppermute | solution.py:166
  21.0 2.3 %collective-permute-done.refs_1_.refs_5_ = bf16[64,2176]{1,0:T(8,128)(2,1)} collective-permute-done((bf16[64,2176]{1,0:T(8,128)(2,1)S(1)}, bf16[64,2176]{1,0:T(8,128)(2,1)}, u32[]{:S(2)}, u32[]{:S(2)}) %collective-permute-start) | collective-permute-done | bytes 278560 | tf_op jit(solution)/shard_map/ppermute | solution.py:158
  23.3 2.1 %collective-permute-done.4.refs_6_.refs_10_ = bf16[64,2176]{1,0:T(8,128)(2,1)S(1)} collective-permute-done((bf16[64,2176]{1,0:T(8,128)(2,1)S(1)}, bf16[64,2176]{1,0:T(8,128)(2,1)S(1)}, u32[]{:S(2)}, u32[]{:S(2)}) %collective-permute-start.4) | collective-permute-done | bytes 278560 | tf_op jit(solution)/shard_map/ppermute | solution.py:166
  26.0 2.0 %collective-permute-start.9 = (bf16[64,2176]{1,0:T(8,128)(2,1)}, bf16[64,2176]{1,0:T(8,128)(2,1)}, u32[]{:S(2)}, u32[]{:S(2)}) collective-permute-start(bf16[64,2176]{1,0:T(8,128)(2,1)} %collective-permute-done.2.refs_4_.refs_8_), channel_id=1, source_target_pairs={{0,4},{1,3},{2,6},{3,1},{4,0},{5,7},{6,2},{7,5},{8,12},{9,11},{10,... | collective-permute-start | bytes 835592 | tf_op jit(solution)/shard_map/ppermute | solution.py:166
  29.4 4.0 %collective-permute-start.8 = (bf16[64,2176]{1,0:T(8,128)(2,1)}, bf16[64,2176]{1,0:T(8,128)(2,1)}, u32[]{:S(2)}, u32[]{:S(2)}) collective-permute-start(bf16[64,2176]{1,0:T(8,128)(2,1)} %collective-permute-done.refs_1_.refs_5_), channel_id=1, source_target_pairs={{0,4},{1,3},{2,6},{3,1},{4,0},{5,7},{6,2},{7,5},{8,12},{9,11},{10,... | collective-permute-start | bytes 835592 | tf_op jit(solution)/shard_map/ppermute | solution.py:166
  33.5 4.9 %shard_map.110 = (bf16[2048,768]{1,0:T(8,128)(2,1)S(1)}, bf16[2048,768]{1,0:T(8,128)(2,1)S(1)}, bf16[768,2048]{1,0:T(8,128)(2,1)S(1)}, s32[2]{0:T(128)S(1)}) custom-call(s32[2]{0:T(128)S(1)} %pad_add_fusion.where_ref, bf16[1024,768]{1,0:T(8,128)(2,1)} %bitcast.15, bf16[1024,768]{1,0:T(8,128)(2,1)} %copy-done.1, bf16[1024,768]{1,0:T(8,128)(2,1)} %bitcast.17, ...), custom_call_target="tpu_custom_call" | custom-call | tf_op jit(solution)/shard_map/pallas_call | solution.py:420
  42.9 5.7 %collective-permute-done.13.refs_7_.refs_11_ = bf16[64,2176]{1,0:T(8,128)(2,1)S(1)} collective-permute-done((bf16[64,2176]{1,0:T(8,128)(2,1)}, bf16[64,2176]{1,0:T(8,128)(2,1)S(1)}, u32[]{:S(2)}, u32[]{:S(2)}) %collective-permute-start.13) | collective-permute-done | bytes 278560 | tf_op jit(solution)/shard_map/ppermute | solution.py:166
  48.6 2.1 %collective-permute-start.17 = (bf16[64,2176]{1,0:T(8,128)(2,1)S(1)}, bf16[64,2176]{1,0:T(8,128)(2,1)S(1)}, u32[]{:S(2)}, u32[]{:S(2)}) collective-permute-start(bf16[64,2176]{1,0:T(8,128)(2,1)S(1)} %collective-permute-done.13.refs_7_.refs_11_), channel_id=1, source_target_pairs={{0,4},{1,3},{2,6},{3,1},{4,0},{5,7},{6,2},{7,5},{8,12},{9,11},{10,... | collective-permute-start | bytes 835592 | tf_op jit(solution)/shard_map/ppermute | solution.py:166
  50.7 5.8 %shard_map.111 = (bf16[256,2048]{1,0:T(8,128)(2,1)}, bf16[256,768]{1,0:T(8,128)(2,1)}, bf16[256,768]{1,0:T(8,128)(2,1)}, bf16[256,768]{1,0:T(8,128)(2,1)}) custom-call(s32[2]{0:T(128)S(1)} %get-tuple-element.73.where_ref, bf16[64,2176]{1,0:T(8,128)(2,1)} %copy-done, bf16[64,2176]{1,0:T(8,128)(2,1)} %collective-permute-done.refs_1_.refs_5_, ...), custom_call_target="tpu_custom_call" | custom-call | flops 2415919104 | bytes 11665412 | tf_op jit(solution)/shard_map/pallas_call | solution.py:396
  57.5 5.8 %shard_map.112 = (bf16[256,2048]{1,0:T(8,128)(2,1)}, bf16[256,768]{1,0:T(8,128)(2,1)}, bf16[256,768]{1,0:T(8,128)(2,1)}, bf16[256,768]{1,0:T(8,128)(2,1)}) custom-call(s32[2]{0:T(128)S(1)} %get-tuple-element.73.where_ref, bf16[64,2176]{1,0:T(8,128)(2,1)} %copy-done.4, bf16[64,2176]{1,0:T(8,128)(2,1)} %collective-permute-done.8.refs_1_.refs_13_.refs_9_, ...), custom_call_target="tpu_custom_call" | custom-call | flops 2415919104 | bytes 11665412 | tf_op jit(solution)/shard_map/pallas_call | solution.py:396
  64.1 9.6 %shard_map.113 = (bf16[256,2048]{1,0:T(8,128)(2,1)}, bf16[256,2048]{1,0:T(8,128)(2,1)}, bf16[512,768]{1,0:T(8,128)(2,1)}, bf16[512,768]{1,0:T(8,128)(2,1)}, bf16[512,2048]{1,0:T(8,128)(2,1)}) custom-call(s32[2]{0:T(128)S(1)} %get-tuple-element.73.where_ref, bf16[256,768]{1,0:T(8,128)(2,1)} %get-tuple-element.94.refs_0_, ...), custom_call_target="tpu_custom_call" | custom-call | flops 4831838208 | bytes 15466500 | tf_op jit(solution)/shard_map/pallas_call | solution.py:396
  73.7 4.7 %collective-permute-done.18 = bf16[256,2048]{1,0:T(8,128)(2,1)S(1)} collective-permute-done((bf16[256,2048]{1,0:T(8,128)(2,1)}, bf16[256,2048]{1,0:T(8,128)(2,1)S(1)}, u32[]{:S(2)}, u32[]{:S(2)}) %collective-permute-start.18) | collective-permute-done | bytes 1048608 | tf_op jit(solution)/shard_map/ppermute | solution.py:166
  80.8 2.2 %shard_map.114 = (bf16[512,2048]{1,0:T(8,128)(2,1)S(1)}, bf16[512,768]{1,0:T(8,128)(2,1)S(1)}) custom-call(bf16[64,2176]{1,0:T(8,128)(2,1)} %copy-done, bf16[64,2176]{1,0:T(8,128)(2,1)} %collective-permute-done.refs_1_.refs_5_, bf16[64,2176]{1,0:T(8,128)(2,1)} %copy-done.3, bf16[64,2176]{1,0:T(8,128)(2,1)} %collective-permute-done.6.refs_3_.refs_7_, ...), custom_call_target="tpu_custom_call" | custom-call | tf_op jit(solution)/shard_map/pallas_call | solution.py:485
  83.1 11.9 %collective-permute-done.20 = bf16[128,2048]{1,0:T(8,128)(2,1)} collective-permute-done((bf16[128,2048]{1,0:T(8,128)(2,1)}, bf16[128,2048]{1,0:T(8,128)(2,1)}, u32[]{:S(2)}, u32[]{:S(2)}) %collective-permute-start.20) | collective-permute-done | bytes 524320 | tf_op jit(solution)/shard_map/ppermute | solution.py:166
  105.1 2.1 %collective-permute-done.23 = bf16[128,2048]{1,0:T(8,128)(2,1)S(1)} collective-permute-done((bf16[128,2048]{1,0:T(8,128)(2,1)S(1)}, bf16[128,2048]{1,0:T(8,128)(2,1)S(1)}, u32[]{:S(2)}, u32[]{:S(2)}) %collective-permute-start.23) | collective-permute-done | bytes 524320 | tf_op jit(solution)/shard_map/ppermute | solution.py:166
  107.4 2.2 %collective-permute-start.24 = (bf16[32,2048]{1,0:T(8,128)(2,1)S(1)}, bf16[32,2048]{1,0:T(8,128)(2,1)S(1)}, u32[]{:S(2)}, u32[]{:S(2)}) collective-permute-start(bf16[32,2048]{1,0:T(8,128)(2,1)S(1)} %get-tuple-element.129), channel_id=1, source_target_pairs={{0,16},{8,24},{16,0},{24,8},{1,17},{9,25},{17,1},{25,9},{2,18},{10... | collective-permute-start | bytes 393224 | tf_op jit(solution)/shard_map/ppermute | solution.py:158
  111.0 2.2 %add_convert_fusion.2 = bf16[1024,768]{1,0:T(8,128)(2,1)} fusion(bf16[1024,768]{1,0:T(8,128)(2,1)S(1)} %collective-permute-done.25, bf16[512,768]{1,0:T(8,128)(2,1)S(1)} %copy-done.17, bf16[512,2048]{1,0:T(8,128)(2,1)S(1)} %get-tuple-element.116, s32[]{:T(128)S(6)} %select_n.19), kind=kOutput, calls=%fused_computation.2 | convolution fusion | flops 807665664 | bytes 4980740 | tf_op jit(solution)/shard_map/dot_general | solution.py:20
  113.2 2.2 %add_convert_fusion = bf16[384,2048]{1,0:T(8,128)(2,1)} fusion(bf16[384,2048]{1,0:T(8,128)(2,1)S(1)} %collective-permute-done.27, bf16[512,2048]{1,0:T(8,128)(2,1)S(1)} %copy-done.15, bf16[512,768]{1,0:T(8,128)(2,1)S(1)} %get-tuple-element.119, s32[]{:T(128)S(6)} %select_n.21), kind=kOutput, calls=%fused_computation | convolution fusion | flops 807665664 | bytes 5636100 | tf_op jit(solution)/shard_map/dot_general | solution.py:20
  115.4 2.2 %add_convert_fusion.1 = bf16[1024,768]{1,0:T(8,128)(2,1)} fusion(bf16[1024,768]{1,0:T(8,128)(2,1)S(1)} %collective-permute-done.26, bf16[512,768]{1,0:T(8,128)(2,1)S(1)} %copy-done.16, bf16[512,2048]{1,0:T(8,128)(2,1)S(1)} %get-tuple-element.116, s32[]{:T(128)S(6)} %select_n.19), kind=kOutput, calls=%fused_computation.1 | convolution fusion | flops 807665664 | bytes 4980740 | tf_op jit(solution)/shard_map/dot_general | solution.py:20
  118.7 2.8 %collective-permute-done.24 = bf16[32,2048]{1,0:T(8,128)(2,1)S(1)} collective-permute-done((bf16[32,2048]{1,0:T(8,128)(2,1)S(1)}, bf16[32,2048]{1,0:T(8,128)(2,1)S(1)}, u32[]{:S(2)}, u32[]{:S(2)}) %collective-permute-start.24) | collective-permute-done | bytes 131104 | tf_op jit(solution)/shard_map/ppermute | solution.py:158
  (101 shorter events, 29.8 us)
Async XLA Ops:
  2.6 13.0 %collective-permute-start.1 = (bf16[64,2176]{1,0:T(8,128)(2,1)S(1)}, bf16[64,2176]{1,0:T(8,128)(2,1)S(1)}, u32[]{:S(2)}, u32[]{:S(2)}) collective-permute-start(bf16[64,2176]{1,0:T(8,128)(2,1)S(1)} %pad_maximum_fusion.refs_0_.refs_4_), channel_id=1, source_target_pairs={{0,8},{8,0},{16,24},{24,16},{1,9},{9,1},{17,25},{25,17},{2,10},{10... | collective-permute-start | bytes 835592 | tf_op jit(solution)/shard_map/ppermute | solution.py:158
  5.7 9.9 %collective-permute-start.2 = (bf16[64,2176]{1,0:T(8,128)(2,1)S(1)}, bf16[64,2176]{1,0:T(8,128)(2,1)}, u32[]{:S(2)}, u32[]{:S(2)}) collective-permute-start(bf16[64,2176]{1,0:T(8,128)(2,1)S(1)} %pad_maximum_fusion.refs_0_.refs_4_), channel_id=1, source_target_pairs={{0,2},{1,5},{2,0},{3,7},{4,6},{5,1},{6,4},{7,3},{8,10},{9,13},{10,... | collective-permute-start | bytes 835592 | tf_op jit(solution)/shard_map/ppermute | solution.py:166
  7.2 8.4 %collective-permute-start.3 = (bf16[64,2176]{1,0:T(8,128)(2,1)S(1)}, bf16[64,2176]{1,0:T(8,128)(2,1)S(1)}, u32[]{:S(2)}, u32[]{:S(2)}) collective-permute-start(bf16[64,2176]{1,0:T(8,128)(2,1)S(1)} %pad_maximum_fusion.refs_0_.refs_4_), channel_id=1, source_target_pairs={{0,4},{1,3},{2,6},{3,1},{4,0},{5,7},{6,2},{7,5},{8,12},{9,11},{10,... | collective-permute-start | bytes 835592 | tf_op jit(solution)/shard_map/ppermute | solution.py:166
  8.7 14.6 %collective-permute-start = (bf16[64,2176]{1,0:T(8,128)(2,1)S(1)}, bf16[64,2176]{1,0:T(8,128)(2,1)}, u32[]{:S(2)}, u32[]{:S(2)}) collective-permute-start(bf16[64,2176]{1,0:T(8,128)(2,1)S(1)} %pad_maximum_fusion.refs_0_.refs_4_), channel_id=1, source_target_pairs={{0,16},{8,24},{16,0},{24,8},{1,17},{9,25},{17,1},{25,9},{2,18},{10... | collective-permute-start | bytes 835592 | tf_op jit(solution)/shard_map/ppermute | solution.py:158
  15.6 9.8 %collective-permute-start.4 = (bf16[64,2176]{1,0:T(8,128)(2,1)S(1)}, bf16[64,2176]{1,0:T(8,128)(2,1)S(1)}, u32[]{:S(2)}, u32[]{:S(2)}) collective-permute-start(bf16[64,2176]{1,0:T(8,128)(2,1)S(1)} %collective-permute-done.1.refs_2_.refs_6_), channel_id=1, source_target_pairs={{0,2},{1,5},{2,0},{3,7},{4,6},{5,1},{6,4},{7,3},{8,10},{9,13},{10,... | collective-permute-start | bytes 835592 | tf_op jit(solution)/shard_map/ppermute | solution.py:166
  26.0 12.4 %collective-permute-start.9 = (bf16[64,2176]{1,0:T(8,128)(2,1)}, bf16[64,2176]{1,0:T(8,128)(2,1)}, u32[]{:S(2)}, u32[]{:S(2)}) collective-permute-start(bf16[64,2176]{1,0:T(8,128)(2,1)} %collective-permute-done.2.refs_4_.refs_8_), channel_id=1, source_target_pairs={{0,4},{1,3},{2,6},{3,1},{4,0},{5,7},{6,2},{7,5},{8,12},{9,11},{10,... | collective-permute-start | bytes 835592 | tf_op jit(solution)/shard_map/ppermute | solution.py:166
  28.1 10.4 %collective-permute-start.6 = (bf16[64,2176]{1,0:T(8,128)(2,1)}, bf16[64,2176]{1,0:T(8,128)(2,1)}, u32[]{:S(2)}, u32[]{:S(2)}) collective-permute-start(bf16[64,2176]{1,0:T(8,128)(2,1)} %collective-permute-done.refs_1_.refs_5_), channel_id=1, source_target_pairs={{0,8},{8,0},{16,24},{24,16},{1,9},{9,1},{17,25},{25,17},{2,10},{10... | collective-permute-start | bytes 835592 | tf_op jit(solution)/shard_map/ppermute | solution.py:158
  28.1 10.4 %collective-permute-start.7 = (bf16[64,2176]{1,0:T(8,128)(2,1)}, bf16[64,2176]{1,0:T(8,128)(2,1)}, u32[]{:S(2)}, u32[]{:S(2)}) collective-permute-start(bf16[64,2176]{1,0:T(8,128)(2,1)} %collective-permute-done.refs_1_.refs_5_), channel_id=1, source_target_pairs={{0,2},{1,5},{2,0},{3,7},{4,6},{5,1},{6,4},{7,3},{8,10},{9,13},{10,... | collective-permute-start | bytes 835592 | tf_op jit(solution)/shard_map/ppermute | solution.py:166
  29.4 9.5 %collective-permute-start.8 = (bf16[64,2176]{1,0:T(8,128)(2,1)}, bf16[64,2176]{1,0:T(8,128)(2,1)}, u32[]{:S(2)}, u32[]{:S(2)}) collective-permute-start(bf16[64,2176]{1,0:T(8,128)(2,1)} %collective-permute-done.refs_1_.refs_5_), channel_id=1, source_target_pairs={{0,4},{1,3},{2,6},{3,1},{4,0},{5,7},{6,2},{7,5},{8,12},{9,11},{10,... | collective-permute-start | bytes 835592 | tf_op jit(solution)/shard_map/ppermute | solution.py:166
  38.9 9.7 %collective-permute-start.13 = (bf16[64,2176]{1,0:T(8,128)(2,1)}, bf16[64,2176]{1,0:T(8,128)(2,1)S(1)}, u32[]{:S(2)}, u32[]{:S(2)}) collective-permute-start(bf16[64,2176]{1,0:T(8,128)(2,1)} %collective-permute-done.6.refs_3_.refs_7_), channel_id=1, source_target_pairs={{0,2},{1,5},{2,0},{3,7},{4,6},{5,1},{6,4},{7,3},{8,10},{9,13},{10,... | collective-permute-start | bytes 835592 | tf_op jit(solution)/shard_map/ppermute | solution.py:166
  40.3 16.2 %collective-permute-start.16 = (bf16[64,2176]{1,0:T(8,128)(2,1)S(1)}, bf16[64,2176]{1,0:T(8,128)(2,1)S(1)}, u32[]{:S(2)}, u32[]{:S(2)}) collective-permute-start(bf16[64,2176]{1,0:T(8,128)(2,1)S(1)} %copy-done.6), channel_id=1, source_target_pairs={{0,4},{1,3},{2,6},{3,1},{4,0},{5,7},{6,2},{7,5},{8,12},{9,11},{10,... | collective-permute-start | bytes 835592 | tf_op jit(solution)/shard_map/ppermute | solution.py:166
  41.8 14.8 %collective-permute-start.14 = (bf16[64,2176]{1,0:T(8,128)(2,1)}, bf16[64,2176]{1,0:T(8,128)(2,1)S(1)}, u32[]{:S(2)}, u32[]{:S(2)}) collective-permute-start(bf16[64,2176]{1,0:T(8,128)(2,1)} %collective-permute-done.8.refs_1_.refs_13_.refs_9_), channel_id=1, source_target_pairs={{0,8},{8,0},{16,24},{24,16},{1,9},{9,1},{17,25},{25,17},{2,10},{10... | collective-permute-start | bytes 835592 | tf_op jit(solution)/shard_map/ppermute | solution.py:158
  42.2 14.4 %collective-permute-start.15 = (bf16[64,2176]{1,0:T(8,128)(2,1)}, bf16[64,2176]{1,0:T(8,128)(2,1)S(1)}, u32[]{:S(2)}, u32[]{:S(2)}) collective-permute-start(bf16[64,2176]{1,0:T(8,128)(2,1)} %collective-permute-done.7.refs_5_.refs_9_), channel_id=1, source_target_pairs={{0,4},{1,3},{2,6},{3,1},{4,0},{5,7},{6,2},{7,5},{8,12},{9,11},{10,... | collective-permute-start | bytes 835592 | tf_op jit(solution)/shard_map/ppermute | solution.py:166
  63.3 15.1 %collective-permute-start.18 = (bf16[256,2048]{1,0:T(8,128)(2,1)}, bf16[256,2048]{1,0:T(8,128)(2,1)S(1)}, u32[]{:S(2)}, u32[]{:S(2)}) collective-permute-start(bf16[256,2048]{1,0:T(8,128)(2,1)} %get-tuple-element.93), channel_id=1, source_target_pairs={{0,4},{1,3},{2,6},{3,1},{4,0},{5,7},{6,2},{7,5},{8,12},{9,11},{10,... | collective-permute-start | bytes 3145736 | tf_op jit(solution)/shard_map/ppermute | solution.py:166
  78.4 18.3 %collective-permute-start.19 = (bf16[256,2048]{1,0:T(8,128)(2,1)}, bf16[256,2048]{1,0:T(8,128)(2,1)S(1)}, u32[]{:S(2)}, u32[]{:S(2)}) collective-permute-start(bf16[256,2048]{1,0:T(8,128)(2,1)} %get-tuple-element.103), channel_id=1, source_target_pairs={{0,4},{1,3},{2,6},{3,1},{4,0},{5,7},{6,2},{7,5},{8,12},{9,11},{10,... | collective-permute-start | bytes 3145736 | tf_op jit(solution)/shard_map/ppermute | solution.py:166
  80.0 14.9 %collective-permute-start.20 = (bf16[128,2048]{1,0:T(8,128)(2,1)}, bf16[128,2048]{1,0:T(8,128)(2,1)}, u32[]{:S(2)}, u32[]{:S(2)}) collective-permute-start(bf16[128,2048]{1,0:T(8,128)(2,1)} %add_convert_fusion.6), channel_id=1, source_target_pairs={{0,2},{1,5},{2,0},{3,7},{4,6},{5,1},{6,4},{7,3},{8,10},{9,13},{10,... | collective-permute-start | bytes 1572872 | tf_op jit(solution)/shard_map/ppermute | solution.py:166
  97.9 9.2 %collective-permute-start.23 = (bf16[128,2048]{1,0:T(8,128)(2,1)S(1)}, bf16[128,2048]{1,0:T(8,128)(2,1)S(1)}, u32[]{:S(2)}, u32[]{:S(2)}) collective-permute-start(bf16[128,2048]{1,0:T(8,128)(2,1)S(1)} %add_convert_fusion.4), channel_id=1, source_target_pairs={{0,2},{1,5},{2,0},{3,7},{4,6},{5,1},{6,4},{7,3},{8,10},{9,13},{10,... | collective-permute-start | bytes 1572872 | tf_op jit(solution)/shard_map/ppermute | solution.py:166
  99.3 10.3 %collective-permute-start.25 = (bf16[1024,768]{1,0:T(8,128)(2,1)S(1)}, bf16[1024,768]{1,0:T(8,128)(2,1)S(1)}, u32[]{:S(2)}, u32[]{:S(2)}) collective-permute-start(bf16[1024,768]{1,0:T(8,128)(2,1)S(1)} %convolution_convert_fusion.2), channel_id=1, source_target_pairs={{0,1},{1,0},{2,3},{3,2},{4,5},{5,4},{6,7},{7,6},{8,9},{9,8},{10,11... | collective-permute-start | bytes 4718600 | tf_op jit(solution)/shard_map/ppermute | solution.py:16
  100.4 15.0 %collective-permute-start.26 = (bf16[1024,768]{1,0:T(8,128)(2,1)S(1)}, bf16[1024,768]{1,0:T(8,128)(2,1)S(1)}, u32[]{:S(2)}, u32[]{:S(2)}) collective-permute-start(bf16[1024,768]{1,0:T(8,128)(2,1)S(1)} %convolution_convert_fusion.1), channel_id=1, source_target_pairs={{0,1},{1,0},{2,3},{3,2},{4,5},{5,4},{6,7},{7,6},{8,9},{9,8},{10,11... | collective-permute-start | bytes 4718600 | tf_op jit(solution)/shard_map/ppermute | solution.py:16
  102.0 11.2 %collective-permute-start.27 = (bf16[384,2048]{1,0:T(8,128)(2,1)S(1)}, bf16[384,2048]{1,0:T(8,128)(2,1)S(1)}, u32[]{:S(2)}, u32[]{:S(2)}) collective-permute-start(bf16[384,2048]{1,0:T(8,128)(2,1)S(1)} %convolution_convert_fusion), channel_id=1, source_target_pairs={{0,1},{1,0},{2,3},{3,2},{4,5},{5,4},{6,7},{7,6},{8,9},{9,8},{10,11... | collective-permute-start | bytes 4718600 | tf_op jit(solution)/shard_map/ppermute | solution.py:16
  103.3 15.4 %collective-permute-start.22 = (bf16[32,2048]{1,0:T(8,128)(2,1)S(1)}, bf16[32,2048]{1,0:T(8,128)(2,1)S(1)}, u32[]{:S(2)}, u32[]{:S(2)}) collective-permute-start(bf16[32,2048]{1,0:T(8,128)(2,1)S(1)} %get-tuple-element.130), channel_id=1, source_target_pairs={{0,16},{8,24},{16,0},{24,8},{1,17},{9,25},{17,1},{25,9},{2,18},{10... | collective-permute-start | bytes 393224 | tf_op jit(solution)/shard_map/ppermute | solution.py:158
  107.4 14.0 %collective-permute-start.24 = (bf16[32,2048]{1,0:T(8,128)(2,1)S(1)}, bf16[32,2048]{1,0:T(8,128)(2,1)S(1)}, u32[]{:S(2)}, u32[]{:S(2)}) collective-permute-start(bf16[32,2048]{1,0:T(8,128)(2,1)S(1)} %get-tuple-element.129), channel_id=1, source_target_pairs={{0,16},{8,24},{16,0},{24,8},{1,17},{9,25},{17,1},{25,9},{2,18},{10... | collective-permute-start | bytes 393224 | tf_op jit(solution)/shard_map/ppermute | solution.py:158
  109.6 12.5 %collective-permute-start.29 = (bf16[32,2048]{1,0:T(8,128)(2,1)S(1)}, bf16[32,2048]{1,0:T(8,128)(2,1)S(1)}, u32[]{:S(2)}, u32[]{:S(2)}) collective-permute-start(bf16[32,2048]{1,0:T(8,128)(2,1)S(1)} %get-tuple-element.128), channel_id=1, source_target_pairs={{0,24},{8,16},{16,8},{24,0},{1,25},{9,17},{17,9},{25,1},{2,26},{10... | collective-permute-start | bytes 393224 | tf_op jit(solution)/shard_map/ppermute | solution.py:158
  113.2 8.9 %collective-permute-start.28 = (bf16[32,2048]{1,0:T(8,128)(2,1)S(1)}, bf16[32,2048]{1,0:T(8,128)(2,1)S(1)}, u32[]{:S(2)}, u32[]{:S(2)}) collective-permute-start(bf16[32,2048]{1,0:T(8,128)(2,1)S(1)} %get-tuple-element.127), channel_id=1, source_target_pairs={{0,8},{8,0},{16,24},{24,16},{1,9},{9,1},{17,25},{25,17},{2,10},{10... | collective-permute-start | bytes 393224 | tf_op jit(solution)/shard_map/ppermute | solution.py:158
  (24 other events, 193.1 us)

commit v7 on v6

--- a/solution.py
+++ b/solution.py
@@ -179,7 +179,7 @@
     for k in range(count + 1):
         due = [
             (part, step)
-            for part, step in ((moved, k), (first, k - 1), (second, k - 1), (both, k - 3))
+            for part, step in ((moved, k), (first, k - 1), (second, k - 2), (both, k - 2))
             if k > 0 and step in part
         ]
         values = beside(k, [part[step] for part, step in due])
@@ -504,9 +504,6 @@
         flops,
         [where, *gate_pre, *up_pre, *pieces, *weights],
     )
-    out_came, grad_keep, grad_send, dgate, dup, rows_scaled = tie(
-        (out_came, grad_keep, grad_send, dgate, dup, rows_scaled)
-    )
     grad_came = swap_inner(grad_send, SECOND)
     out_column = reduce_part(out_keep.reshape(2, -1, width), out_came)
     grad_came, out_column, dgate, dup, rows_scaled, hidden, rows_in = tie(

time: 123 us -> 120 us (0.976)
  starting transfers between devices: 37.6 us -> 30.4 us
  waiting for transfers between devices: 39.1 us -> 43.3 us
    ppermute x15, starting transfers between devices: 24 us -> 17.8 us  [swap_inner(): return lax.ppermute(value, ('exp', 'rep'), pairs)]
    ppermute x15, waiting for transfers between devices: 27.5 us -> 29.7 us  [swap_inner(): return lax.ppermute(value, ('exp', 'rep'), pairs)]
    ppermute x6, waiting for transfers between devices: 0.02 us -> 1.9 us  [partner_2(): return lax.ppermute(value, axis, pairs)]
  transfers between devices with their start and end apart: 30 -> 30, of which waited for: 13 -> 14; matrix products, arithmetic and copies ran while one was open for 11% -> 11% of each run, Pallas kernels for 18% -> 19%
where the time goes in v7:
time: 120 us
  waiting for transfers between devices  43.3 us (36%)
  starting transfers between devices  30.4 us (25%)
  Pallas kernels  28.4 us (24%)
  matrix products  9.68 us (8%)
  other arithmetic  5.92 us (5%)
    ppermute x15, waiting for transfers between devices, swap_inner(): return lax.ppermute(value, ('exp', 'rep'), pairs)  29.7 us
    pallas_call x3, Pallas kernels, expert_call(): pl.pallas_call(kernel, out_shape=[pltpu.HBM(shape, dtype) for shape, dtyp...  21.2 us
    ppermute x15, starting transfers between devices, swap_inner(): return lax.ppermute(value, ('exp', 'rep'), pairs)  17.8 us
    ppermute x9, waiting for transfers between devices, swap_group(): return lax.ppermute(value, 'grp', [(i, i ^ mask) for i in range(count)])  11.7 us
    ppermute x9, starting transfers between devices, swap_group(): return lax.ppermute(value, 'grp', [(i, i ^ mask) for i in range(count)])  11.4 us
    dot_general x6, matrix products, contract_rows(): lax.dot_general(left, right, (((0,), (0,)), ((), ())), preferred_element_...  9.68 us
    pallas_call x1, Pallas kernels, load(): pl.pallas_call(weights_kernel, out_shape=[pltpu.VMEM(shape, jnp.bfloat16)...  4.93 us
    convert_element_type x5, other arithmetic, add_bf16(): (left.astype(jnp.float32) + right.astype(jnp.float32)).astype(jnp.bfloat16)  2.63 us
  transfers between devices with their start and end apart: 30, of which 14 were waited for; matrix products, arithmetic and copies ran while one was open for 11% of the time, Pallas kernels for 19%

profile of v7, /device:TPU:0, one launch (start us, length us, event | category | flops | bytes accessed | tf_op | source)
XLA Modules:
  0.0 119.9 jit_solution(13631276529383219380)
XLA Ops:
  2.6 3.1 %collective-permute-start.1 = (bf16[64,2176]{1,0:T(8,128)(2,1)S(1)}, bf16[64,2176]{1,0:T(8,128)(2,1)}, u32[]{:S(2)}, u32[]{:S(2)}) collective-permute-start(bf16[64,2176]{1,0:T(8,128)(2,1)S(1)} %pad_maximum_fusion.refs_0_.refs_4_), channel_id=1, source_target_pairs={{0,8},{8,0},{16,24},{24,16},{1,9},{9,1},{17,25},{25,17},{2,10},{10... | collective-permute-start | bytes 835592 | tf_op jit(solution)/shard_map/ppermute | solution.py:158
  7.2 2.6 %collective-permute-start = (bf16[64,2176]{1,0:T(8,128)(2,1)S(1)}, bf16[64,2176]{1,0:T(8,128)(2,1)}, u32[]{:S(2)}, u32[]{:S(2)}) collective-permute-start(bf16[64,2176]{1,0:T(8,128)(2,1)S(1)} %pad_maximum_fusion.refs_0_.refs_4_), channel_id=1, source_target_pairs={{0,16},{8,24},{16,0},{24,8},{1,17},{9,25},{17,1},{25,9},{2,18},{10... | collective-permute-start | bytes 835592 | tf_op jit(solution)/shard_map/ppermute | solution.py:158
  11.3 5.8 %collective-permute-done.1.refs_2_.refs_6_ = bf16[64,2176]{1,0:T(8,128)(2,1)} collective-permute-done((bf16[64,2176]{1,0:T(8,128)(2,1)S(1)}, bf16[64,2176]{1,0:T(8,128)(2,1)}, u32[]{:S(2)}, u32[]{:S(2)}) %collective-permute-start.1) | collective-permute-done | bytes 278560 | tf_op jit(solution)/shard_map/ppermute | solution.py:158
  18.7 2.5 %collective-permute-start.5 = (bf16[64,2176]{1,0:T(8,128)(2,1)S(1)}, bf16[64,2176]{1,0:T(8,128)(2,1)S(1)}, u32[]{:S(2)}, u32[]{:S(2)}) collective-permute-start(bf16[64,2176]{1,0:T(8,128)(2,1)S(1)} %collective-permute-done.2.refs_4_.refs_8_), channel_id=1, source_target_pairs={{0,4},{1,3},{2,6},{3,1},{4,0},{5,7},{6,2},{7,5},{8,12},{9,11},{10,... | collective-permute-start | bytes 835592 | tf_op jit(solution)/shard_map/ppermute | solution.py:166
  22.1 4.6 %collective-permute-done.3.refs_6_.refs_10_ = bf16[64,2176]{1,0:T(8,128)(2,1)} collective-permute-done((bf16[64,2176]{1,0:T(8,128)(2,1)}, bf16[64,2176]{1,0:T(8,128)(2,1)}, u32[]{:S(2)}, u32[]{:S(2)}) %collective-permute-start.3) | collective-permute-done | bytes 278560 | tf_op jit(solution)/shard_map/ppermute | solution.py:166
  29.6 1.9 %collective-permute-done.11.refs_3_ = bf16[1024,768]{1,0:T(8,128)(2,1)S(1)} collective-permute-done((bf16[1024,768]{1,0:T(8,128)(2,1)}, bf16[1024,768]{1,0:T(8,128)(2,1)S(1)}, u32[]{:S(2)}, u32[]{:S(2)}) %collective-permute-start.11) | collective-permute-done | bytes 1572896 | tf_op jit(solution)/shard_map/ppermute | solution.py:16
  31.5 2.2 %collective-permute-start.9 = (bf16[64,2176]{1,0:T(8,128)(2,1)}, bf16[64,2176]{1,0:T(8,128)(2,1)}, u32[]{:S(2)}, u32[]{:S(2)}) collective-permute-start(bf16[64,2176]{1,0:T(8,128)(2,1)} %collective-permute-done.3.refs_6_.refs_10_), channel_id=1, source_target_pairs={{0,4},{1,3},{2,6},{3,1},{4,0},{5,7},{6,2},{7,5},{8,12},{9,11},{10,... | collective-permute-start | bytes 835592 | tf_op jit(solution)/shard_map/ppermute | solution.py:166
  33.8 4.9 %shard_map.110 = (bf16[2048,768]{1,0:T(8,128)(2,1)S(1)}, bf16[2048,768]{1,0:T(8,128)(2,1)S(1)}, bf16[768,2048]{1,0:T(8,128)(2,1)S(1)}, s32[2]{0:T(128)S(1)}) custom-call(s32[2]{0:T(128)S(1)} %pad_add_fusion.where_ref, bf16[1024,768]{1,0:T(8,128)(2,1)} %bitcast.15, bf16[1024,768]{1,0:T(8,128)(2,1)} %copy-done.1, bf16[1024,768]{1,0:T(8,128)(2,1)} %bitcast.17, ...), custom_call_target="tpu_custom_call" | custom-call | tf_op jit(solution)/shard_map/pallas_call | solution.py:420
  41.1 2.4 %collective-permute-done.14.refs_1_.refs_13_.refs_9_ = bf16[64,2176]{1,0:T(8,128)(2,1)S(1)} collective-permute-done((bf16[64,2176]{1,0:T(8,128)(2,1)}, bf16[64,2176]{1,0:T(8,128)(2,1)S(1)}, u32[]{:S(2)}, u32[]{:S(2)}) %collective-permute-start.14) | collective-permute-done | bytes 278560 | tf_op jit(solution)/shard_map/ppermute | solution.py:166
  44.8 3.6 %collective-permute-done.13.refs_7_.refs_11_ = bf16[64,2176]{1,0:T(8,128)(2,1)S(1)} collective-permute-done((bf16[64,2176]{1,0:T(8,128)(2,1)}, bf16[64,2176]{1,0:T(8,128)(2,1)S(1)}, u32[]{:S(2)}, u32[]{:S(2)}) %collective-permute-start.13) | collective-permute-done | bytes 278560 | tf_op jit(solution)/shard_map/ppermute | solution.py:166
  49.3 5.8 %shard_map.111 = (bf16[256,2048]{1,0:T(8,128)(2,1)}, bf16[256,768]{1,0:T(8,128)(2,1)}, bf16[256,768]{1,0:T(8,128)(2,1)}, bf16[256,768]{1,0:T(8,128)(2,1)}) custom-call(s32[2]{0:T(128)S(1)} %get-tuple-element.68.where_ref, bf16[64,2176]{1,0:T(8,128)(2,1)} %copy-done, bf16[64,2176]{1,0:T(8,128)(2,1)} %collective-permute-done.refs_1_.refs_5_, ...), custom_call_target="tpu_custom_call" | custom-call | flops 2415919104 | bytes 11665412 | tf_op jit(solution)/shard_map/pallas_call | solution.py:396
  56.1 5.8 %shard_map.112 = (bf16[256,2048]{1,0:T(8,128)(2,1)}, bf16[256,768]{1,0:T(8,128)(2,1)}, bf16[256,768]{1,0:T(8,128)(2,1)}, bf16[256,768]{1,0:T(8,128)(2,1)}) custom-call(s32[2]{0:T(128)S(1)} %get-tuple-element.68.where_ref, bf16[64,2176]{1,0:T(8,128)(2,1)} %copy-done.4, bf16[64,2176]{1,0:T(8,128)(2,1)} %copy-done.6, ...), custom_call_target="tpu_custom_call" | custom-call | flops 2415919104 | bytes 11665412 | tf_op jit(solution)/shard_map/pallas_call | solution.py:396
  63.0 9.6 %shard_map.113 = (bf16[256,2048]{1,0:T(8,128)(2,1)}, bf16[256,2048]{1,0:T(8,128)(2,1)}, bf16[512,768]{1,0:T(8,128)(2,1)}, bf16[512,768]{1,0:T(8,128)(2,1)}, bf16[512,2048]{1,0:T(8,128)(2,1)}) custom-call(s32[2]{0:T(128)S(1)} %get-tuple-element.68.where_ref, bf16[256,768]{1,0:T(8,128)(2,1)} %get-tuple-element.74.refs_0_, ...), custom_call_target="tpu_custom_call" | custom-call | flops 4831838208 | bytes 15466500 | tf_op jit(solution)/shard_map/pallas_call | solution.py:396
  73.7 3.3 %collective-permute-done.19 = bf16[256,2048]{1,0:T(8,128)(2,1)S(1)} collective-permute-done((bf16[256,2048]{1,0:T(8,128)(2,1)}, bf16[256,2048]{1,0:T(8,128)(2,1)S(1)}, u32[]{:S(2)}, u32[]{:S(2)}) %collective-permute-start.19) | collective-permute-done | bytes 1048608 | tf_op jit(solution)/shard_map/ppermute | solution.py:166
  78.1 2.2 %shard_map.114 = (bf16[512,2048]{1,0:T(8,128)(2,1)S(1)}, bf16[512,768]{1,0:T(8,128)(2,1)S(1)}) custom-call(bf16[64,2176]{1,0:T(8,128)(2,1)} %copy-done, bf16[64,2176]{1,0:T(8,128)(2,1)} %collective-permute-done.refs_1_.refs_5_, bf16[64,2176]{1,0:T(8,128)(2,1)} %collective-permute-done.1.refs_2_.refs_6_, ...), custom_call_target="tpu_custom_call" | custom-call | tf_op jit(solution)/shard_map/pallas_call | solution.py:485
  80.4 10.1 %collective-permute-done.20 = bf16[128,2048]{1,0:T(8,128)(2,1)} collective-permute-done((bf16[128,2048]{1,0:T(8,128)(2,1)}, bf16[128,2048]{1,0:T(8,128)(2,1)}, u32[]{:S(2)}, u32[]{:S(2)}) %collective-permute-start.20) | collective-permute-done | bytes 524320 | tf_op jit(solution)/shard_map/ppermute | solution.py:166
  91.8 2.7 %collective-permute-done.18 = bf16[256,2048]{1,0:T(8,128)(2,1)S(1)} collective-permute-done((bf16[256,2048]{1,0:T(8,128)(2,1)}, bf16[256,2048]{1,0:T(8,128)(2,1)S(1)}, u32[]{:S(2)}, u32[]{:S(2)}) %collective-permute-start.18) | collective-permute-done | bytes 1048608 | tf_op jit(solution)/shard_map/ppermute | solution.py:166
  99.0 2.0 %collective-permute-done.21 = bf16[64,2048]{1,0:T(8,128)(2,1)S(1)} collective-permute-done((bf16[64,2048]{1,0:T(8,128)(2,1)S(1)}, bf16[64,2048]{1,0:T(8,128)(2,1)S(1)}, u32[]{:S(2)}, u32[]{:S(2)}) %collective-permute-start.21) | collective-permute-done | bytes 262176 | tf_op jit(solution)/shard_map/ppermute | solution.py:158
  102.3 1.7 %collective-permute-done.23 = bf16[128,2048]{1,0:T(8,128)(2,1)S(1)} collective-permute-done((bf16[128,2048]{1,0:T(8,128)(2,1)S(1)}, bf16[128,2048]{1,0:T(8,128)(2,1)S(1)}, u32[]{:S(2)}, u32[]{:S(2)}) %collective-permute-start.23) | collective-permute-done | bytes 524320 | tf_op jit(solution)/shard_map/ppermute | solution.py:166
  104.2 3.2 %collective-permute-start.24 = (bf16[32,2048]{1,0:T(8,128)(2,1)S(1)}, bf16[32,2048]{1,0:T(8,128)(2,1)S(1)}, u32[]{:S(2)}, u32[]{:S(2)}) collective-permute-start(bf16[32,2048]{1,0:T(8,128)(2,1)S(1)} %get-tuple-element.117), channel_id=1, source_target_pairs={{0,16},{8,24},{16,0},{24,8},{1,17},{9,25},{17,1},{25,9},{2,18},{10... | collective-permute-start | bytes 393224 | tf_op jit(solution)/shard_map/ppermute | solution.py:158
  108.7 2.2 %add_convert_fusion.2 = bf16[1024,768]{1,0:T(8,128)(2,1)} fusion(bf16[1024,768]{1,0:T(8,128)(2,1)S(1)} %collective-permute-done.25, bf16[512,768]{1,0:T(8,128)(2,1)S(1)} %copy-done.15, bf16[512,2048]{1,0:T(8,128)(2,1)S(1)} %get-tuple-element.104, s32[]{:T(128)S(6)} %select_n.19), kind=kOutput, calls=%fused_computation.2 | convolution fusion | flops 807665664 | bytes 4980740 | tf_op jit(solution)/shard_map/dot_general | solution.py:20
  110.9 2.2 %add_convert_fusion = bf16[384,2048]{1,0:T(8,128)(2,1)} fusion(bf16[384,2048]{1,0:T(8,128)(2,1)S(1)} %collective-permute-done.27, bf16[512,2048]{1,0:T(8,128)(2,1)S(1)} %copy-done.13, bf16[512,768]{1,0:T(8,128)(2,1)S(1)} %get-tuple-element.107, s32[]{:T(128)S(6)} %select_n.21), kind=kOutput, calls=%fused_computation | convolution fusion | flops 807665664 | bytes 5636100 | tf_op jit(solution)/shard_map/dot_general | solution.py:20
  113.1 2.2 %add_convert_fusion.1 = bf16[1024,768]{1,0:T(8,128)(2,1)} fusion(bf16[1024,768]{1,0:T(8,128)(2,1)S(1)} %collective-permute-done.26, bf16[512,768]{1,0:T(8,128)(2,1)S(1)} %copy-done.14, bf16[512,2048]{1,0:T(8,128)(2,1)S(1)} %get-tuple-element.104, s32[]{:T(128)S(6)} %select_n.19), kind=kOutput, calls=%fused_computation.1 | convolution fusion | flops 807665664 | bytes 4980740 | tf_op jit(solution)/shard_map/dot_general | solution.py:20
  115.7 2.8 %collective-permute-done.24 = bf16[32,2048]{1,0:T(8,128)(2,1)S(1)} collective-permute-done((bf16[32,2048]{1,0:T(8,128)(2,1)S(1)}, bf16[32,2048]{1,0:T(8,128)(2,1)S(1)}, u32[]{:S(2)}, u32[]{:S(2)}) %collective-permute-start.24) | collective-permute-done | bytes 131104 | tf_op jit(solution)/shard_map/ppermute | solution.py:158
  (97 shorter events, 29.5 us)
Async XLA Ops:
  2.6 14.5 %collective-permute-start.1 = (bf16[64,2176]{1,0:T(8,128)(2,1)S(1)}, bf16[64,2176]{1,0:T(8,128)(2,1)}, u32[]{:S(2)}, u32[]{:S(2)}) collective-permute-start(bf16[64,2176]{1,0:T(8,128)(2,1)S(1)} %pad_maximum_fusion.refs_0_.refs_4_), channel_id=1, source_target_pairs={{0,8},{8,0},{16,24},{24,16},{1,9},{9,1},{17,25},{25,17},{2,10},{10... | collective-permute-start | bytes 835592 | tf_op jit(solution)/shard_map/ppermute | solution.py:158
  5.7 11.4 %collective-permute-start.2 = (bf16[64,2176]{1,0:T(8,128)(2,1)S(1)}, bf16[64,2176]{1,0:T(8,128)(2,1)S(1)}, u32[]{:S(2)}, u32[]{:S(2)}) collective-permute-start(bf16[64,2176]{1,0:T(8,128)(2,1)S(1)} %pad_maximum_fusion.refs_0_.refs_4_), channel_id=1, source_target_pairs={{0,2},{1,5},{2,0},{3,7},{4,6},{5,1},{6,4},{7,3},{8,10},{9,13},{10,... | collective-permute-start | bytes 835592 | tf_op jit(solution)/shard_map/ppermute | solution.py:166
  7.2 14.9 %collective-permute-start = (bf16[64,2176]{1,0:T(8,128)(2,1)S(1)}, bf16[64,2176]{1,0:T(8,128)(2,1)}, u32[]{:S(2)}, u32[]{:S(2)}) collective-permute-start(bf16[64,2176]{1,0:T(8,128)(2,1)S(1)} %pad_maximum_fusion.refs_0_.refs_4_), channel_id=1, source_target_pairs={{0,16},{8,24},{16,0},{24,8},{1,17},{9,25},{17,1},{25,9},{2,18},{10... | collective-permute-start | bytes 835592 | tf_op jit(solution)/shard_map/ppermute | solution.py:158
  9.8 12.3 %collective-permute-start.4 = (bf16[64,2176]{1,0:T(8,128)(2,1)S(1)}, bf16[64,2176]{1,0:T(8,128)(2,1)S(1)}, u32[]{:S(2)}, u32[]{:S(2)}) collective-permute-start(bf16[64,2176]{1,0:T(8,128)(2,1)S(1)} %pad_maximum_fusion.refs_0_.refs_4_), channel_id=1, source_target_pairs={{0,4},{1,3},{2,6},{3,1},{4,0},{5,7},{6,2},{7,5},{8,12},{9,11},{10,... | collective-permute-start | bytes 835592 | tf_op jit(solution)/shard_map/ppermute | solution.py:166
  17.1 9.6 %collective-permute-start.3 = (bf16[64,2176]{1,0:T(8,128)(2,1)}, bf16[64,2176]{1,0:T(8,128)(2,1)}, u32[]{:S(2)}, u32[]{:S(2)}) collective-permute-start(bf16[64,2176]{1,0:T(8,128)(2,1)} %collective-permute-done.1.refs_2_.refs_6_), channel_id=1, source_target_pairs={{0,2},{1,5},{2,0},{3,7},{4,6},{5,1},{6,4},{7,3},{8,10},{9,13},{10,... | collective-permute-start | bytes 835592 | tf_op jit(solution)/shard_map/ppermute | solution.py:166
  27.2 11.5 %collective-permute-start.8 = (bf16[64,2176]{1,0:T(8,128)(2,1)}, bf16[64,2176]{1,0:T(8,128)(2,1)}, u32[]{:S(2)}, u32[]{:S(2)}) collective-permute-start(bf16[64,2176]{1,0:T(8,128)(2,1)} %collective-permute-done.1.refs_2_.refs_6_), channel_id=1, source_target_pairs={{0,4},{1,3},{2,6},{3,1},{4,0},{5,7},{6,2},{7,5},{8,12},{9,11},{10,... | collective-permute-start | bytes 835592 | tf_op jit(solution)/shard_map/ppermute | solution.py:166
  28.3 10.5 %collective-permute-start.6 = (bf16[64,2176]{1,0:T(8,128)(2,1)}, bf16[64,2176]{1,0:T(8,128)(2,1)}, u32[]{:S(2)}, u32[]{:S(2)}) collective-permute-start(bf16[64,2176]{1,0:T(8,128)(2,1)} %collective-permute-done.refs_1_.refs_5_), channel_id=1, source_target_pairs={{0,8},{8,0},{16,24},{24,16},{1,9},{9,1},{17,25},{25,17},{2,10},{10... | collective-permute-start | bytes 835592 | tf_op jit(solution)/shard_map/ppermute | solution.py:158
  28.3 10.5 %collective-permute-start.7 = (bf16[64,2176]{1,0:T(8,128)(2,1)}, bf16[64,2176]{1,0:T(8,128)(2,1)}, u32[]{:S(2)}, u32[]{:S(2)}) collective-permute-start(bf16[64,2176]{1,0:T(8,128)(2,1)} %collective-permute-done.refs_1_.refs_5_), channel_id=1, source_target_pairs={{0,2},{1,5},{2,0},{3,7},{4,6},{5,1},{6,4},{7,3},{8,10},{9,13},{10,... | collective-permute-start | bytes 835592 | tf_op jit(solution)/shard_map/ppermute | solution.py:166
  31.5 8.6 %collective-permute-start.9 = (bf16[64,2176]{1,0:T(8,128)(2,1)}, bf16[64,2176]{1,0:T(8,128)(2,1)}, u32[]{:S(2)}, u32[]{:S(2)}) collective-permute-start(bf16[64,2176]{1,0:T(8,128)(2,1)} %collective-permute-done.3.refs_6_.refs_10_), channel_id=1, source_target_pairs={{0,4},{1,3},{2,6},{3,1},{4,0},{5,7},{6,2},{7,5},{8,12},{9,11},{10,... | collective-permute-start | bytes 835592 | tf_op jit(solution)/shard_map/ppermute | solution.py:166
  33.7 9.8 %collective-permute-start.14 = (bf16[64,2176]{1,0:T(8,128)(2,1)}, bf16[64,2176]{1,0:T(8,128)(2,1)S(1)}, u32[]{:S(2)}, u32[]{:S(2)}) collective-permute-start(bf16[64,2176]{1,0:T(8,128)(2,1)} %collective-permute-done.refs_1_.refs_5_), channel_id=1, source_target_pairs={{0,4},{1,3},{2,6},{3,1},{4,0},{5,7},{6,2},{7,5},{8,12},{9,11},{10,... | collective-permute-start | bytes 835592 | tf_op jit(solution)/shard_map/ppermute | solution.py:166
  40.1 8.3 %collective-permute-start.13 = (bf16[64,2176]{1,0:T(8,128)(2,1)}, bf16[64,2176]{1,0:T(8,128)(2,1)S(1)}, u32[]{:S(2)}, u32[]{:S(2)}) collective-permute-start(bf16[64,2176]{1,0:T(8,128)(2,1)} %collective-permute-done.6.refs_3_.refs_7_), channel_id=1, source_target_pairs={{0,2},{1,5},{2,0},{3,7},{4,6},{5,1},{6,4},{7,3},{8,10},{9,13},{10,... | collective-permute-start | bytes 835592 | tf_op jit(solution)/shard_map/ppermute | solution.py:166
  43.6 11.6 %collective-permute-start.15 = (bf16[64,2176]{1,0:T(8,128)(2,1)S(1)}, bf16[64,2176]{1,0:T(8,128)(2,1)S(1)}, u32[]{:S(2)}, u32[]{:S(2)}) collective-permute-start(bf16[64,2176]{1,0:T(8,128)(2,1)S(1)} %collective-permute-done.14.refs_1_.refs_13_.refs_9_), channel_id=1, source_target_pairs={{0,8},{8,0},{16,24},{24,16},{1,9},{9,1},{17,25},{25,17},{2,10},{10... | collective-permute-start | bytes 835592 | tf_op jit(solution)/shard_map/ppermute | solution.py:158
  43.6 11.6 %collective-permute-start.16 = (bf16[64,2176]{1,0:T(8,128)(2,1)}, bf16[64,2176]{1,0:T(8,128)(2,1)S(1)}, u32[]{:S(2)}, u32[]{:S(2)}) collective-permute-start(bf16[64,2176]{1,0:T(8,128)(2,1)} %collective-permute-done.7.refs_5_.refs_9_), channel_id=1, source_target_pairs={{0,4},{1,3},{2,6},{3,1},{4,0},{5,7},{6,2},{7,5},{8,12},{9,11},{10,... | collective-permute-start | bytes 835592 | tf_op jit(solution)/shard_map/ppermute | solution.py:166
  61.9 15.1 %collective-permute-start.19 = (bf16[256,2048]{1,0:T(8,128)(2,1)}, bf16[256,2048]{1,0:T(8,128)(2,1)S(1)}, u32[]{:S(2)}, u32[]{:S(2)}) collective-permute-start(bf16[256,2048]{1,0:T(8,128)(2,1)} %get-tuple-element.93), channel_id=1, source_target_pairs={{0,4},{1,3},{2,6},{3,1},{4,0},{5,7},{6,2},{7,5},{8,12},{9,11},{10,... | collective-permute-start | bytes 3145736 | tf_op jit(solution)/shard_map/ppermute | solution.py:166
  72.7 21.8 %collective-permute-start.18 = (bf16[256,2048]{1,0:T(8,128)(2,1)}, bf16[256,2048]{1,0:T(8,128)(2,1)S(1)}, u32[]{:S(2)}, u32[]{:S(2)}) collective-permute-start(bf16[256,2048]{1,0:T(8,128)(2,1)} %get-tuple-element.91), channel_id=1, source_target_pairs={{0,4},{1,3},{2,6},{3,1},{4,0},{5,7},{6,2},{7,5},{8,12},{9,11},{10,... | collective-permute-start | bytes 3145736 | tf_op jit(solution)/shard_map/ppermute | solution.py:166
  77.9 12.6 %collective-permute-start.20 = (bf16[128,2048]{1,0:T(8,128)(2,1)}, bf16[128,2048]{1,0:T(8,128)(2,1)}, u32[]{:S(2)}, u32[]{:S(2)}) collective-permute-start(bf16[128,2048]{1,0:T(8,128)(2,1)} %add_convert_fusion.6), channel_id=1, source_target_pairs={{0,2},{1,5},{2,0},{3,7},{4,6},{5,1},{6,4},{7,3},{8,10},{9,13},{10,... | collective-permute-start | bytes 1572872 | tf_op jit(solution)/shard_map/ppermute | solution.py:166
  94.7 9.2 %collective-permute-start.23 = (bf16[128,2048]{1,0:T(8,128)(2,1)S(1)}, bf16[128,2048]{1,0:T(8,128)(2,1)S(1)}, u32[]{:S(2)}, u32[]{:S(2)}) collective-permute-start(bf16[128,2048]{1,0:T(8,128)(2,1)S(1)} %add_convert_fusion.4), channel_id=1, source_target_pairs={{0,2},{1,5},{2,0},{3,7},{4,6},{5,1},{6,4},{7,3},{8,10},{9,13},{10,... | collective-permute-start | bytes 1572872 | tf_op jit(solution)/shard_map/ppermute | solution.py:166
  96.2 11.3 %collective-permute-start.25 = (bf16[1024,768]{1,0:T(8,128)(2,1)S(1)}, bf16[1024,768]{1,0:T(8,128)(2,1)S(1)}, u32[]{:S(2)}, u32[]{:S(2)}) collective-permute-start(bf16[1024,768]{1,0:T(8,128)(2,1)S(1)} %convolution_convert_fusion.2), channel_id=1, source_target_pairs={{0,1},{1,0},{2,3},{3,2},{4,5},{5,4},{6,7},{7,6},{8,9},{9,8},{10,11... | collective-permute-start | bytes 4718600 | tf_op jit(solution)/shard_map/ppermute | solution.py:16
  97.3 15.8 %collective-permute-start.26 = (bf16[1024,768]{1,0:T(8,128)(2,1)S(1)}, bf16[1024,768]{1,0:T(8,128)(2,1)S(1)}, u32[]{:S(2)}, u32[]{:S(2)}) collective-permute-start(bf16[1024,768]{1,0:T(8,128)(2,1)S(1)} %convolution_convert_fusion.1), channel_id=1, source_target_pairs={{0,1},{1,0},{2,3},{3,2},{4,5},{5,4},{6,7},{7,6},{8,9},{9,8},{10,11... | collective-permute-start | bytes 4718600 | tf_op jit(solution)/shard_map/ppermute | solution.py:16
  98.9 12.0 %collective-permute-start.27 = (bf16[384,2048]{1,0:T(8,128)(2,1)S(1)}, bf16[384,2048]{1,0:T(8,128)(2,1)S(1)}, u32[]{:S(2)}, u32[]{:S(2)}) collective-permute-start(bf16[384,2048]{1,0:T(8,128)(2,1)S(1)} %convolution_convert_fusion), channel_id=1, source_target_pairs={{0,1},{1,0},{2,3},{3,2},{4,5},{5,4},{6,7},{7,6},{8,9},{9,8},{10,11... | collective-permute-start | bytes 4718600 | tf_op jit(solution)/shard_map/ppermute | solution.py:16
  101.0 14.7 %collective-permute-start.22 = (bf16[32,2048]{1,0:T(8,128)(2,1)S(1)}, bf16[32,2048]{1,0:T(8,128)(2,1)S(1)}, u32[]{:S(2)}, u32[]{:S(2)}) collective-permute-start(bf16[32,2048]{1,0:T(8,128)(2,1)S(1)} %get-tuple-element.118), channel_id=1, source_target_pairs={{0,16},{8,24},{16,0},{24,8},{1,17},{9,25},{17,1},{25,9},{2,18},{10... | collective-permute-start | bytes 393224 | tf_op jit(solution)/shard_map/ppermute | solution.py:158
  104.2 14.2 %collective-permute-start.24 = (bf16[32,2048]{1,0:T(8,128)(2,1)S(1)}, bf16[32,2048]{1,0:T(8,128)(2,1)S(1)}, u32[]{:S(2)}, u32[]{:S(2)}) collective-permute-start(bf16[32,2048]{1,0:T(8,128)(2,1)S(1)} %get-tuple-element.117), channel_id=1, source_target_pairs={{0,16},{8,24},{16,0},{24,8},{1,17},{9,25},{17,1},{25,9},{2,18},{10... | collective-permute-start | bytes 393224 | tf_op jit(solution)/shard_map/ppermute | solution.py:158
  107.5 11.6 %collective-permute-start.29 = (bf16[32,2048]{1,0:T(8,128)(2,1)S(1)}, bf16[32,2048]{1,0:T(8,128)(2,1)S(1)}, u32[]{:S(2)}, u32[]{:S(2)}) collective-permute-start(bf16[32,2048]{1,0:T(8,128)(2,1)S(1)} %get-tuple-element.116), channel_id=1, source_target_pairs={{0,24},{8,16},{16,8},{24,0},{1,25},{9,17},{17,9},{25,1},{2,26},{10... | collective-permute-start | bytes 393224 | tf_op jit(solution)/shard_map/ppermute | solution.py:158
  110.9 8.2 %collective-permute-start.28 = (bf16[32,2048]{1,0:T(8,128)(2,1)S(1)}, bf16[32,2048]{1,0:T(8,128)(2,1)S(1)}, u32[]{:S(2)}, u32[]{:S(2)}) collective-permute-start(bf16[32,2048]{1,0:T(8,128)(2,1)S(1)} %get-tuple-element.115), channel_id=1, source_target_pairs={{0,8},{8,0},{16,24},{24,16},{1,9},{9,1},{17,25},{25,17},{2,10},{10... | collective-permute-start | bytes 393224 | tf_op jit(solution)/shard_map/ppermute | solution.py:158
  (22 other events, 178.0 us)

commit v8 on v7

--- a/solution.py
+++ b/solution.py
@@ -433,7 +433,7 @@
             return values
         count = len(values)
         if step <= 2:
-            new = self.own[:1] if step == 1 else self.own[1:]
+            new = self.own[:2] if step == 1 else self.own[2:]
             values = list(tie((*values, *new)))
             self.came += [partner_2(value, "rep", 0) for value in values[count:]]
         elif self.whole is None:

time: 120 us -> 120 us (level)
  starting transfers between devices: 30.4 us -> 32.4 us
  waiting for transfers between devices: 43.3 us -> 41.4 us
    ppermute x6, waiting for transfers between devices: 1.9 us -> 0.02 us  [partner_2(): return lax.ppermute(value, axis, pairs)]
    ppermute x15, starting transfers between devices: 17.8 us -> 19.5 us  [swap_inner(): return lax.ppermute(value, ('exp', 'rep'), pairs)]
    ppermute x9, waiting for transfers between devices: 11.7 us -> 13.1 us  [swap_group(): return lax.ppermute(value, 'grp', [(i, i ^ mask) for i in range(count)])]
    ppermute x15, waiting for transfers between devices: 29.7 us -> 28.3 us  [swap_inner(): return lax.ppermute(value, ('exp', 'rep'), pairs)]
  transfers between devices with their start and end apart: 30 -> 30, of which waited for: 14 -> 15; matrix products, arithmetic and copies ran while one was open for 11% -> 11% of each run, Pallas kernels for 19% -> 19%
where the time goes in v8:
time: 120 us
  waiting for transfers between devices  41.4 us (34%)
  starting transfers between devices  32.4 us (27%)
  Pallas kernels  28.4 us (24%)
  matrix products  9.68 us (8%)
  other arithmetic  5.92 us (5%)
    ppermute x15, waiting for transfers between devices, swap_inner(): return lax.ppermute(value, ('exp', 'rep'), pairs)  28.3 us
    pallas_call x3, Pallas kernels, expert_call(): pl.pallas_call(kernel, out_shape=[pltpu.HBM(shape, dtype) for shape, dtyp...  21.2 us
    ppermute x15, starting transfers between devices, swap_inner(): return lax.ppermute(value, ('exp', 'rep'), pairs)  19.5 us
    ppermute x9, waiting for transfers between devices, swap_group(): return lax.ppermute(value, 'grp', [(i, i ^ mask) for i in range(count)])  13.1 us
    ppermute x9, starting transfers between devices, swap_group(): return lax.ppermute(value, 'grp', [(i, i ^ mask) for i in range(count)])  12 us
    dot_general x6, matrix products, contract_rows(): lax.dot_general(left, right, (((0,), (0,)), ((), ())), preferred_element_...  9.68 us
    pallas_call x1, Pallas kernels, load(): pl.pallas_call(weights_kernel, out_shape=[pltpu.VMEM(shape, jnp.bfloat16)...  4.93 us
    convert_element_type x5, other arithmetic, add_bf16(): (left.astype(jnp.float32) + right.astype(jnp.float32)).astype(jnp.bfloat16)  2.63 us
  transfers between devices with their start and end apart: 30, of which 15 were waited for; matrix products, arithmetic and copies ran while one was open for 11% of the time, Pallas kernels for 19%

profile of v8, /device:TPU:0, one launch (start us, length us, event | category | flops | bytes accessed | tf_op | source)
XLA Modules:
  0.0 119.9 jit_solution(2729610163524968394)
XLA Ops:
  2.6 3.1 %collective-permute-start.1 = (bf16[64,2176]{1,0:T(8,128)(2,1)S(1)}, bf16[64,2176]{1,0:T(8,128)(2,1)}, u32[]{:S(2)}, u32[]{:S(2)}) collective-permute-start(bf16[64,2176]{1,0:T(8,128)(2,1)S(1)} %pad_maximum_fusion.refs_0_.refs_4_), channel_id=1, source_target_pairs={{0,8},{8,0},{16,24},{24,16},{1,9},{9,1},{17,25},{25,17},{2,10},{10... | collective-permute-start | bytes 835592 | tf_op jit(solution)/shard_map/ppermute | solution.py:158
  7.2 2.6 %collective-permute-start = (bf16[64,2176]{1,0:T(8,128)(2,1)S(1)}, bf16[64,2176]{1,0:T(8,128)(2,1)}, u32[]{:S(2)}, u32[]{:S(2)}) collective-permute-start(bf16[64,2176]{1,0:T(8,128)(2,1)S(1)} %pad_maximum_fusion.refs_0_.refs_4_), channel_id=1, source_target_pairs={{0,16},{8,24},{16,0},{24,8},{1,17},{9,25},{17,1},{25,9},{2,18},{10... | collective-permute-start | bytes 835592 | tf_op jit(solution)/shard_map/ppermute | solution.py:158
  11.3 5.8 %collective-permute-done.1.refs_2_.refs_6_ = bf16[64,2176]{1,0:T(8,128)(2,1)} collective-permute-done((bf16[64,2176]{1,0:T(8,128)(2,1)S(1)}, bf16[64,2176]{1,0:T(8,128)(2,1)}, u32[]{:S(2)}, u32[]{:S(2)}) %collective-permute-start.1) | collective-permute-done | bytes 278560 | tf_op jit(solution)/shard_map/ppermute | solution.py:158
  17.1 1.7 %collective-permute-start.3 = (bf16[64,2176]{1,0:T(8,128)(2,1)}, bf16[64,2176]{1,0:T(8,128)(2,1)}, u32[]{:S(2)}, u32[]{:S(2)}) collective-permute-start(bf16[64,2176]{1,0:T(8,128)(2,1)} %collective-permute-done.1.refs_2_.refs_6_), channel_id=1, source_target_pairs={{0,2},{1,5},{2,0},{3,7},{4,6},{5,1},{6,4},{7,3},{8,10},{9,13},{10,... | collective-permute-start | bytes 835592 | tf_op jit(solution)/shard_map/ppermute | solution.py:166
  18.7 2.5 %collective-permute-start.5 = (bf16[64,2176]{1,0:T(8,128)(2,1)S(1)}, bf16[64,2176]{1,0:T(8,128)(2,1)S(1)}, u32[]{:S(2)}, u32[]{:S(2)}) collective-permute-start(bf16[64,2176]{1,0:T(8,128)(2,1)S(1)} %collective-permute-done.2.refs_4_.refs_8_), channel_id=1, source_target_pairs={{0,4},{1,3},{2,6},{3,1},{4,0},{5,7},{6,2},{7,5},{8,12},{9,11},{10,... | collective-permute-start | bytes 835592 | tf_op jit(solution)/shard_map/ppermute | solution.py:166
  22.1 4.6 %collective-permute-done.3.refs_6_.refs_10_ = bf16[64,2176]{1,0:T(8,128)(2,1)} collective-permute-done((bf16[64,2176]{1,0:T(8,128)(2,1)}, bf16[64,2176]{1,0:T(8,128)(2,1)}, u32[]{:S(2)}, u32[]{:S(2)}) %collective-permute-start.3) | collective-permute-done | bytes 278560 | tf_op jit(solution)/shard_map/ppermute | solution.py:166
  29.1 1.7 %collective-permute-start.9 = (bf16[64,2176]{1,0:T(8,128)(2,1)}, bf16[64,2176]{1,0:T(8,128)(2,1)}, u32[]{:S(2)}, u32[]{:S(2)}) collective-permute-start(bf16[64,2176]{1,0:T(8,128)(2,1)} %collective-permute-done.3.refs_6_.refs_10_), channel_id=1, source_target_pairs={{0,4},{1,3},{2,6},{3,1},{4,0},{5,7},{6,2},{7,5},{8,12},{9,11},{10,... | collective-permute-start | bytes 835592 | tf_op jit(solution)/shard_map/ppermute | solution.py:166
  31.6 4.9 %shard_map.110 = (bf16[2048,768]{1,0:T(8,128)(2,1)S(1)}, bf16[2048,768]{1,0:T(8,128)(2,1)S(1)}, bf16[768,2048]{1,0:T(8,128)(2,1)S(1)}, s32[2]{0:T(128)S(1)}) custom-call(s32[2]{0:T(128)S(1)} %pad_add_fusion.where_ref, bf16[1024,768]{1,0:T(8,128)(2,1)} %bitcast.15, bf16[1024,768]{1,0:T(8,128)(2,1)} %copy-done.1, bf16[1024,768]{1,0:T(8,128)(2,1)} %bitcast.17, ...), custom_call_target="tpu_custom_call" | custom-call | tf_op jit(solution)/shard_map/pallas_call | solution.py:420
  37.8 1.9 %collective-permute-done.9.refs_6_.refs_18_.refs_14_ = bf16[64,2176]{1,0:T(8,128)(2,1)} collective-permute-done((bf16[64,2176]{1,0:T(8,128)(2,1)}, bf16[64,2176]{1,0:T(8,128)(2,1)}, u32[]{:S(2)}, u32[]{:S(2)}) %collective-permute-start.9) | collective-permute-done | bytes 278560 | tf_op jit(solution)/shard_map/ppermute | solution.py:166
  41.0 1.9 %collective-permute-done.14.refs_1_.refs_13_.refs_9_ = bf16[64,2176]{1,0:T(8,128)(2,1)S(1)} collective-permute-done((bf16[64,2176]{1,0:T(8,128)(2,1)}, bf16[64,2176]{1,0:T(8,128)(2,1)S(1)}, u32[]{:S(2)}, u32[]{:S(2)}) %collective-permute-start.14) | collective-permute-done | bytes 278560 | tf_op jit(solution)/shard_map/ppermute | solution.py:166
  43.9 3.9 %collective-permute-done.13.refs_7_.refs_11_ = bf16[64,2176]{1,0:T(8,128)(2,1)S(1)} collective-permute-done((bf16[64,2176]{1,0:T(8,128)(2,1)}, bf16[64,2176]{1,0:T(8,128)(2,1)S(1)}, u32[]{:S(2)}, u32[]{:S(2)}) %collective-permute-start.13) | collective-permute-done | bytes 278560 | tf_op jit(solution)/shard_map/ppermute | solution.py:166
  48.8 5.8 %shard_map.111 = (bf16[256,2048]{1,0:T(8,128)(2,1)}, bf16[256,768]{1,0:T(8,128)(2,1)}, bf16[256,768]{1,0:T(8,128)(2,1)}, bf16[256,768]{1,0:T(8,128)(2,1)}) custom-call(s32[2]{0:T(128)S(1)} %get-tuple-element.68.where_ref, bf16[64,2176]{1,0:T(8,128)(2,1)} %copy-done, bf16[64,2176]{1,0:T(8,128)(2,1)} %collective-permute-done.refs_1_.refs_5_, ...), custom_call_target="tpu_custom_call" | custom-call | flops 2415919104 | bytes 11665412 | tf_op jit(solution)/shard_map/pallas_call | solution.py:396
  55.5 5.8 %shard_map.112 = (bf16[256,2048]{1,0:T(8,128)(2,1)}, bf16[256,768]{1,0:T(8,128)(2,1)}, bf16[256,768]{1,0:T(8,128)(2,1)}, bf16[256,768]{1,0:T(8,128)(2,1)}) custom-call(s32[2]{0:T(128)S(1)} %get-tuple-element.68.where_ref, bf16[64,2176]{1,0:T(8,128)(2,1)} %copy-done.4, bf16[64,2176]{1,0:T(8,128)(2,1)} %copy-done.6, ...), custom_call_target="tpu_custom_call" | custom-call | flops 2415919104 | bytes 11665412 | tf_op jit(solution)/shard_map/pallas_call | solution.py:396
  62.5 9.6 %shard_map.113 = (bf16[256,2048]{1,0:T(8,128)(2,1)}, bf16[256,2048]{1,0:T(8,128)(2,1)}, bf16[512,768]{1,0:T(8,128)(2,1)}, bf16[512,768]{1,0:T(8,128)(2,1)}, bf16[512,2048]{1,0:T(8,128)(2,1)}) custom-call(s32[2]{0:T(128)S(1)} %get-tuple-element.68.where_ref, bf16[256,768]{1,0:T(8,128)(2,1)} %get-tuple-element.74.refs_0_, ...), custom_call_target="tpu_custom_call" | custom-call | flops 4831838208 | bytes 15466500 | tf_op jit(solution)/shard_map/pallas_call | solution.py:396
  73.1 3.3 %collective-permute-done.19 = bf16[256,2048]{1,0:T(8,128)(2,1)S(1)} collective-permute-done((bf16[256,2048]{1,0:T(8,128)(2,1)}, bf16[256,2048]{1,0:T(8,128)(2,1)S(1)}, u32[]{:S(2)}, u32[]{:S(2)}) %collective-permute-start.19) | collective-permute-done | bytes 1048608 | tf_op jit(solution)/shard_map/ppermute | solution.py:166
  78.6 2.2 %shard_map.114 = (bf16[512,2048]{1,0:T(8,128)(2,1)S(1)}, bf16[512,768]{1,0:T(8,128)(2,1)S(1)}) custom-call(bf16[64,2176]{1,0:T(8,128)(2,1)} %copy-done, bf16[64,2176]{1,0:T(8,128)(2,1)} %collective-permute-done.refs_1_.refs_5_, bf16[64,2176]{1,0:T(8,128)(2,1)} %collective-permute-done.1.refs_2_.refs_6_, ...), custom_call_target="tpu_custom_call" | custom-call | tf_op jit(solution)/shard_map/pallas_call | solution.py:485
  80.8 9.5 %collective-permute-done.20 = bf16[128,2048]{1,0:T(8,128)(2,1)} collective-permute-done((bf16[128,2048]{1,0:T(8,128)(2,1)}, bf16[128,2048]{1,0:T(8,128)(2,1)}, u32[]{:S(2)}, u32[]{:S(2)}) %collective-permute-start.20) | collective-permute-done | bytes 524320 | tf_op jit(solution)/shard_map/ppermute | solution.py:166
  91.6 1.9 %collective-permute-done.18 = bf16[256,2048]{1,0:T(8,128)(2,1)S(1)} collective-permute-done((bf16[256,2048]{1,0:T(8,128)(2,1)}, bf16[256,2048]{1,0:T(8,128)(2,1)S(1)}, u32[]{:S(2)}, u32[]{:S(2)}) %collective-permute-start.18) | collective-permute-done | bytes 1048608 | tf_op jit(solution)/shard_map/ppermute | solution.py:166
  100.0 1.8 %collective-permute-start.22 = (bf16[32,2048]{1,0:T(8,128)(2,1)S(1)}, bf16[32,2048]{1,0:T(8,128)(2,1)S(1)}, u32[]{:S(2)}, u32[]{:S(2)}) collective-permute-start(bf16[32,2048]{1,0:T(8,128)(2,1)S(1)} %get-tuple-element.118), channel_id=1, source_target_pairs={{0,16},{8,24},{16,0},{24,8},{1,17},{9,25},{17,1},{25,9},{2,18},{10... | collective-permute-start | bytes 393224 | tf_op jit(solution)/shard_map/ppermute | solution.py:158
  103.3 3.2 %collective-permute-start.24 = (bf16[32,2048]{1,0:T(8,128)(2,1)S(1)}, bf16[32,2048]{1,0:T(8,128)(2,1)S(1)}, u32[]{:S(2)}, u32[]{:S(2)}) collective-permute-start(bf16[32,2048]{1,0:T(8,128)(2,1)S(1)} %get-tuple-element.117), channel_id=1, source_target_pairs={{0,16},{8,24},{16,0},{24,8},{1,17},{9,25},{17,1},{25,9},{2,18},{10... | collective-permute-start | bytes 393224 | tf_op jit(solution)/shard_map/ppermute | solution.py:158
  107.7 2.2 %add_convert_fusion.2 = bf16[1024,768]{1,0:T(8,128)(2,1)} fusion(bf16[1024,768]{1,0:T(8,128)(2,1)S(1)} %collective-permute-done.25, bf16[512,768]{1,0:T(8,128)(2,1)S(1)} %copy-done.15, bf16[512,2048]{1,0:T(8,128)(2,1)S(1)} %get-tuple-element.104, s32[]{:T(128)S(6)} %select_n.19), kind=kOutput, calls=%fused_computation.2 | convolution fusion | flops 807665664 | bytes 4980740 | tf_op jit(solution)/shard_map/dot_general | solution.py:20
  109.9 2.2 %add_convert_fusion = bf16[384,2048]{1,0:T(8,128)(2,1)} fusion(bf16[384,2048]{1,0:T(8,128)(2,1)S(1)} %collective-permute-done.27, bf16[512,2048]{1,0:T(8,128)(2,1)S(1)} %copy-done.13, bf16[512,768]{1,0:T(8,128)(2,1)S(1)} %get-tuple-element.107, s32[]{:T(128)S(6)} %select_n.21), kind=kOutput, calls=%fused_computation | convolution fusion | flops 807665664 | bytes 5636100 | tf_op jit(solution)/shard_map/dot_general | solution.py:20
  112.1 2.2 %add_convert_fusion.1 = bf16[1024,768]{1,0:T(8,128)(2,1)} fusion(bf16[1024,768]{1,0:T(8,128)(2,1)S(1)} %collective-permute-done.26, bf16[512,768]{1,0:T(8,128)(2,1)S(1)} %copy-done.14, bf16[512,2048]{1,0:T(8,128)(2,1)S(1)} %get-tuple-element.104, s32[]{:T(128)S(6)} %select_n.19), kind=kOutput, calls=%fused_computation.1 | convolution fusion | flops 807665664 | bytes 4980740 | tf_op jit(solution)/shard_map/dot_general | solution.py:20
  115.7 2.8 %collective-permute-done.24 = bf16[32,2048]{1,0:T(8,128)(2,1)S(1)} collective-permute-done((bf16[32,2048]{1,0:T(8,128)(2,1)S(1)}, bf16[32,2048]{1,0:T(8,128)(2,1)S(1)}, u32[]{:S(2)}, u32[]{:S(2)}) %collective-permute-start.24) | collective-permute-done | bytes 131104 | tf_op jit(solution)/shard_map/ppermute | solution.py:158
  (97 shorter events, 31.9 us)
Async XLA Ops:
  2.6 14.5 %collective-permute-start.1 = (bf16[64,2176]{1,0:T(8,128)(2,1)S(1)}, bf16[64,2176]{1,0:T(8,128)(2,1)}, u32[]{:S(2)}, u32[]{:S(2)}) collective-permute-start(bf16[64,2176]{1,0:T(8,128)(2,1)S(1)} %pad_maximum_fusion.refs_0_.refs_4_), channel_id=1, source_target_pairs={{0,8},{8,0},{16,24},{24,16},{1,9},{9,1},{17,25},{25,17},{2,10},{10... | collective-permute-start | bytes 835592 | tf_op jit(solution)/shard_map/ppermute | solution.py:158
  5.7 11.4 %collective-permute-start.2 = (bf16[64,2176]{1,0:T(8,128)(2,1)S(1)}, bf16[64,2176]{1,0:T(8,128)(2,1)S(1)}, u32[]{:S(2)}, u32[]{:S(2)}) collective-permute-start(bf16[64,2176]{1,0:T(8,128)(2,1)S(1)} %pad_maximum_fusion.refs_0_.refs_4_), channel_id=1, source_target_pairs={{0,2},{1,5},{2,0},{3,7},{4,6},{5,1},{6,4},{7,3},{8,10},{9,13},{10,... | collective-permute-start | bytes 835592 | tf_op jit(solution)/shard_map/ppermute | solution.py:166
  7.2 14.9 %collective-permute-start = (bf16[64,2176]{1,0:T(8,128)(2,1)S(1)}, bf16[64,2176]{1,0:T(8,128)(2,1)}, u32[]{:S(2)}, u32[]{:S(2)}) collective-permute-start(bf16[64,2176]{1,0:T(8,128)(2,1)S(1)} %pad_maximum_fusion.refs_0_.refs_4_), channel_id=1, source_target_pairs={{0,16},{8,24},{16,0},{24,8},{1,17},{9,25},{17,1},{25,9},{2,18},{10... | collective-permute-start | bytes 835592 | tf_op jit(solution)/shard_map/ppermute | solution.py:158
  9.8 12.3 %collective-permute-start.4 = (bf16[64,2176]{1,0:T(8,128)(2,1)S(1)}, bf16[64,2176]{1,0:T(8,128)(2,1)S(1)}, u32[]{:S(2)}, u32[]{:S(2)}) collective-permute-start(bf16[64,2176]{1,0:T(8,128)(2,1)S(1)} %pad_maximum_fusion.refs_0_.refs_4_), channel_id=1, source_target_pairs={{0,4},{1,3},{2,6},{3,1},{4,0},{5,7},{6,2},{7,5},{8,12},{9,11},{10,... | collective-permute-start | bytes 835592 | tf_op jit(solution)/shard_map/ppermute | solution.py:166
  17.1 9.6 %collective-permute-start.3 = (bf16[64,2176]{1,0:T(8,128)(2,1)}, bf16[64,2176]{1,0:T(8,128)(2,1)}, u32[]{:S(2)}, u32[]{:S(2)}) collective-permute-start(bf16[64,2176]{1,0:T(8,128)(2,1)} %collective-permute-done.1.refs_2_.refs_6_), channel_id=1, source_target_pairs={{0,2},{1,5},{2,0},{3,7},{4,6},{5,1},{6,4},{7,3},{8,10},{9,13},{10,... | collective-permute-start | bytes 835592 | tf_op jit(solution)/shard_map/ppermute | solution.py:166
  26.8 9.7 %collective-permute-start.8 = (bf16[64,2176]{1,0:T(8,128)(2,1)}, bf16[64,2176]{1,0:T(8,128)(2,1)}, u32[]{:S(2)}, u32[]{:S(2)}) collective-permute-start(bf16[64,2176]{1,0:T(8,128)(2,1)} %collective-permute-done.1.refs_2_.refs_6_), channel_id=1, source_target_pairs={{0,4},{1,3},{2,6},{3,1},{4,0},{5,7},{6,2},{7,5},{8,12},{9,11},{10,... | collective-permute-start | bytes 835592 | tf_op jit(solution)/shard_map/ppermute | solution.py:166
  27.8 9.8 %collective-permute-start.6 = (bf16[64,2176]{1,0:T(8,128)(2,1)}, bf16[64,2176]{1,0:T(8,128)(2,1)}, u32[]{:S(2)}, u32[]{:S(2)}) collective-permute-start(bf16[64,2176]{1,0:T(8,128)(2,1)} %collective-permute-done.refs_1_.refs_5_), channel_id=1, source_target_pairs={{0,8},{8,0},{16,24},{24,16},{1,9},{9,1},{17,25},{25,17},{2,10},{10... | collective-permute-start | bytes 835592 | tf_op jit(solution)/shard_map/ppermute | solution.py:158
  27.8 10.0 %collective-permute-start.7 = (bf16[64,2176]{1,0:T(8,128)(2,1)}, bf16[64,2176]{1,0:T(8,128)(2,1)}, u32[]{:S(2)}, u32[]{:S(2)}) collective-permute-start(bf16[64,2176]{1,0:T(8,128)(2,1)} %collective-permute-done.refs_1_.refs_5_), channel_id=1, source_target_pairs={{0,2},{1,5},{2,0},{3,7},{4,6},{5,1},{6,4},{7,3},{8,10},{9,13},{10,... | collective-permute-start | bytes 835592 | tf_op jit(solution)/shard_map/ppermute | solution.py:166
  29.1 10.5 %collective-permute-start.9 = (bf16[64,2176]{1,0:T(8,128)(2,1)}, bf16[64,2176]{1,0:T(8,128)(2,1)}, u32[]{:S(2)}, u32[]{:S(2)}) collective-permute-start(bf16[64,2176]{1,0:T(8,128)(2,1)} %collective-permute-done.3.refs_6_.refs_10_), channel_id=1, source_target_pairs={{0,4},{1,3},{2,6},{3,1},{4,0},{5,7},{6,2},{7,5},{8,12},{9,11},{10,... | collective-permute-start | bytes 835592 | tf_op jit(solution)/shard_map/ppermute | solution.py:166
  30.9 12.0 %collective-permute-start.14 = (bf16[64,2176]{1,0:T(8,128)(2,1)}, bf16[64,2176]{1,0:T(8,128)(2,1)S(1)}, u32[]{:S(2)}, u32[]{:S(2)}) collective-permute-start(bf16[64,2176]{1,0:T(8,128)(2,1)} %collective-permute-done.refs_1_.refs_5_), channel_id=1, source_target_pairs={{0,4},{1,3},{2,6},{3,1},{4,0},{5,7},{6,2},{7,5},{8,12},{9,11},{10,... | collective-permute-start | bytes 835592 | tf_op jit(solution)/shard_map/ppermute | solution.py:166
  39.7 8.1 %collective-permute-start.13 = (bf16[64,2176]{1,0:T(8,128)(2,1)}, bf16[64,2176]{1,0:T(8,128)(2,1)S(1)}, u32[]{:S(2)}, u32[]{:S(2)}) collective-permute-start(bf16[64,2176]{1,0:T(8,128)(2,1)} %collective-permute-done.6.refs_3_.refs_7_), channel_id=1, source_target_pairs={{0,2},{1,5},{2,0},{3,7},{4,6},{5,1},{6,4},{7,3},{8,10},{9,13},{10,... | collective-permute-start | bytes 835592 | tf_op jit(solution)/shard_map/ppermute | solution.py:166
  43.0 11.6 %collective-permute-start.15 = (bf16[64,2176]{1,0:T(8,128)(2,1)S(1)}, bf16[64,2176]{1,0:T(8,128)(2,1)S(1)}, u32[]{:S(2)}, u32[]{:S(2)}) collective-permute-start(bf16[64,2176]{1,0:T(8,128)(2,1)S(1)} %collective-permute-done.14.refs_1_.refs_13_.refs_9_), channel_id=1, source_target_pairs={{0,8},{8,0},{16,24},{24,16},{1,9},{9,1},{17,25},{25,17},{2,10},{10... | collective-permute-start | bytes 835592 | tf_op jit(solution)/shard_map/ppermute | solution.py:158
  43.0 11.7 %collective-permute-start.16 = (bf16[64,2176]{1,0:T(8,128)(2,1)}, bf16[64,2176]{1,0:T(8,128)(2,1)S(1)}, u32[]{:S(2)}, u32[]{:S(2)}) collective-permute-start(bf16[64,2176]{1,0:T(8,128)(2,1)} %collective-permute-done.7.refs_5_.refs_9_), channel_id=1, source_target_pairs={{0,4},{1,3},{2,6},{3,1},{4,0},{5,7},{6,2},{7,5},{8,12},{9,11},{10,... | collective-permute-start | bytes 835592 | tf_op jit(solution)/shard_map/ppermute | solution.py:166
  61.3 15.1 %collective-permute-start.19 = (bf16[256,2048]{1,0:T(8,128)(2,1)}, bf16[256,2048]{1,0:T(8,128)(2,1)S(1)}, u32[]{:S(2)}, u32[]{:S(2)}) collective-permute-start(bf16[256,2048]{1,0:T(8,128)(2,1)} %get-tuple-element.93), channel_id=1, source_target_pairs={{0,4},{1,3},{2,6},{3,1},{4,0},{5,7},{6,2},{7,5},{8,12},{9,11},{10,... | collective-permute-start | bytes 3145736 | tf_op jit(solution)/shard_map/ppermute | solution.py:166
  72.1 21.4 %collective-permute-start.18 = (bf16[256,2048]{1,0:T(8,128)(2,1)}, bf16[256,2048]{1,0:T(8,128)(2,1)S(1)}, u32[]{:S(2)}, u32[]{:S(2)}) collective-permute-start(bf16[256,2048]{1,0:T(8,128)(2,1)} %get-tuple-element.91), channel_id=1, source_target_pairs={{0,4},{1,3},{2,6},{3,1},{4,0},{5,7},{6,2},{7,5},{8,12},{9,11},{10,... | collective-permute-start | bytes 3145736 | tf_op jit(solution)/shard_map/ppermute | solution.py:166
  77.3 13.0 %collective-permute-start.20 = (bf16[128,2048]{1,0:T(8,128)(2,1)}, bf16[128,2048]{1,0:T(8,128)(2,1)}, u32[]{:S(2)}, u32[]{:S(2)}) collective-permute-start(bf16[128,2048]{1,0:T(8,128)(2,1)} %add_convert_fusion.6), channel_id=1, source_target_pairs={{0,2},{1,5},{2,0},{3,7},{4,6},{5,1},{6,4},{7,3},{8,10},{9,13},{10,... | collective-permute-start | bytes 1572872 | tf_op jit(solution)/shard_map/ppermute | solution.py:166
  93.7 9.2 %collective-permute-start.23 = (bf16[128,2048]{1,0:T(8,128)(2,1)S(1)}, bf16[128,2048]{1,0:T(8,128)(2,1)S(1)}, u32[]{:S(2)}, u32[]{:S(2)}) collective-permute-start(bf16[128,2048]{1,0:T(8,128)(2,1)S(1)} %add_convert_fusion.4), channel_id=1, source_target_pairs={{0,2},{1,5},{2,0},{3,7},{4,6},{5,1},{6,4},{7,3},{8,10},{9,13},{10,... | collective-permute-start | bytes 1572872 | tf_op jit(solution)/shard_map/ppermute | solution.py:166
  95.9 10.6 %collective-permute-start.25 = (bf16[1024,768]{1,0:T(8,128)(2,1)S(1)}, bf16[1024,768]{1,0:T(8,128)(2,1)S(1)}, u32[]{:S(2)}, u32[]{:S(2)}) collective-permute-start(bf16[1024,768]{1,0:T(8,128)(2,1)S(1)} %convolution_convert_fusion.2), channel_id=1, source_target_pairs={{0,1},{1,0},{2,3},{3,2},{4,5},{5,4},{6,7},{7,6},{8,9},{9,8},{10,11... | collective-permute-start | bytes 4718600 | tf_op jit(solution)/shard_map/ppermute | solution.py:16
  97.0 15.1 %collective-permute-start.26 = (bf16[1024,768]{1,0:T(8,128)(2,1)S(1)}, bf16[1024,768]{1,0:T(8,128)(2,1)S(1)}, u32[]{:S(2)}, u32[]{:S(2)}) collective-permute-start(bf16[1024,768]{1,0:T(8,128)(2,1)S(1)} %convolution_convert_fusion.1), channel_id=1, source_target_pairs={{0,1},{1,0},{2,3},{3,2},{4,5},{5,4},{6,7},{7,6},{8,9},{9,8},{10,11... | collective-permute-start | bytes 4718600 | tf_op jit(solution)/shard_map/ppermute | solution.py:16
  98.6 11.3 %collective-permute-start.27 = (bf16[384,2048]{1,0:T(8,128)(2,1)S(1)}, bf16[384,2048]{1,0:T(8,128)(2,1)S(1)}, u32[]{:S(2)}, u32[]{:S(2)}) collective-permute-start(bf16[384,2048]{1,0:T(8,128)(2,1)S(1)} %convolution_convert_fusion), channel_id=1, source_target_pairs={{0,1},{1,0},{2,3},{3,2},{4,5},{5,4},{6,7},{7,6},{8,9},{9,8},{10,11... | collective-permute-start | bytes 4718600 | tf_op jit(solution)/shard_map/ppermute | solution.py:16
  100.0 15.7 %collective-permute-start.22 = (bf16[32,2048]{1,0:T(8,128)(2,1)S(1)}, bf16[32,2048]{1,0:T(8,128)(2,1)S(1)}, u32[]{:S(2)}, u32[]{:S(2)}) collective-permute-start(bf16[32,2048]{1,0:T(8,128)(2,1)S(1)} %get-tuple-element.118), channel_id=1, source_target_pairs={{0,16},{8,24},{16,0},{24,8},{1,17},{9,25},{17,1},{25,9},{2,18},{10... | collective-permute-start | bytes 393224 | tf_op jit(solution)/shard_map/ppermute | solution.py:158
  103.3 15.2 %collective-permute-start.24 = (bf16[32,2048]{1,0:T(8,128)(2,1)S(1)}, bf16[32,2048]{1,0:T(8,128)(2,1)S(1)}, u32[]{:S(2)}, u32[]{:S(2)}) collective-permute-start(bf16[32,2048]{1,0:T(8,128)(2,1)S(1)} %get-tuple-element.117), channel_id=1, source_target_pairs={{0,16},{8,24},{16,0},{24,8},{1,17},{9,25},{17,1},{25,9},{2,18},{10... | collective-permute-start | bytes 393224 | tf_op jit(solution)/shard_map/ppermute | solution.py:158
  106.4 12.7 %collective-permute-start.29 = (bf16[32,2048]{1,0:T(8,128)(2,1)S(1)}, bf16[32,2048]{1,0:T(8,128)(2,1)S(1)}, u32[]{:S(2)}, u32[]{:S(2)}) collective-permute-start(bf16[32,2048]{1,0:T(8,128)(2,1)S(1)} %get-tuple-element.116), channel_id=1, source_target_pairs={{0,24},{8,16},{16,8},{24,0},{1,25},{9,17},{17,9},{25,1},{2,26},{10... | collective-permute-start | bytes 393224 | tf_op jit(solution)/shard_map/ppermute | solution.py:158
  109.9 9.2 %collective-permute-start.28 = (bf16[32,2048]{1,0:T(8,128)(2,1)S(1)}, bf16[32,2048]{1,0:T(8,128)(2,1)S(1)}, u32[]{:S(2)}, u32[]{:S(2)}) collective-permute-start(bf16[32,2048]{1,0:T(8,128)(2,1)S(1)} %get-tuple-element.115), channel_id=1, source_target_pairs={{0,8},{8,0},{16,24},{24,16},{1,9},{9,1},{17,25},{25,17},{2,10},{10... | collective-permute-start | bytes 393224 | tf_op jit(solution)/shard_map/ppermute | solution.py:158
  (22 other events, 163.7 us)
